TPU v7x, 32 devices: a whole 2x2x4 slice. The times are simulated.
32 devices in a mesh: parts: 2 (over x), expert: 16 (over z, y, core).
Axes of the slice: x: 2, y: 2, z: 4, core: 2. Of those that a mesh axis runs over, the one named last changes fastest.
Arguments:
- tokens: bfloat16 [4096, 2048], P(('parts', 'expert')), parts along dimension 0, may hold values from -6 to 6
- cotangent: bfloat16 [4096, 2048], P(('parts', 'expert')), parts along dimension 0, may hold values from -1.25 to 1.25
- expert_ids: int32 [4096, 4], P(('parts', 'expert')), parts along dimension 0, may hold values from 0 to 15, as said below
- gate_weights: bfloat16 [4096, 4], P(('parts', 'expert')), parts along dimension 0, may hold values from 0.099609375 to 1
- w_gate_up: bfloat16 [32, 2048, 1536], P(('parts', 'expert')), parts along dimension 0, may hold values from -0.125 to 0.125
- w_down: bfloat16 [32, 768, 2048], P(('parts', 'expert')), parts along dimension 0, may hold values from -0.21875 to 0.21875
Outputs:
- grad_tokens: bfloat16 [4096, 2048], P(('parts', 'expert')), parts along dimension 0
- grad_gates: bfloat16 [4096, 4], P(('parts', 'expert')), parts along dimension 0
There are 2 independent parts, one for each index of `parts`. A program takes and returns all parts, laid end to end along the dimension named above; each array names one. Nothing has to cross between parts.
Inputs may be any that keep to these rules, and one draw needn't show every extreme that they name: `expert_ids`: each token names 4 different experts. Among the tokens of one device no expert is named more than 56 times, and one expert is named exactly 56 times by the tokens of every device.
All inputs are finite; a program needn't handle non-finite values.
Results may differ from a plain program's by a relative error of at most 0.0058.
Values may be sent and summed in bfloat16 or wider, within the bound.
No kernel may reach another device: no remote copies, remote signals or barrier semaphores. Data moves between devices by JAX's collectives and lax.ppermute only.
A program may use at most 128 MiB of HBM per device.

v0:
```python
import jax
import jax.numpy as jnp
from jax import lax
from jax.sharding import PartitionSpec as P


def shards(tokens, cotangent, expert_ids, gate_weights, w_gate_up, w_down):
    devices = lax.axis_size("expert")
    tok_rows, fanout = expert_ids.shape
    features = tokens.shape[1]
    hidden_units = w_down.shape[1]
    capacity = 7 * tok_rows * fanout // (4 * devices)
    routes = tok_rows * fanout
    slot_count = devices * capacity
    joined = w_gate_up[0]
    down_matrix = w_down[0]
    flat_ids = expert_ids.reshape(routes)
    onehot = (flat_ids[:, None] == jnp.arange(devices, dtype=jnp.int32)[None, :]).astype(jnp.int32)
    rank_in = jnp.sum((jnp.cumsum(onehot, axis=0) - onehot) * onehot, axis=1)
    slot_of = flat_ids * capacity + rank_in
    filler = (
        jnp.zeros((slot_count,), jnp.int32)
        .at[slot_of]
        .set(jnp.arange(1, routes + 1, dtype=jnp.int32))
    )
    in_use = filler > 0
    source = jnp.maximum(filler - 1, 0)
    token_of = source // fanout
    send_rows = jnp.where(in_use[:, None], tokens[token_of], 0).reshape(devices, capacity, features)
    send_grads = jnp.where(in_use[:, None], cotangent[token_of], 0).reshape(
        devices, capacity, features
    )
    send_weights = jnp.where(in_use, gate_weights.reshape(routes)[source], 0).reshape(
        devices, capacity
    )
    recv_rows, recv_grads, recv_weights = (
        lax.all_to_all(send_rows, "expert", split_axis=0, concat_axis=0, tiled=True),
        lax.all_to_all(send_grads, "expert", split_axis=0, concat_axis=0, tiled=True),
        lax.all_to_all(send_weights, "expert", split_axis=0, concat_axis=0, tiled=True),
    )
    projections = jnp.dot(
        recv_rows.reshape(slot_count, features), joined, preferred_element_type=jnp.float32
    )
    sources, slot_rows, width = recv_grads.shape
    gate_pre = projections[:, :hidden_units]
    up_pre = projections[:, hidden_units:]
    sigmoid_gate = jax.nn.sigmoid(gate_pre)
    active = gate_pre * sigmoid_gate
    hidden = active * up_pre
    hidden_grad = lax.dot_general(
        recv_grads.reshape(sources * slot_rows, width),
        down_matrix,
        (((1,), (1,)), ((), ())),
        preferred_element_type=jnp.float32,
    )
    gate_grad = jnp.sum(hidden_grad * hidden, axis=1).astype(jnp.bfloat16)
    scaled = recv_weights.reshape(sources * slot_rows).astype(jnp.float32)[:, None] * hidden_grad
    first_half = scaled * up_pre * sigmoid_gate * (1.0 + gate_pre * (1.0 - sigmoid_gate))
    second_half = scaled * active
    projection_grad = jnp.concatenate([first_half, second_half], axis=1).astype(jnp.bfloat16)
    route_grad = lax.dot_general(
        projection_grad, joined, (((1,), (1,)), ((), ())), preferred_element_type=jnp.float32
    )
    route_part = route_grad.astype(jnp.bfloat16)
    send_route_part = route_part.reshape(sources, slot_rows, width)
    send_gate_part = gate_grad.reshape(sources, slot_rows)
    return_rows = lax.all_to_all(send_route_part, "expert", split_axis=0, concat_axis=0, tiled=True)
    return_gates = lax.all_to_all(send_gate_part, "expert", split_axis=0, concat_axis=0, tiled=True)
    route_grad = return_rows.reshape(slot_count, features)[slot_of].astype(jnp.float32)
    grad_tokens = jnp.sum(route_grad.reshape(tok_rows, fanout, features), axis=1).astype(
        jnp.bfloat16
    )
    grad_gates = return_gates.reshape(slot_count)[slot_of].reshape(tok_rows, fanout)
    return (grad_tokens, grad_gates)


def solution(mesh):
    in_specs = (
        P(("parts", "expert"), None),
        P(("parts", "expert"), None),
        P(("parts", "expert"), None),
        P(("parts", "expert"), None),
        P(("parts", "expert"), None, None),
        P(("parts", "expert"), None, None),
    )
    out_specs = (P(("parts", "expert"), None), P(("parts", "expert"), None))
    return jax.shard_map(shards, mesh=mesh, in_specs=in_specs, out_specs=out_specs, check_vma=False)
```

profile of v0, /device:TPU:15, one launch (start us, length us, event | category | flops | bytes accessed | tf_op | source)
XLA Modules:
  0.0 348.1 jit_solution(3669417480772626091)
XLA Ops:
  0.6 0.9 copy.19
  1.7 0.1 eq.25
  1.8 0.7 broadcast_multiply_fusion
  2.5 1.2 reduce-window.6
  3.7 0.2 slice_reduce_fusion
  3.9 0.1 copy.18
  4.0 0.1 mul.53
  4.2 2.4 scatter_custom_fusion
  6.7 0.8 copy.22
  7.5 0.1 reshape.117
  7.7 5.8 %gather_fusion = bf16[896]{0:T(1024)(128)(2,1)S(1)} fusion(bf16[512]{0:T(512)(128)(2,1)S(1)} %reshape.117, s32[1024]{0:T(1024)S(1)} %get-tuple-element.16), kind=kCustom, calls=%fused_computation | custom fusion | bytes 7168 | tf_op jit(solution)/shard_map/gather | solution.py:33
  13.5 0.7 all_to_all.25
  14.2 6.6 %all-to-all-start = ((bf16[16,1,56]{2,1,0:T(2,128)(2,1)}), bf16[16,1,56]{2,1,0:T(2,128)(2,1)S(1)}, u32[]{:S(2)}, u32[]{:S(2)}) async-start(bf16[16,1,56]{2,1,0:T(2,128)(2,1)} %all_to_all.25), calls=%async_computation | async-start | bytes 16384 | tf_op jit(solution)/shard_map/all_to_all | solution.py:39
  20.8 9.9 %gather_fusion.1 = bf16[896,2048]{1,0:T(8,128)(2,1)} fusion(bf16[128,2048]{1,0:T(8,128)(2,1)} %param.7, s32[1024]{0:T(1024)S(1)} %get-tuple-element.15), kind=kCustom, calls=%fused_computation.1 | custom fusion | bytes 7343616 | tf_op jit(solution)/shard_map/gather | solution.py:30
  30.7 9.9 %gather_fusion.2 = bf16[896,2048]{1,0:T(8,128)(2,1)} fusion(bf16[128,2048]{1,0:T(8,128)(2,1)} %param.6, s32[1024]{0:T(1024)S(1)} %get-tuple-element.15), kind=kCustom, calls=%fused_computation.2 | custom fusion | bytes 7343616 | tf_op jit(solution)/shard_map/gather | solution.py:29
  40.6 5.4 %broadcast_select_fusion = (bf16[16,56,2048]{2,1,0:T(8,128)(2,1)}, bf16[16,56,2048]{2,1,0:T(8,128)(2,1)}) fusion(bf16[16,56,2048]{2,1,0:T(8,128)(2,1)} %bitcast.42, pred[16,56]{1,0:T(8,128)(4,1)S(1)} %broadcast_in_dim.38, bf16[16,56,2048]{2,1,0:T(8,128)(2,1)} %bitcast.41), kind=kLoop, calls=%fused_computation.10 | loop fusion | flops 3670016 | bytes 14680960 | tf_op jit(solution)/shard_map/jit(_where)/select_n | solution.py:29
  46.0 87.1 %all_to_all.31 = bf16[16,56,2048]{2,1,0:T(8,128)(2,1)} all-to-all(bf16[16,56,2048]{2,1,0:T(8,128)(2,1)} %get-tuple-element.13), channel_id=1, replica_groups=mesh['parts'=2,'expert'=16] {'expert'}, dimensions={0} | all-to-all | bytes 7340032 | tf_op jit(solution)/shard_map/all_to_all | solution.py:37
  133.2 5.2 %all-to-all-start.1 = ((bf16[16,56,2048]{2,1,0:T(8,128)(2,1)}), bf16[16,56,2048]{2,1,0:T(8,128)(2,1)}, u32[]{:S(2)}, u32[]{:S(2)}) async-start(bf16[16,56,2048]{2,1,0:T(8,128)(2,1)} %get-tuple-element.14), calls=%async_computation.1 | async-start | bytes 7340032 | tf_op jit(solution)/shard_map/all_to_all | solution.py:38
  138.5 11.5 %fusion.2 = f32[896,1536]{0,1:T(8,128)} fusion(bf16[896,2048]{1,0:T(8,128)(2,1)} %bitcast.44, bf16[1,2048,1536]{2,1,0:T(8,128)(2,1)} %param.10), kind=kOutput, calls=%fused_computation.8 | convolution fusion | flops 5637144576 | bytes 15466496 | tf_op jit(solution)/shard_map/dot_general | solution.py:41
  150.1 69.6 %all-to-all-done.1 = bf16[16,56,2048]{2,1,0:T(8,128)(2,1)} async-done(((bf16[16,56,2048]{2,1,0:T(8,128)(2,1)}), bf16[16,56,2048]{2,1,0:T(8,128)(2,1)}, u32[]{:S(2)}, u32[]{:S(2)}) %all-to-all-start.1) | async-done | bytes 3670048 | tf_op jit(solution)/shard_map/all_to_all | solution.py:38
  219.6 8.6 %multiply_convert_fusion.1 = (bf16[896,768]{0,1:T(8,128)(2,1)}, bf16[896,768]{0,1:T(8,128)(2,1)}, bf16[896]{0:T(1024)(128)(2,1)S(1)}) fusion(f32[896,1536]{0,1:T(8,128)} %fusion.2, f32[896]{0:T(1024)S(1)} %reshape.124, bf16[896,2048]{1,0:T(8,128)(2,1)} %bitcast.4, bf16[1,768,2048]{2,1,0:T(8,128)(2,1)S(1)} %copy-done), kind=kOutput, calls=%fused_computation.20 | convolution fusion | flops 2830269440 | bytes 15078656 | tf_op jit(solution)/shard_map/dot_general | solution.py:50
  228.2 0.7 convert_element_type.51
  228.9 4.9 %all-to-all-start.4 = ((bf16[16,1,56]{2,1,0:T(2,128)(2,1)}), bf16[16,1,56]{2,1,0:T(2,128)(2,1)S(1)}, u32[]{:S(2)}, u32[]{:S(2)}) async-start(bf16[16,1,56]{2,1,0:T(2,128)(2,1)} %convert_element_type.51), calls=%async_computation.4 | async-start | bytes 16384 | tf_op jit(solution)/shard_map/all_to_all | solution.py:68
  233.8 10.1 %fusion.4 = bf16[896,2048]{1,0:T(8,128)(2,1)} fusion(bf16[1,2048,1536]{2,1,0:T(8,128)(2,1)} %param.10, bf16[896,768]{0,1:T(8,128)(2,1)} %get-tuple-element.9, bf16[896,768]{0,1:T(8,128)(2,1)} %get-tuple-element.8), kind=kOutput, calls=%fused_computation.12 | convolution fusion | flops 5644484608 | bytes 12713984 | tf_op jit(solution)/shard_map/dot_general | solution.py:61
  243.9 6.0 %all-to-all-start.3 = ((bf16[16,56,2048]{2,1,0:T(8,128)(2,1)}), bf16[16,56,2048]{2,1,0:T(8,128)(2,1)}, u32[]{:S(2)}, u32[]{:S(2)}) async-start(bf16[16,56,2048]{2,1,0:T(8,128)(2,1)} %bitcast.43), calls=%async_computation.3 | async-start | bytes 7340032 | tf_op jit(solution)/shard_map/all_to_all | solution.py:67
  250.1 3.5 %gather_fusion.4 = bf16[512]{0:T(512)(128)(2,1)S(1)} fusion(bf16[896]{0:T(1024)(128)(2,1)S(1)} %reshape.122, s32[1024]{0:T(1024)S(1)} %pad_clamp_fusion), kind=kCustom, calls=%fused_computation.4 | custom fusion | bytes 4096 | tf_op jit(solution)/shard_map/gather | solution.py:73
  253.6 0.1 reshape.123
  253.8 0.7 copy.27
  254.4 76.8 %all-to-all-done.3 = bf16[16,56,2048]{2,1,0:T(8,128)(2,1)} async-done(((bf16[16,56,2048]{2,1,0:T(8,128)(2,1)}), bf16[16,56,2048]{2,1,0:T(8,128)(2,1)}, u32[]{:S(2)}, u32[]{:S(2)}) %all-to-all-start.3) | async-done | bytes 3670048 | tf_op jit(solution)/shard_map/all_to_all | solution.py:67
  331.2 7.8 %gather_fusion.3 = bf16[512,2048]{1,0:T(8,128)(2,1)} fusion(bf16[896,2048]{1,0:T(8,128)(2,1)} %bitcast.10, s32[1024]{0:T(1024)S(1)} %pad_clamp_fusion), kind=kCustom, calls=%fused_computation.3 | custom fusion | bytes 4196352 | tf_op jit(solution)/shard_map/gather | solution.py:69
  339.0 4.1 %gather.27 = bf16[128,4,2048]{2,1,0:T(4,128)(2,1)} reshape(bf16[512,2048]{1,0:T(8,128)(2,1)} %gather_fusion.3) | data formatting | bytes 4194304 | tf_op jit(solution)/shard_map/gather | solution.py:69
  343.1 5.0 %reduce_sum.34 = bf16[128,2048]{1,0:T(8,128)(2,1)} reduce(bf16[128,4,2048]{2,1,0:T(4,128)(2,1)} %gather.27, bf16[]{:T(256)} %constant.37.clone.1), dimensions={1}, to_apply=%region_4.5 | reduce | flops 786432 | bytes 2621442 | tf_op jit(solution)/shard_map/reduce_sum | solution.py:70
  (20 shorter events, 0.6 us)
Async XLA Ops:
  0.6 219.0 %copy-start = (bf16[1,768,2048]{2,1,0:T(8,128)(2,1)S(1)}, bf16[1,768,2048]{2,1,0:T(8,128)(2,1)}, u32[]{:S(2)}) copy-start(bf16[1,768,2048]{2,1,0:T(8,128)(2,1)} %param.11) | copy-start | bytes 9437188
  14.2 31.9 %all-to-all-start = ((bf16[16,1,56]{2,1,0:T(2,128)(2,1)}), bf16[16,1,56]{2,1,0:T(2,128)(2,1)S(1)}, u32[]{:S(2)}, u32[]{:S(2)}) async-start(bf16[16,1,56]{2,1,0:T(2,128)(2,1)} %all_to_all.25), calls=%async_computation | async-start | bytes 16384 | tf_op jit(solution)/shard_map/all_to_all | solution.py:39
  133.2 86.5 %all-to-all-start.1 = ((bf16[16,56,2048]{2,1,0:T(8,128)(2,1)}), bf16[16,56,2048]{2,1,0:T(8,128)(2,1)}, u32[]{:S(2)}, u32[]{:S(2)}) async-start(bf16[16,56,2048]{2,1,0:T(8,128)(2,1)} %get-tuple-element.14), calls=%async_computation.1 | async-start | bytes 7340032 | tf_op jit(solution)/shard_map/all_to_all | solution.py:38
  228.9 15.0 %all-to-all-start.4 = ((bf16[16,1,56]{2,1,0:T(2,128)(2,1)}), bf16[16,1,56]{2,1,0:T(2,128)(2,1)S(1)}, u32[]{:S(2)}, u32[]{:S(2)}) async-start(bf16[16,1,56]{2,1,0:T(2,128)(2,1)} %convert_element_type.51), calls=%async_computation.4 | async-start | bytes 16384 | tf_op jit(solution)/shard_map/all_to_all | solution.py:68
  243.9 87.2 %all-to-all-start.3 = ((bf16[16,56,2048]{2,1,0:T(8,128)(2,1)}), bf16[16,56,2048]{2,1,0:T(8,128)(2,1)}, u32[]{:S(2)}, u32[]{:S(2)}) async-start(bf16[16,56,2048]{2,1,0:T(8,128)(2,1)} %bitcast.43), calls=%async_computation.3 | async-start | bytes 7340032 | tf_op jit(solution)/shard_map/all_to_all | solution.py:67
where the time goes:
time: 349 us; the launch traced here: 348 us
  waiting for transfers between devices  146 us (42%)
  blocking collectives  87.1 us (25%)
  local copies, waits for them, and re-layouts  48.4 us (14%)
  matrix products  30.2 us (9%)
  starting transfers between devices  22.7 us (7%)
  other arithmetic  12.4 us (4%)
    all_to_all x1, blocking collectives, shards(): lax.all_to_all(send_rows, 'expert', split_axis=0, concat_axis=0, tiled=True)  87.1 us
    all_to_all x1, waiting for transfers between devices, shards(): lax.all_to_all(send_route_part, 'expert', split_axis=0, concat_axis=0, ti...  76.8 us
    all_to_all x1, waiting for transfers between devices, shards(): lax.all_to_all(send_grads, 'expert', split_axis=0, concat_axis=0, tiled=T...  69.6 us
    gather x2, local copies, waits for them, and re-layouts, shards(): return_rows.reshape(slot_count, features)[slot_of].astype(jnp.float32)  11.9 us
    dot_general x1, matrix products, shards(): jnp.dot(recv_rows.reshape(slot_count, features), joined, preferred_elemen...  11.5 us
    dot_general x1, matrix products, shards(): lax.dot_general(projection_grad, joined, (((1,), (1,)), ((), ())), prefer...  10.1 us
    gather x1, local copies, waits for them, and re-layouts, shards(): cotangent[token_of]  9.93 us
    gather x1, local copies, waits for them, and re-layouts, shards(): tokens[token_of]  9.89 us
  transfers between devices with their start and end apart: 4, of which 2 were waited for; matrix products, arithmetic and copies ran while one was open for 15% of the time, Pallas kernels for 0%

commit v1 on v0

v1 whole, which is shorter than its diff:
```python
import functools

import jax
import jax.numpy as jnp
from jax import lax
from jax.experimental import pallas as pl
from jax.experimental.pallas import tpu as pltpu
from jax.sharding import PartitionSpec as P

F32, BF16 = jnp.float32, jnp.bfloat16
LANES = 128
VMEM_BYTES = 48 * 2**20
NT = (((1,), (1,)), ((), ()))


def project_kernel(rows, features, own_ref, far_ref, w0_ref, w1_ref, out0_ref, out1_ref, both):
    @pl.when(pl.program_id(0) == 0)
    def _():
        both[:rows, :] = own_ref[:, :features]
        both[rows:, :] = far_ref[:, :features]

    out0_ref[...] = jnp.dot(both[...], w0_ref[...], preferred_element_type=F32)
    out1_ref[...] = jnp.dot(both[...], w1_ref[...], preferred_element_type=F32)


def project(own, far, w0, w1, tile=384):
    rows = own.shape[0]
    features, width = w0.shape
    whole = lambda a: pl.BlockSpec(a.shape, lambda i: (0, 0))
    weight = pl.BlockSpec((features, tile), lambda i: (0, i))
    out = pl.BlockSpec((2 * rows, tile), lambda i: (0, i))
    return pl.pallas_call(
        functools.partial(project_kernel, rows, features),
        grid=(width // tile,),
        in_specs=[whole(own), whole(far), weight, weight],
        out_specs=[out, out],
        out_shape=[jax.ShapeDtypeStruct((2 * rows, width), F32)] * 2,
        scratch_shapes=[pltpu.VMEM((2 * rows, features), BF16)],
        compiler_params=pltpu.CompilerParams(vmem_limit_bytes=VMEM_BYTES),
        cost_estimate=pl.CostEstimate(
            flops=8 * rows * features * width,
            bytes_accessed=4 * features * width + 16 * rows * width,
            transcendentals=0,
        ),
    )(own, far, w0, w1)


def backward_kernel(
    rows, features, hidden, tile, split, experts_ref,
    g0_ref, u0_ref, g1_ref, u1_ref, own_ref, far_ref, meta_own, meta_far, d0_ref, d1_ref, w0_ref, w1_ref,
    out_own, out_far, both, grads, gates, weights,
):
    step = pl.program_id(0)
    lane = lax.broadcasted_iota(jnp.int32, (2 * rows, LANES), 1)

    @pl.when(step == 0)
    def _():
        both[:rows, :] = own_ref[...]
        both[rows:, :] = far_ref[...]
        weights[:rows, :] = meta_own[...].astype(F32)
        weights[rows:, :] = meta_far[...].astype(F32)
        gates[...] = jnp.zeros_like(gates)

    def first(expert, g_ref, u_ref, d_ref, base, part):
        gate_pre, up_pre = g_ref[...], u_ref[...]
        hidden_grad = lax.dot_general(both[...], d_ref[...], NT, preferred_element_type=F32)
        sigmoid = 1.0 / (1.0 + jnp.exp(-gate_pre))
        active = gate_pre * sigmoid
        here = lane == experts_ref[expert]
        scale = jnp.sum(jnp.where(here, weights[...], 0.0), axis=1, keepdims=True)
        total = jnp.sum(hidden_grad * active * up_pre, axis=1, keepdims=True)
        gates[...] += jnp.where(here, total, 0.0)
        scaled = scale * hidden_grad
        grads[:, pl.ds(base + part * tile, tile)] = (
            scaled * up_pre * sigmoid * (1.0 + gate_pre * (1.0 - sigmoid))
        ).astype(BF16)
        grads[:, pl.ds(base + hidden + part * tile, tile)] = (scaled * active).astype(BF16)

    parts = hidden // tile
    for part in range(parts):
        pl.when(step == part)(
            functools.partial(first, 0, g0_ref, u0_ref, d0_ref, 0, part)
        )
        pl.when(step == parts + part)(
            functools.partial(first, 1, g1_ref, u1_ref, d1_ref, 2 * hidden, part)
        )

    def second(part):
        out = lax.dot_general(grads[:, : 2 * hidden], w0_ref[...], NT, preferred_element_type=F32)
        out += lax.dot_general(grads[:, 2 * hidden :], w1_ref[...], NT, preferred_element_type=F32)
        out = out.astype(BF16)
        out_own[:, pl.ds(part * split, split)] = out[:rows]
        out_far[:, pl.ds(part * split, split)] = out[rows:]

    for part in range(features // split):
        pl.when(step == 2 * parts + part)(functools.partial(second, part))

    @pl.when(step == 2 * parts)
    def _():
        out_own[:, features:] = gates[:rows].astype(BF16)
        out_far[:, features:] = gates[rows:].astype(BF16)


def backward(experts, p0, p1, own, far, tok_own, tok_far, d0, d1, w0, w1, tile=384, split=256):
    rows, features = own.shape
    hidden = d0.shape[0]
    parts = hidden // tile
    steps = 2 * parts + features // split
    at0 = lambda i: jnp.minimum(i, parts - 1)
    at1 = lambda i: jnp.clip(i - parts, 0, parts - 1)
    late = lambda i: jnp.maximum(i - 2 * parts, 0)
    whole = lambda a: pl.BlockSpec(a.shape, lambda i, e: (0, 0))
    pre = lambda at, off: pl.BlockSpec((2 * rows, tile), lambda i, e: (0, at(i) + off))
    meta = pl.BlockSpec((rows, LANES), lambda i, e: (0, features // LANES))
    down = lambda at: pl.BlockSpec((tile, features), lambda i, e: (at(i), 0))
    weight = pl.BlockSpec((split, 2 * hidden), lambda i, e: (late(i), 0))
    out = pl.BlockSpec((rows, features + LANES), lambda i, e: (0, 0))
    return pl.pallas_call(
        functools.partial(backward_kernel, rows, features, hidden, tile, split),
        grid_spec=pltpu.PrefetchScalarGridSpec(
            num_scalar_prefetch=1,
            grid=(steps,),
            in_specs=[
                pre(at0, 0), pre(at0, parts), pre(at1, 0), pre(at1, parts),
                whole(own), whole(far), meta, meta, down(at0), down(at1), weight, weight,
            ],
            out_specs=[out, out],
            scratch_shapes=[
                pltpu.VMEM((2 * rows, features), BF16),
                pltpu.VMEM((2 * rows, 4 * hidden), BF16),
                pltpu.VMEM((2 * rows, LANES), F32),
                pltpu.VMEM((2 * rows, LANES), F32),
            ],
        ),
        out_shape=[jax.ShapeDtypeStruct((rows, features + LANES), BF16)] * 2,
        compiler_params=pltpu.CompilerParams(vmem_limit_bytes=VMEM_BYTES),
        cost_estimate=pl.CostEstimate(
            flops=24 * rows * features * hidden,
            bytes_accessed=12 * features * hidden + 32 * rows * hidden,
            transcendentals=4 * rows * hidden,
        ),
    )(experts, p0, p0, p1, p1, own, far, tok_own, tok_far, d0, d1, w0, w1)


def ring_shards(lines, tokens, cotangent, expert_ids, gate_weights, w_gate_up, w_down):
    devices = lax.axis_size("expert")
    depth = devices // (2 * lines)
    rows, features = tokens.shape
    index = lambda z, y, c: (z * lines + y) * 2 + c
    places = [(z, y, c) for z in range(depth) for y in range(lines) for c in range(2)]
    up = [(index(z, y, c), index((z + 1) % depth, y, c)) for z, y, c in places]
    across = [(index(z, y, c), index(z, 1 - y, c)) for z, y, c in places]
    twin = [(index(z, y, c), index(z, y, 1 - c)) for z, y, c in places]
    move = lambda a, pairs: lax.ppermute(a, "expert", pairs)

    me = lax.axis_index("expert")
    experts = jnp.stack([me, me ^ 1]).astype(jnp.int32)
    lane = jnp.arange(LANES, dtype=jnp.int32)
    at = expert_ids[:, :, None] == lane
    table = jnp.sum(jnp.where(at, gate_weights[:, :, None], 0), axis=1).astype(BF16)
    x = [jnp.concatenate([tokens, table], axis=1)]
    g = [cotangent]
    w0, d0 = w_gate_up[0], w_down[0]
    w1, d1 = move(w0, twin), move(d0, twin)
    for _ in range(depth - 1):
        x.append(move(x[-1], up))
        g.append(move(g[-1], up))
    xf = [move(a, across) for a in x]
    gf = [move(a, across) for a in g]
    mine, total = [], []
    for s in range(depth):
        p0, p1 = project(x[s], xf[s], w0, w1)
        own, far = backward(experts, p0, p1, g[s], gf[s], x[s], xf[s], d0, d1, w0, w1)
        mine.append((own, move(far, across)))
    for s in list(range(1, depth)) + [0]:
        own, back = mine[s]
        here = own.astype(F32) + back.astype(F32)
        if total:
            here = here + move(total[-1], up).astype(F32)
        total.append(here.astype(BF16))
    last = total[-1]
    picked = jnp.where(at, last[:, None, features:], 0)
    return last[:, :features], jnp.sum(picked, axis=2).astype(BF16)


def solution(mesh):
    row, cube = P(("parts", "expert"), None), P(("parts", "expert"), None, None)
    body = functools.partial(ring_shards, 2)
    return jax.shard_map(
        body, mesh=mesh, in_specs=(row, row, row, row, cube, cube), out_specs=(row, row), check_vma=False
    )
```

time: 349 us -> 209 us (0.60)
  the two profiles are of different devices: /device:TPU:15 before, /device:TPU:0 now
where the time goes in v1:
time: 209 us
  Pallas kernels  97.8 us (47%)
  waiting for transfers between devices  78.1 us (37%)
  starting transfers between devices  22.8 us (11%)
  local copies, waits for them, and re-layouts  5.42 us (3%)
  other arithmetic  3.58 us (2%)
    ppermute x23, waiting for transfers between devices, ring_shards(): move = lambda a, pairs: lax.ppermute(a, 'expert', pairs)  78.1 us
    pallas_call x4, Pallas kernels, backward(): pl.pallas_call(functools.partial(backward_kernel, rows, features, hidden,...  66.1 us
    pallas_call x4, Pallas kernels, project(): pl.pallas_call(functools.partial(project_kernel, rows, features), grid=(w...  31.8 us
    ppermute x23, starting transfers between devices, ring_shards(): move = lambda a, pairs: lax.ppermute(a, 'expert', pairs)  22.8 us
    unnamed x12, local copies, waits for them, and re-layouts  4.57 us
  transfers between devices with their start and end apart: 23, of which 9 were waited for; matrix products, arithmetic and copies ran while one was open for 1% of the time, Pallas kernels for 47%

profile of v1, /device:TPU:0, one launch (start us, length us, event | category | flops | bytes accessed | tf_op | source)
XLA Modules:
  0.0 208.5 jit_solution(90293008103985255)
XLA Ops:
  1.2 3.0 %collective-permute-start.9 = (bf16[128,2048]{1,0:T(8,128)(2,1)}, bf16[128,2048]{1,0:T(8,128)(2,1)S(1)}, u32[]{:S(2)}, u32[]{:S(2)}) collective-permute-start(bf16[128,2048]{1,0:T(8,128)(2,1)} %own_ref.1), channel_id=1, source_target_pairs={{0,4},{1,5},{2,6},{3,7},{4,8},{5,9},{6,10},{7,11},{8,12},{9,13},{1... | collective-permute-start | bytes 1572872 | tf_op jit(solution)/shard_map/ppermute | solution.py:154
  6.2 1.6 collective-permute-start.5
  7.9 11.3 %collective-permute-done.9.own_ref = bf16[128,2048]{1,0:T(8,128)(2,1)S(1)} collective-permute-done((bf16[128,2048]{1,0:T(8,128)(2,1)}, bf16[128,2048]{1,0:T(8,128)(2,1)S(1)}, u32[]{:S(2)}, u32[]{:S(2)}) %collective-permute-start.9) | collective-permute-done | bytes 524320 | tf_op jit(solution)/shard_map/ppermute | solution.py:154
  19.2 11.9 %collective-permute-done.5.own_ref.meta_own = bf16[128,2176]{1,0:T(8,128)(2,1)S(1)} collective-permute-done((bf16[128,2176]{1,0:T(8,128)(2,1)S(1)}, bf16[128,2176]{1,0:T(8,128)(2,1)S(1)}, u32[]{:S(2)}, u32[]{:S(2)}) %collective-permute-start.5) | collective-permute-done | bytes 557088 | tf_op jit(solution)/shard_map/ppermute | solution.py:154
  31.1 1.8 collective-permute-start.17
  32.9 9.5 %collective-permute-done.10.own_ref = bf16[128,2048]{1,0:T(8,128)(2,1)S(1)} collective-permute-done((bf16[128,2048]{1,0:T(8,128)(2,1)S(1)}, bf16[128,2048]{1,0:T(8,128)(2,1)S(1)}, u32[]{:S(2)}, u32[]{:S(2)}) %collective-permute-start.10) | collective-permute-done | bytes 524320 | tf_op jit(solution)/shard_map/ppermute | solution.py:154
  42.4 1.8 collective-permute-start.18
  45.3 1.3 collective-permute-start
  46.6 7.2 %collective-permute-done.6.own_ref.meta_own = bf16[128,2176]{1,0:T(8,128)(2,1)S(1)} collective-permute-done((bf16[128,2176]{1,0:T(8,128)(2,1)S(1)}, bf16[128,2176]{1,0:T(8,128)(2,1)S(1)}, u32[]{:S(2)}, u32[]{:S(2)}) %collective-permute-start.6) | collective-permute-done | bytes 557088 | tf_op jit(solution)/shard_map/ppermute | solution.py:154
  53.7 1.5 collective-permute-start.15
  55.8 7.9 %shard_map.83 = (f32[256,1536]{1,0:T(8,128)S(1)}, f32[256,1536]{1,0:T(8,128)S(1)}) custom-call(bf16[128,2176]{1,0:T(8,128)(2,1)S(1)} %collective-permute-done.5.own_ref.meta_own, bf16[128,2176]{1,0:T(8,128)(2,1)S(1)} %collective-permute-done.17.far_ref.meta_far, bf16[2048,1536]{1,0:T(8,128)(2,1)} %bitcast.5, bf16[2048,1536]{1,0:T(8,128)(2,1)} %collective-permute-done.1.w1_ref), custom_call_target="tpu_custom_call" | custom-call | flops 3221225472 | bytes 15728640 | tf_op jit(solution)/shard_map/pallas_call | solution.py:32
  63.7 1.1 copy-done.1
  64.9 1.3 collective-permute-start.7
  66.2 16.6 %shard_map.84 = (bf16[128,2176]{1,0:T(8,128)(2,1)S(1)}, bf16[128,2176]{1,0:T(8,128)(2,1)S(1)}) custom-call(s32[2]{0:T(128)S(1)} %pad_add_fusion.experts_ref, f32[256,1536]{1,0:T(8,128)S(1)} %get-tuple-element.30.g0_ref.u0_ref, f32[256,1536]{1,0:T(8,128)S(1)} %get-tuple-element.30.g0_ref.u0_ref, f32[256,1536]{1,0:T(8,128)} %copy-done.1, ...), custom_call_target="tpu_custom_call" | custom-call | flops 4831838208 | bytes 22020096 | tf_op jit(solution)/shard_map/pallas_call | solution.py:118
  82.8 8.2 %collective-permute-done.14.far_ref.meta_far = bf16[128,2176]{1,0:T(8,128)(2,1)S(1)} collective-permute-done((bf16[128,2176]{1,0:T(8,128)(2,1)S(1)}, bf16[128,2176]{1,0:T(8,128)(2,1)S(1)}, u32[]{:S(2)}, u32[]{:S(2)}) %collective-permute-start.14) | collective-permute-done | bytes 557088 | tf_op jit(solution)/shard_map/ppermute | solution.py:154
  91.0 1.3 collective-permute-start.19
  92.3 7.9 %shard_map.81 = (f32[256,1536]{1,0:T(8,128)S(1)}, f32[256,1536]{1,0:T(8,128)S(1)}) custom-call(bf16[128,2176]{1,0:T(8,128)(2,1)S(1)} %collective-permute-done.6.own_ref.meta_own, bf16[128,2176]{1,0:T(8,128)(2,1)S(1)} %collective-permute-done.14.far_ref.meta_far, bf16[2048,1536]{1,0:T(8,128)(2,1)} %bitcast.7, bf16[2048,1536]{1,0:T(8,128)(2,1)} %collective-permute-done.1.w1_ref), custom_call_target="tpu_custom_call" | custom-call | flops 3221225472 | bytes 15728640 | tf_op jit(solution)/shard_map/pallas_call | solution.py:32
  100.2 1.1 copy-done
  102.1 1.3 collective-permute-start.12
  104.2 16.6 %shard_map.82 = (bf16[128,2176]{1,0:T(8,128)(2,1)S(1)}, bf16[128,2176]{1,0:T(8,128)(2,1)S(1)}) custom-call(s32[2]{0:T(128)S(1)} %pad_add_fusion.experts_ref, f32[256,1536]{1,0:T(8,128)S(1)} %get-tuple-element.26.g0_ref.u0_ref, f32[256,1536]{1,0:T(8,128)S(1)} %get-tuple-element.26.g0_ref.u0_ref, f32[256,1536]{1,0:T(8,128)} %copy-done, f32[256,1536]{1,0:T(8,128)} %copy-done, ...), custom_call_target="tpu_custom_call" | custom-call | flops 4831838208 | bytes 22020096 | tf_op jit(solution)/shard_map/pallas_call | solution.py:118
  120.8 1.3 collective-permute-start.16
  122.3 18.7 %collective-permute-done.8.far_ref.meta_far = bf16[128,2176]{1,0:T(8,128)(2,1)S(1)} collective-permute-done((bf16[128,2176]{1,0:T(8,128)(2,1)S(1)}, bf16[128,2176]{1,0:T(8,128)(2,1)S(1)}, u32[]{:S(2)}, u32[]{:S(2)}) %collective-permute-start.8) | collective-permute-done | bytes 557088 | tf_op jit(solution)/shard_map/ppermute | solution.py:154
  141.0 7.9 %shard_map.79 = (f32[256,1536]{1,0:T(8,128)S(1)}, f32[256,1536]{1,0:T(8,128)S(1)}) custom-call(bf16[128,2176]{1,0:T(8,128)(2,1)S(1)} %collective-permute-done.7.own_ref.meta_own, bf16[128,2176]{1,0:T(8,128)(2,1)S(1)} %collective-permute-done.8.far_ref.meta_far, bf16[2048,1536]{1,0:T(8,128)(2,1)} %bitcast.9, bf16[2048,1536]{1,0:T(8,128)(2,1)} %collective-permute-done.1.w1_ref), custom_call_target="tpu_custom_call" | custom-call | flops 3221225472 | bytes 15728640 | tf_op jit(solution)/shard_map/pallas_call | solution.py:32
  148.9 1.1 copy-done.3
  150.1 16.4 %shard_map.80 = (bf16[128,2176]{1,0:T(8,128)(2,1)S(1)}, bf16[128,2176]{1,0:T(8,128)(2,1)S(1)}) custom-call(s32[2]{0:T(128)S(1)} %pad_add_fusion.experts_ref, f32[256,1536]{1,0:T(8,128)S(1)} %get-tuple-element.22.g0_ref.u0_ref, f32[256,1536]{1,0:T(8,128)S(1)} %get-tuple-element.22.g0_ref.u0_ref, f32[256,1536]{1,0:T(8,128)} %copy-done.3, ...), custom_call_target="tpu_custom_call" | custom-call | flops 4831838208 | bytes 22020096 | tf_op jit(solution)/shard_map/pallas_call | solution.py:118
  167.4 1.6 collective-permute-start.21
  169.0 7.9 %shard_map.77 = (f32[256,1536]{1,0:T(8,128)S(1)}, f32[256,1536]{1,0:T(8,128)S(1)}) custom-call(bf16[128,2176]{1,0:T(8,128)(2,1)S(1)} %pad_maximum_fusion.own_ref.meta_own, bf16[128,2176]{1,0:T(8,128)(2,1)S(1)} %collective-permute-done.far_ref.meta_far, bf16[2048,1536]{1,0:T(8,128)(2,1)} %bitcast.11, bf16[2048,1536]{1,0:T(8,128)(2,1)} %collective-permute-done.1.w1_ref), custom_call_target="tpu_custom_call" | custom-call | flops 3221225472 | bytes 15728640 | tf_op jit(solution)/shard_map/pallas_call | solution.py:32
  177.0 1.1 copy-done.2
  178.1 16.4 %shard_map.78 = (bf16[128,2176]{1,0:T(8,128)(2,1)S(1)}, bf16[128,2176]{1,0:T(8,128)(2,1)S(1)}) custom-call(s32[2]{0:T(128)S(1)} %pad_add_fusion.experts_ref, f32[256,1536]{1,0:T(8,128)S(1)} %get-tuple-element.18.g0_ref.u0_ref, f32[256,1536]{1,0:T(8,128)S(1)} %get-tuple-element.18.g0_ref.u0_ref, f32[256,1536]{1,0:T(8,128)} %copy-done.2, ...), custom_call_target="tpu_custom_call" | custom-call | flops 4831838208 | bytes 22020096 | tf_op jit(solution)/shard_map/pallas_call | solution.py:118
  195.0 1.5 collective-permute-start.22
  196.5 7.6 %collective-permute-done.4 = bf16[128,2176]{1,0:T(8,128)(2,1)S(1)} collective-permute-done((bf16[128,2176]{1,0:T(8,128)(2,1)S(1)}, bf16[128,2176]{1,0:T(8,128)(2,1)S(1)}, u32[]{:S(2)}, u32[]{:S(2)}) %collective-permute-start.4) | collective-permute-done | bytes 557088 | tf_op jit(solution)/shard_map/ppermute | solution.py:154
  204.2 2.5 %collective-permute-done.22 = bf16[128,2176]{1,0:T(8,128)(2,1)S(1)} collective-permute-done((bf16[128,2176]{1,0:T(8,128)(2,1)S(1)}, bf16[128,2176]{1,0:T(8,128)(2,1)S(1)}, u32[]{:S(2)}, u32[]{:S(2)}) %collective-permute-start.22) | collective-permute-done | bytes 557088 | tf_op jit(solution)/shard_map/ppermute | solution.py:154
  (44 shorter events, 9.1 us)
Async XLA Ops:
  0.6 54.6 %collective-permute-start.1 = (bf16[2048,1536]{1,0:T(8,128)(2,1)}, bf16[2048,1536]{1,0:T(8,128)(2,1)}, u32[]{:S(2)}, u32[]{:S(2)}) collective-permute-start(bf16[2048,1536]{1,0:T(8,128)(2,1)} %bitcast.4), channel_id=1, source_target_pairs={{0,1},{1,0},{2,3},{3,2},{4,5},{5,4},{6,7},{7,6},{8,9},{9,8},{10,11... | collective-permute-start | bytes 18874376 | tf_op jit(solution)/shard_map/ppermute | solution.py:154
  1.1 63.7 %collective-permute-start.3 = (bf16[768,2048]{1,0:T(8,128)(2,1)}, bf16[768,2048]{1,0:T(8,128)(2,1)}, u32[]{:S(2)}, u32[]{:S(2)}) collective-permute-start(bf16[768,2048]{1,0:T(8,128)(2,1)} %bitcast.13), channel_id=1, source_target_pairs={{0,1},{1,0},{2,3},{3,2},{4,5},{5,4},{6,7},{7,6},{8,9},{9,8},{10,11... | collective-permute-start | bytes 9437192 | tf_op jit(solution)/shard_map/ppermute | solution.py:154
  1.2 18.0 %collective-permute-start.9 = (bf16[128,2048]{1,0:T(8,128)(2,1)}, bf16[128,2048]{1,0:T(8,128)(2,1)S(1)}, u32[]{:S(2)}, u32[]{:S(2)}) collective-permute-start(bf16[128,2048]{1,0:T(8,128)(2,1)} %own_ref.1), channel_id=1, source_target_pairs={{0,4},{1,5},{2,6},{3,7},{4,8},{5,9},{6,10},{7,11},{8,12},{9,13},{1... | collective-permute-start | bytes 1572872 | tf_op jit(solution)/shard_map/ppermute | solution.py:154
  6.2 24.9 %collective-permute-start.5 = (bf16[128,2176]{1,0:T(8,128)(2,1)S(1)}, bf16[128,2176]{1,0:T(8,128)(2,1)S(1)}, u32[]{:S(2)}, u32[]{:S(2)}) collective-permute-start(bf16[128,2176]{1,0:T(8,128)(2,1)S(1)} %pad_maximum_fusion.own_ref.meta_own), channel_id=1, source_target_pairs={{0,4},{1,5},{2,6},{3,7},{4,8},{5,9},{6,10},{7,11},{8,12},{9,13},{1... | collective-permute-start | bytes 1671176 | tf_op jit(solution)/shard_map/ppermute | solution.py:154
  19.2 23.2 %collective-permute-start.10 = (bf16[128,2048]{1,0:T(8,128)(2,1)S(1)}, bf16[128,2048]{1,0:T(8,128)(2,1)S(1)}, u32[]{:S(2)}, u32[]{:S(2)}) collective-permute-start(bf16[128,2048]{1,0:T(8,128)(2,1)S(1)} %collective-permute-done.9.own_ref), channel_id=1, source_target_pairs={{0,4},{1,5},{2,6},{3,7},{4,8},{5,9},{6,10},{7,11},{8,12},{9,13},{1... | collective-permute-start | bytes 1572872 | tf_op jit(solution)/shard_map/ppermute | solution.py:154
  31.1 14.2 %collective-permute-start.17 = (bf16[128,2176]{1,0:T(8,128)(2,1)S(1)}, bf16[128,2176]{1,0:T(8,128)(2,1)S(1)}, u32[]{:S(2)}, u32[]{:S(2)}) collective-permute-start(bf16[128,2176]{1,0:T(8,128)(2,1)S(1)} %collective-permute-done.5.own_ref.meta_own), channel_id=1, source_target_pairs={{0,2},{1,3},{2,0},{3,1},{4,6},{5,7},{6,4},{7,5},{8,10},{9,11},{10,... | collective-permute-start | bytes 1671176 | tf_op jit(solution)/shard_map/ppermute | solution.py:154
  32.9 20.9 %collective-permute-start.6 = (bf16[128,2176]{1,0:T(8,128)(2,1)S(1)}, bf16[128,2176]{1,0:T(8,128)(2,1)S(1)}, u32[]{:S(2)}, u32[]{:S(2)}) collective-permute-start(bf16[128,2176]{1,0:T(8,128)(2,1)S(1)} %collective-permute-done.5.own_ref.meta_own), channel_id=1, source_target_pairs={{0,4},{1,5},{2,6},{3,7},{4,8},{5,9},{6,10},{7,11},{8,12},{9,13},{1... | collective-permute-start | bytes 1671176 | tf_op jit(solution)/shard_map/ppermute | solution.py:154
  42.4 22.5 %collective-permute-start.18 = (bf16[128,2048]{1,0:T(8,128)(2,1)S(1)}, bf16[128,2048]{1,0:T(8,128)(2,1)}, u32[]{:S(2)}, u32[]{:S(2)}) collective-permute-start(bf16[128,2048]{1,0:T(8,128)(2,1)S(1)} %collective-permute-done.9.own_ref), channel_id=1, source_target_pairs={{0,2},{1,3},{2,0},{3,1},{4,6},{5,7},{6,4},{7,5},{8,10},{9,11},{10,... | collective-permute-start | bytes 1572872 | tf_op jit(solution)/shard_map/ppermute | solution.py:154
  45.3 123.7 %collective-permute-start = (bf16[128,2176]{1,0:T(8,128)(2,1)S(1)}, bf16[128,2176]{1,0:T(8,128)(2,1)S(1)}, u32[]{:S(2)}, u32[]{:S(2)}) collective-permute-start(bf16[128,2176]{1,0:T(8,128)(2,1)S(1)} %pad_maximum_fusion.own_ref.meta_own), channel_id=1, source_target_pairs={{0,2},{1,3},{2,0},{3,1},{4,6},{5,7},{6,4},{7,5},{8,10},{9,11},{10,... | collective-permute-start | bytes 1671176 | tf_op jit(solution)/shard_map/ppermute | solution.py:154
  53.7 47.6 %collective-permute-start.15 = (bf16[128,2048]{1,0:T(8,128)(2,1)S(1)}, bf16[128,2048]{1,0:T(8,128)(2,1)S(1)}, u32[]{:S(2)}, u32[]{:S(2)}) collective-permute-start(bf16[128,2048]{1,0:T(8,128)(2,1)S(1)} %collective-permute-done.10.own_ref), channel_id=1, source_target_pairs={{0,2},{1,3},{2,0},{3,1},{4,6},{5,7},{6,4},{7,5},{8,10},{9,11},{10,... | collective-permute-start | bytes 1572872 | tf_op jit(solution)/shard_map/ppermute | solution.py:154
  55.3 35.7 %collective-permute-start.14 = (bf16[128,2176]{1,0:T(8,128)(2,1)S(1)}, bf16[128,2176]{1,0:T(8,128)(2,1)S(1)}, u32[]{:S(2)}, u32[]{:S(2)}) collective-permute-start(bf16[128,2176]{1,0:T(8,128)(2,1)S(1)} %collective-permute-done.6.own_ref.meta_own), channel_id=1, source_target_pairs={{0,2},{1,3},{2,0},{3,1},{4,6},{5,7},{6,4},{7,5},{8,10},{9,11},{10,... | collective-permute-start | bytes 1671176 | tf_op jit(solution)/shard_map/ppermute | solution.py:154
  63.7 1.1 copy-start.1
  64.9 37.3 %collective-permute-start.11 = (bf16[128,2048]{1,0:T(8,128)(2,1)S(1)}, bf16[128,2048]{1,0:T(8,128)(2,1)S(1)}, u32[]{:S(2)}, u32[]{:S(2)}) collective-permute-start(bf16[128,2048]{1,0:T(8,128)(2,1)S(1)} %collective-permute-done.10.own_ref), channel_id=1, source_target_pairs={{0,4},{1,5},{2,6},{3,7},{4,8},{5,9},{6,10},{7,11},{8,12},{9,13},{1... | collective-permute-start | bytes 1572872 | tf_op jit(solution)/shard_map/ppermute | solution.py:154
  64.9 38.5 %collective-permute-start.7 = (bf16[128,2176]{1,0:T(8,128)(2,1)S(1)}, bf16[128,2176]{1,0:T(8,128)(2,1)S(1)}, u32[]{:S(2)}, u32[]{:S(2)}) collective-permute-start(bf16[128,2176]{1,0:T(8,128)(2,1)S(1)} %collective-permute-done.6.own_ref.meta_own), channel_id=1, source_target_pairs={{0,4},{1,5},{2,6},{3,7},{4,8},{5,9},{6,10},{7,11},{8,12},{9,13},{1... | collective-permute-start | bytes 1671176 | tf_op jit(solution)/shard_map/ppermute | solution.py:154
  91.0 10.4 %copy-start.4 = (bf16[128,2048]{1,0:T(8,128)(2,1)S(1)}, bf16[128,2048]{1,0:T(8,128)(2,1)}, u32[]{:S(2)}) copy-start(bf16[128,2048]{1,0:T(8,128)(2,1)} %own_ref.1) | copy-start | bytes 1572868
  91.0 29.8 %collective-permute-start.19 = (bf16[128,2176]{1,0:T(8,128)(2,1)S(1)}, bf16[128,2176]{1,0:T(8,128)(2,1)S(1)}, u32[]{:S(2)}, u32[]{:S(2)}) collective-permute-start(bf16[128,2176]{1,0:T(8,128)(2,1)S(1)} %get-tuple-element.33), channel_id=1, source_target_pairs={{0,2},{1,3},{2,0},{3,1},{4,6},{5,7},{6,4},{7,5},{8,10},{9,11},{10,... | collective-permute-start | bytes 1671176 | tf_op jit(solution)/shard_map/ppermute | solution.py:154
  100.2 1.1 copy-start
  101.4 76.7 %collective-permute-start.2 = (bf16[128,2048]{1,0:T(8,128)(2,1)S(1)}, bf16[128,2048]{1,0:T(8,128)(2,1)S(1)}, u32[]{:S(2)}, u32[]{:S(2)}) collective-permute-start(bf16[128,2048]{1,0:T(8,128)(2,1)S(1)} %copy-done.4), channel_id=1, source_target_pairs={{0,2},{1,3},{2,0},{3,1},{4,6},{5,7},{6,4},{7,5},{8,10},{9,11},{10,... | collective-permute-start | bytes 1572872 | tf_op jit(solution)/shard_map/ppermute | solution.py:154
  102.1 47.9 %collective-permute-start.12 = (bf16[128,2048]{1,0:T(8,128)(2,1)S(1)}, bf16[128,2048]{1,0:T(8,128)(2,1)S(1)}, u32[]{:S(2)}, u32[]{:S(2)}) collective-permute-start(bf16[128,2048]{1,0:T(8,128)(2,1)S(1)} %collective-permute-done.11.own_ref), channel_id=1, source_target_pairs={{0,2},{1,3},{2,0},{3,1},{4,6},{5,7},{6,4},{7,5},{8,10},{9,11},{10,... | collective-permute-start | bytes 1572872 | tf_op jit(solution)/shard_map/ppermute | solution.py:154
  103.4 37.6 %collective-permute-start.8 = (bf16[128,2176]{1,0:T(8,128)(2,1)S(1)}, bf16[128,2176]{1,0:T(8,128)(2,1)S(1)}, u32[]{:S(2)}, u32[]{:S(2)}) collective-permute-start(bf16[128,2176]{1,0:T(8,128)(2,1)S(1)} %collective-permute-done.7.own_ref.meta_own), channel_id=1, source_target_pairs={{0,2},{1,3},{2,0},{3,1},{4,6},{5,7},{6,4},{7,5},{8,10},{9,11},{10,... | collective-permute-start | bytes 1671176 | tf_op jit(solution)/shard_map/ppermute | solution.py:154
  120.8 46.4 %collective-permute-start.16 = (bf16[128,2176]{1,0:T(8,128)(2,1)S(1)}, bf16[128,2176]{1,0:T(8,128)(2,1)S(1)}, u32[]{:S(2)}, u32[]{:S(2)}) collective-permute-start(bf16[128,2176]{1,0:T(8,128)(2,1)S(1)} %get-tuple-element.29), channel_id=1, source_target_pairs={{0,2},{1,3},{2,0},{3,1},{4,6},{5,7},{6,4},{7,5},{8,10},{9,11},{10,... | collective-permute-start | bytes 1671176 | tf_op jit(solution)/shard_map/ppermute | solution.py:154
  141.0 26.2 %collective-permute-start.20 = (bf16[128,2176]{1,0:T(8,128)(2,1)S(1)}, bf16[128,2176]{1,0:T(8,128)(2,1)S(1)}, u32[]{:S(2)}, u32[]{:S(2)}) collective-permute-start(bf16[128,2176]{1,0:T(8,128)(2,1)S(1)} %add_convert_fusion.3), channel_id=1, source_target_pairs={{0,4},{1,5},{2,6},{3,7},{4,8},{5,9},{6,10},{7,11},{8,12},{9,13},{1... | collective-permute-start | bytes 1671176 | tf_op jit(solution)/shard_map/ppermute | solution.py:154
  148.9 1.1 copy-start.3
  166.5 28.3 %collective-permute-start.13 = (bf16[128,2176]{1,0:T(8,128)(2,1)S(1)}, bf16[128,2176]{1,0:T(8,128)(2,1)S(1)}, u32[]{:S(2)}, u32[]{:S(2)}) collective-permute-start(bf16[128,2176]{1,0:T(8,128)(2,1)S(1)} %get-tuple-element.25), channel_id=1, source_target_pairs={{0,2},{1,3},{2,0},{3,1},{4,6},{5,7},{6,4},{7,5},{8,10},{9,11},{10,... | collective-permute-start | bytes 1671176 | tf_op jit(solution)/shard_map/ppermute | solution.py:154
  167.4 27.4 %collective-permute-start.21 = (bf16[128,2176]{1,0:T(8,128)(2,1)S(1)}, bf16[128,2176]{1,0:T(8,128)(2,1)S(1)}, u32[]{:S(2)}, u32[]{:S(2)}) collective-permute-start(bf16[128,2176]{1,0:T(8,128)(2,1)S(1)} %add_convert_fusion.2), channel_id=1, source_target_pairs={{0,4},{1,5},{2,6},{3,7},{4,8},{5,9},{6,10},{7,11},{8,12},{9,13},{1... | collective-permute-start | bytes 1671176 | tf_op jit(solution)/shard_map/ppermute | solution.py:154
  177.0 1.1 copy-start.2
  194.6 9.6 %collective-permute-start.4 = (bf16[128,2176]{1,0:T(8,128)(2,1)S(1)}, bf16[128,2176]{1,0:T(8,128)(2,1)S(1)}, u32[]{:S(2)}, u32[]{:S(2)}) collective-permute-start(bf16[128,2176]{1,0:T(8,128)(2,1)S(1)} %get-tuple-element.21), channel_id=1, source_target_pairs={{0,2},{1,3},{2,0},{3,1},{4,6},{5,7},{6,4},{7,5},{8,10},{9,11},{10,... | collective-permute-start | bytes 1671176 | tf_op jit(solution)/shard_map/ppermute | solution.py:154
  195.0 11.7 %collective-permute-start.22 = (bf16[128,2176]{1,0:T(8,128)(2,1)S(1)}, bf16[128,2176]{1,0:T(8,128)(2,1)S(1)}, u32[]{:S(2)}, u32[]{:S(2)}) collective-permute-start(bf16[128,2176]{1,0:T(8,128)(2,1)S(1)} %add_convert_fusion.1), channel_id=1, source_target_pairs={{0,4},{1,5},{2,6},{3,7},{4,8},{5,9},{6,10},{7,11},{8,12},{9,13},{1... | collective-permute-start | bytes 1671176 | tf_op jit(solution)/shard_map/ppermute | solution.py:154
  206.7 1.1 copy-start.5

commit v2 on v0

v2 whole, which is shorter than its diff:
```python
import functools

import jax
import jax.numpy as jnp
from jax import lax
from jax.experimental import pallas as pl
from jax.experimental.pallas import tpu as pltpu
from jax.sharding import PartitionSpec as P

F32, BF16 = jnp.float32, jnp.bfloat16
LANES = 128
VMEM_BYTES = 16 * 2**20
COST = 30
NT = (((1,), (1,)), ((), ()))
LOCAL = pl.BlockSpec(memory_space=pltpu.VMEM)
SCALAR = pl.BlockSpec(memory_space=pltpu.SMEM)
ANYWHERE = pl.BlockSpec(memory_space=pl.ANY)


def resident(a):
    return pltpu.with_memory_space_constraint(a, pltpu.VMEM)


def call(kernel, ins, outs, scratch=(), flops=0):
    return pl.pallas_call(
        kernel,
        in_specs=ins,
        out_specs=[spec for spec, _ in outs],
        out_shape=[shape for _, shape in outs],
        scratch_shapes=list(scratch),
        compiler_params=pltpu.CompilerParams(vmem_limit_bytes=VMEM_BYTES),
        cost_estimate=pl.CostEstimate(flops=COST * flops // 100, bytes_accessed=1024, transcendentals=0),
    )


def array(*shape, dtype=BF16):
    return LOCAL, jax.ShapeDtypeStruct(shape, dtype)


def load_kernel(count, *refs):
    sems = refs[-1]
    copies = [pltpu.make_async_copy(refs[i], refs[count + i], sems.at[i]) for i in range(count)]
    for c in copies:
        c.start()
    for c in copies:
        c.wait()


def load(*arrays):
    n = len(arrays)
    return call(
        functools.partial(load_kernel, n), [ANYWHERE] * n, [array(*a.shape) for a in arrays],
        [pltpu.SemaphoreType.DMA((n,))],
    )(*arrays)


def choose_kernel(near, pair_ref, x_ref, _, out_ref, sel_ref, *same_ref):
    for ref in same_ref:
        ref[...] = x_ref[...]
    rows = x_ref.shape[0]
    table = x_ref[:, x_ref.shape[1] - LANES :].astype(F32)
    lane = lax.broadcasted_iota(jnp.int32, (8, LANES), 1)
    pick = jnp.where((lane == pair_ref[0]) | (lane == pair_ref[1]), 1.0, 0.0)
    named = jnp.where(table > 0.0, 1.0, 0.0)
    need = jnp.minimum(lax.dot_general(pick, named, NT, preferred_element_type=F32), 1.0)
    before = lax.broadcasted_iota(jnp.int32, (rows, rows), 0) < lax.broadcasted_iota(jnp.int32, (rows, rows), 1)
    place = jnp.dot(need, jnp.where(before, 1.0, 0.0), preferred_element_type=F32)
    slot = lax.broadcasted_iota(jnp.int32, (near, rows), 0)
    sel = jnp.where((place[:1].astype(jnp.int32) == slot) & (need[:1] > 0.0), 1.0, 0.0).astype(BF16)
    sel_ref[...] = sel
    out_ref[...] = jnp.dot(sel, x_ref[...], preferred_element_type=F32).astype(BF16)


def choose(pair, x, near, ticket, again):
    rows, width = x.shape
    return call(
        functools.partial(choose_kernel, near),
        [SCALAR, LOCAL, SCALAR],
        [array(near, width), array(near, rows)] + [array(*x.shape)] * again,
        flops=2 * near * rows * width,
    )(pair, resident(x), ticket)


def pack_kernel(sel_ref, g_ref, _, out_ref, *same_ref):
    for ref in same_ref:
        ref[...] = g_ref[...]
    out_ref[...] = jnp.dot(sel_ref[...], g_ref[...], preferred_element_type=F32).astype(BF16)


def pack(sel, g, ticket, again):
    near, rows = sel.shape
    width = g.shape[1]
    return call(
        pack_kernel, [LOCAL] * 2 + [SCALAR], [array(near, width)] + [array(*g.shape)] * again,
        flops=2 * near * rows * width,
    )(sel, resident(g), ticket)


def spread(sel_ref, back_ref, at):
    return lax.dot_general(
        sel_ref[...], back_ref[:, at], (((0,), (0,)), ((), ())), preferred_element_type=F32
    )


def gather_kernel(own_ref, back_ref, sel_ref, *refs):
    total = own_ref[...].astype(F32) + spread(sel_ref, back_ref, slice(None))
    if len(refs) > 1:
        total += refs[0][...].astype(F32)
    refs[-1][...] = total.astype(BF16)


def gather(own, back, sel, *carried):
    return call(
        gather_kernel, [LOCAL] * (3 + len(carried)), [array(*own.shape)], flops=2 * back.size * sel.shape[1]
    )(own, back, sel, *carried)[0]


def finish_kernel(own_ref, back_ref, sel_ref, carried_ref, ids_ref, out_ref, gates_ref):
    features = out_ref.shape[1]
    fanout = ids_ref.shape[1]
    total = own_ref[...].astype(F32) + spread(sel_ref, back_ref, slice(None)) + carried_ref[...].astype(F32)
    out_ref[...] = total[:, :features].astype(BF16)
    gates = total[:, features:]
    lane = lax.broadcasted_iota(jnp.int32, gates.shape, 1)
    column = lax.broadcasted_iota(jnp.int32, gates_ref.shape, 1)
    chosen = jnp.zeros(gates_ref.shape, F32)
    for k in range(fanout):
        value = jnp.sum(jnp.where(lane == ids_ref[:, k : k + 1], gates, 0.0), axis=1, keepdims=True)
        chosen = jnp.where(column == k, value, chosen)
    gates_ref[...] = chosen.astype(BF16)


def finish(own, back, sel, carried, ids):
    rows, width = own.shape
    return call(
        finish_kernel, [LOCAL] * 5, [array(rows, width - LANES), array(*ids.shape)],
        flops=2 * back.size * rows,
    )(own, back, sel, carried, ids)


def project_kernel(tile, ticket_ref, own_ref, far_ref, w0_ref, w1_ref, _, out0_ref, out1_ref, ticket_out, both):
    features, width = w0_ref.shape
    rows = own_ref.shape[0]
    both[:rows, :] = own_ref[:, :features]
    both[rows:, :] = far_ref[:, :features]
    for w_ref, out_ref in ((w0_ref, out0_ref), (w1_ref, out1_ref)):
        for j in range(width // tile):
            at = pl.ds(j * tile, tile)
            out_ref[:, at] = jnp.dot(both[...], w_ref[:, at], preferred_element_type=F32)
    for i in range(2):
        ticket_out[i] = ticket_ref[i]


def project(ticket, own, far, w0, w1, after, tile=512):
    rows = own.shape[0] + far.shape[0]
    features, width = w0.shape
    return call(
        functools.partial(project_kernel, tile),
        [SCALAR] + [LOCAL] * 4 + [ANYWHERE],
        [array(rows, width, dtype=F32)] * 2 + [(SCALAR, jax.ShapeDtypeStruct((2,), jnp.int32))],
        [pltpu.VMEM((rows, features), BF16)],
        flops=4 * rows * features * width,
    )(ticket, *map(resident, (own, far, w0, w1)), after)


def backward_kernel(
    tile, split, experts_ref, p0_ref, p1_ref, own_ref, far_ref, tok_own, tok_far, d0_ref, d1_ref, w0_ref, w1_ref,
    _, out_own, out_far, experts_out, both, meta, grads,
):
    hidden, features = d0_ref.shape
    parts, splits = hidden // tile, features // split
    rows = own_ref.shape[0]
    both[:rows, :] = own_ref[...]
    both[rows:, :] = far_ref[...]
    meta[:rows, :] = tok_own[:, features:].astype(F32)
    meta[rows:, :] = tok_far[:, features:].astype(F32)
    lane = lax.broadcasted_iota(jnp.int32, meta.shape, 1)
    gates = jnp.zeros(meta.shape, F32)
    for e, (p_ref, d_ref) in enumerate(((p0_ref, d0_ref), (p1_ref, d1_ref))):
        here = lane == experts_ref[e]
        scale = jnp.sum(jnp.where(here, meta[...], 0.0), axis=1, keepdims=True)
        total = jnp.zeros((meta.shape[0], 1), F32)
        for j in range(parts):
            hidden_grad = lax.dot_general(
                both[...], d_ref[pl.ds(j * tile, tile)], NT, preferred_element_type=F32
            )
            gate_pre = p_ref[:, pl.ds(j * tile, tile)]
            up_pre = p_ref[:, pl.ds(hidden + j * tile, tile)]
            sigmoid = 1.0 / (1.0 + jnp.exp(-gate_pre))
            active = gate_pre * sigmoid
            total += jnp.sum(hidden_grad * active * up_pre, axis=1, keepdims=True)
            scaled = scale * hidden_grad
            base = 2 * e * hidden + j * tile
            grads[:, pl.ds(base, tile)] = (
                scaled * up_pre * sigmoid * (1.0 + gate_pre * (1.0 - sigmoid))
            ).astype(BF16)
            grads[:, pl.ds(base + hidden, tile)] = (scaled * active).astype(BF16)
        gates += jnp.where(here, total, 0.0)
        experts_out[e] = experts_ref[e]
    out_own[:, features:] = gates[:rows].astype(BF16)
    out_far[:, features:] = gates[rows:].astype(BF16)
    for j in range(splits):
        at = pl.ds(j * split, split)
        out = lax.dot_general(grads[:, : 2 * hidden], w0_ref[at], NT, preferred_element_type=F32)
        out += lax.dot_general(grads[:, 2 * hidden :], w1_ref[at], NT, preferred_element_type=F32)
        out_own[:, at] = out[:rows].astype(BF16)
        out_far[:, at] = out[rows:].astype(BF16)


def backward(experts, p0, p1, own, far, tok_own, tok_far, d0, d1, w0, w1, after, tile=256, split=512):
    rows = own.shape[0] + far.shape[0]
    hidden, features = d0.shape
    return call(
        functools.partial(backward_kernel, tile, split),
        [SCALAR] + [LOCAL] * 10 + [ANYWHERE],
        [array(own.shape[0], features + LANES), array(far.shape[0], features + LANES)]
        + [(SCALAR, jax.ShapeDtypeStruct((2,), jnp.int32))],
        [pltpu.VMEM((rows, features), BF16), pltpu.VMEM((rows, LANES), F32), pltpu.VMEM((rows, 4 * hidden), BF16)],
        flops=12 * rows * features * hidden,
    )(experts, p0, p1, *map(resident, (own, far, tok_own, tok_far, d0, d1, w0, w1)), after)


def shards(lines, tokens, cotangent, expert_ids, gate_weights, w_gate_up, w_down):
    devices = lax.axis_size("expert")
    depth = devices // (2 * lines)
    rows, features = tokens.shape
    fanout = expert_ids.shape[1]
    capacity = 7 * rows * fanout // (4 * devices)
    near = min(rows, -(-2 * capacity // 16) * 16)
    index = lambda z, y, c: (z * lines + y) * 2 + c
    places = [(z, y, c) for z in range(depth) for y in range(lines) for c in range(2)]
    up = [(index(z, y, c), index((z + 1) % depth, y, c)) for z, y, c in places]
    across = [(index(z, y, c), index(z, 1 - y, c)) for z, y, c in places]
    twin = [(index(z, y, c), index(z, y, 1 - c)) for z, y, c in places]
    move = lambda a, pairs: lax.ppermute(a, "expert", pairs)

    me = lax.axis_index("expert")
    experts = jnp.stack([me, me ^ 1]).astype(jnp.int32)
    others = experts ^ 2
    at = expert_ids[:, :, None] == jnp.arange(LANES, dtype=jnp.int32)
    table = jnp.sum(jnp.where(at, gate_weights[:, :, None], 0), axis=1).astype(BF16)
    w0, d0 = w_gate_up[0], w_down[0]
    w1, d1 = move(w0, twin), move(d0, twin)
    w0, d0 = load(w0, d0)
    w1, d1 = load(w1, d1)
    x, g = jnp.concatenate([tokens, table], axis=1), cotangent
    nx, ng = move(x, up), move(g, up)
    xs, sel = choose(others, x, near, experts, False)
    gs, = pack(sel, g, experts, False)
    parts = []
    for s in range(depth):
        xf, gf = move(xs, across), move(gs, across)
        now = x, g, sel
        if s + 1 < depth:
            again = s + 2 < depth
            xs, sel, *kept = choose(others, nx, near, experts, again)
            x = kept[0] if again else nx
            if again:
                nx = move(x, up)
        p0, p1, experts = project(experts, now[0], xf, w0, w1, xs)
        if s + 1 < depth:
            gs, *kept = pack(sel, ng, experts, again)
            g = kept[0] if again else ng
            if again:
                ng = move(g, up)
        own, far, experts = backward(experts, p0, p1, now[1], gf, now[0], xf, d0, d1, w0, w1, gs)
        parts.append((own, move(far, across), now[2]))
    carried = ()
    for s in range(1, depth):
        carried = (move(gather(*parts[s], *carried), up),)
    return tuple(finish(*parts[0], *carried, expert_ids))


def solution(mesh):
    row, cube = P(("parts", "expert"), None), P(("parts", "expert"), None, None)
    body = functools.partial(shards, 2)
    return jax.shard_map(
        body, mesh=mesh, in_specs=(row, row, row, row, cube, cube), out_specs=(row, row), check_vma=False
    )
```

time: 349 us -> 150 us (0.43)
  the two profiles are of different devices: /device:TPU:15 before, /device:TPU:0 now
where the time goes in v2:
time: 150 us; the launch traced here: 149 us
  waiting for transfers between devices  58.9 us (39%)
  Pallas kernels  55.5 us (37%)
  starting transfers between devices  26.6 us (18%)
  local copies, waits for them, and re-layouts  5.44 us (4%)
  other arithmetic  2.06 us (1%)
    ppermute x23, waiting for transfers between devices, shards(): move = lambda a, pairs: lax.ppermute(a, 'expert', pairs)  58.9 us
    ppermute x23, starting transfers between devices, shards(): move = lambda a, pairs: lax.ppermute(a, 'expert', pairs)  26.6 us
    pallas_call x4, Pallas kernels, backward(): call(functools.partial(backward_kernel, tile, split), [SCALAR] + [LOCAL]...  26.3 us
    pallas_call x4, Pallas kernels, project(): call(functools.partial(project_kernel, tile), [SCALAR] + [LOCAL] * 4 + [A...  15 us
    unnamed x9, local copies, waits for them, and re-layouts  4.79 us
    pallas_call x4, Pallas kernels, choose(): call(functools.partial(choose_kernel, near), [SCALAR, LOCAL, SCALAR], [ar...  4.39 us
    pallas_call x2, Pallas kernels, load(): call(functools.partial(load_kernel, n), [ANYWHERE] * n, [array(*a.shape)...  4.37 us
    pallas_call x4, Pallas kernels, pack(): call(pack_kernel, [LOCAL] * 2 + [SCALAR], [array(near, width)] + [array(*...  3.27 us
  transfers between devices with their start and end apart: 23, of which 11 were waited for; matrix products, arithmetic and copies ran while one was open for 1% of the time, Pallas kernels for 36%

profile of v2, /device:TPU:0, one launch (start us, length us, event | category | flops | bytes accessed | tf_op | source)
XLA Modules:
  0.0 149.4 jit_solution(10973127770563198071)
XLA Ops:
  3.2 3.1 %collective-permute-start.3 = (bf16[128,2176]{1,0:T(8,128)(2,1)S(1)}, bf16[128,2176]{1,0:T(8,128)(2,1)S(1)}, u32[]{:S(2)}, u32[]{:S(2)}) collective-permute-start(bf16[128,2176]{1,0:T(8,128)(2,1)S(1)} %pad_maximum_fusion.x_ref.own_ref.tok_own), channel_id=1, source_target_pairs={{0,4},{1,5},{2,6},{3,7},{4,8},{5,9},{6,10},{7,11},{8,12},{9,13},{1... | collective-permute-start | bytes 1671176 | tf_op jit(solution)/shard_map/ppermute | solution.py:235
  7.4 1.6 %collective-permute-start = (bf16[112,2176]{1,0:T(8,128)(2,1)S(1)}, bf16[112,2176]{1,0:T(8,128)(2,1)S(1)}, u32[]{:S(2)}, u32[]{:S(2)}) collective-permute-start(bf16[112,2176]{1,0:T(8,128)(2,1)S(1)} %get-tuple-element.43), channel_id=1, source_target_pairs={{0,2},{1,3},{2,0},{3,1},{4,6},{5,7},{6,4},{7,5},{8,10},{9,11},{10,... | collective-permute-start | bytes 1462280 | tf_op jit(solution)/shard_map/ppermute | solution.py:235
  9.0 1.6 %collective-permute-start.5 = (bf16[128,2048]{1,0:T(8,128)(2,1)S(1)}, bf16[128,2048]{1,0:T(8,128)(2,1)S(1)}, u32[]{:S(2)}, u32[]{:S(2)}) collective-permute-start(bf16[128,2048]{1,0:T(8,128)(2,1)S(1)} %copy-done.2), channel_id=1, source_target_pairs={{0,4},{1,5},{2,6},{3,7},{4,8},{5,9},{6,10},{7,11},{8,12},{9,13},{1... | collective-permute-start | bytes 1572872 | tf_op jit(solution)/shard_map/ppermute | solution.py:235
  11.4 10.3 %collective-permute-done.3.x_ref = bf16[128,2176]{1,0:T(8,128)(2,1)S(1)} collective-permute-done((bf16[128,2176]{1,0:T(8,128)(2,1)S(1)}, bf16[128,2176]{1,0:T(8,128)(2,1)S(1)}, u32[]{:S(2)}, u32[]{:S(2)}) %collective-permute-start.3) | collective-permute-done | bytes 557088 | tf_op jit(solution)/shard_map/ppermute | solution.py:235
  21.7 1.8 %collective-permute-start.4 = (bf16[112,2048]{1,0:T(8,128)(2,1)S(1)}, bf16[112,2048]{1,0:T(8,128)(2,1)S(1)}, u32[]{:S(2)}, u32[]{:S(2)}) collective-permute-start(bf16[112,2048]{1,0:T(8,128)(2,1)S(1)} %shard_map.82), channel_id=1, source_target_pairs={{0,2},{1,3},{2,0},{3,1},{4,6},{5,7},{6,4},{7,5},{8,10},{9,11},{10,... | collective-permute-start | bytes 1376264 | tf_op jit(solution)/shard_map/ppermute | solution.py:235
  24.7 2.8 %copy-done = bf16[1,2048,1536]{2,1,0:T(8,128)(2,1)S(1)} copy-done((bf16[1,2048,1536]{2,1,0:T(8,128)(2,1)S(1)}, bf16[1,2048,1536]{2,1,0:T(8,128)(2,1)}, u32[]{:S(2)}) %copy-start) | copy-done | bytes 6291480
  27.5 1.9 %copy-done.1 = bf16[1,768,2048]{2,1,0:T(8,128)(2,1)S(1)} copy-done((bf16[1,768,2048]{2,1,0:T(8,128)(2,1)S(1)}, bf16[1,768,2048]{2,1,0:T(8,128)(2,1)}, u32[]{:S(2)}) %copy-start.1) | copy-done | bytes 3145752
  30.4 3.7 %shard_map.79 = (bf16[2048,1536]{1,0:T(8,128)(2,1)S(1)}, bf16[768,2048]{1,0:T(8,128)(2,1)S(1)}) custom-call(bf16[2048,1536]{1,0:T(8,128)(2,1)} %collective-permute-done.1.refs_0_, bf16[768,2048]{1,0:T(8,128)(2,1)} %collective-permute-done.2.refs_1_), custom_call_target="tpu_custom_call" | custom-call | bytes 1024 | tf_op jit(solution)/shard_map/pallas_call | solution.py:51
  34.1 3.8 %shard_map.81 = (f32[240,1536]{1,0:T(8,128)S(1)}, f32[240,1536]{1,0:T(8,128)S(1)}, s32[2]{0:T(128)S(1)}) custom-call(s32[2]{0:T(128)S(1)} %get-tuple-element.89._.ticket_ref, bf16[128,2176]{1,0:T(8,128)(2,1)S(1)} %pad_maximum_fusion.x_ref.own_ref.tok_own, bf16[112,2176]{1,0:T(8,128)(2,1)S(1)} %collective-permute-done.far_ref.tok_far, ...), custom_call_target="tpu_custom_call" | custom-call | flops 905969664 | bytes 1024 | tf_op jit(solution)/shard_map/pallas_call | solution.py:157
  38.7 1.6 %collective-permute-start.10 = (bf16[128,2048]{1,0:T(8,128)(2,1)S(1)}, bf16[128,2048]{1,0:T(8,128)(2,1)S(1)}, u32[]{:S(2)}, u32[]{:S(2)}) collective-permute-start(bf16[128,2048]{1,0:T(8,128)(2,1)S(1)} %get-tuple-element.63.own_ref), channel_id=1, source_target_pairs={{0,4},{1,5},{2,6},{3,7},{4,8},{5,9},{6,10},{7,11},{8,12},{9,13},{1... | collective-permute-start | bytes 1572872 | tf_op jit(solution)/shard_map/ppermute | solution.py:235
  40.4 1.5 %collective-permute-start.9 = (bf16[112,2048]{1,0:T(8,128)(2,1)S(1)}, bf16[112,2048]{1,0:T(8,128)(2,1)S(1)}, u32[]{:S(2)}, u32[]{:S(2)}) collective-permute-start(bf16[112,2048]{1,0:T(8,128)(2,1)S(1)} %get-tuple-element.54._), channel_id=1, source_target_pairs={{0,2},{1,3},{2,0},{3,1},{4,6},{5,7},{6,4},{7,5},{8,10},{9,11},{10,... | collective-permute-start | bytes 1376264 | tf_op jit(solution)/shard_map/ppermute | solution.py:235
  41.9 6.5 %shard_map.84 = (bf16[128,2176]{1,0:T(8,128)(2,1)S(1)}, bf16[112,2176]{1,0:T(8,128)(2,1)S(1)}, s32[2]{0:T(128)S(1)}) custom-call(s32[2]{0:T(128)S(1)} %get-tuple-element.47._.experts_ref, f32[240,1536]{1,0:T(8,128)S(1)} %get-tuple-element.48.p0_ref, f32[240,1536]{1,0:T(8,128)S(1)} %get-tuple-element.49.p1_ref, bf16[128,2048]{1,0:T(8,128)(2,1)S(1)} %copy-done.2, ...), custom_call_target="tpu_custom_call" | custom-call | flops 1358954496 | bytes 1024 | tf_op jit(solution)/shard_map/pallas_call | solution.py:213
  49.6 1.6 %collective-permute-start.12 = (bf16[128,2176]{1,0:T(8,128)(2,1)S(1)}, bf16[128,2176]{1,0:T(8,128)(2,1)S(1)}, u32[]{:S(2)}, u32[]{:S(2)}) collective-permute-start(bf16[128,2176]{1,0:T(8,128)(2,1)S(1)} %get-tuple-element.67.own_ref.tok_own), channel_id=1, source_target_pairs={{0,4},{1,5},{2,6},{3,7},{4,8},{5,9},{6,10},{7,11},{8,12},{9,13},{1... | collective-permute-start | bytes 1671176 | tf_op jit(solution)/shard_map/ppermute | solution.py:235
  51.7 3.8 %shard_map.86 = (f32[240,1536]{1,0:T(8,128)S(1)}, f32[240,1536]{1,0:T(8,128)S(1)}, s32[2]{0:T(128)S(1)}) custom-call(s32[2]{0:T(128)S(1)} %get-tuple-element.57._.ticket_ref, bf16[128,2176]{1,0:T(8,128)(2,1)S(1)} %get-tuple-element.58.own_ref.tok_own, bf16[112,2176]{1,0:T(8,128)(2,1)S(1)} %collective-permute-done.7.far_ref.tok_far, ...), custom_call_target="tpu_custom_call" | custom-call | flops 905969664 | bytes 1024 | tf_op jit(solution)/shard_map/pallas_call | solution.py:157
  57.0 1.4 collective-permute-start.14
  58.3 6.5 %shard_map.88 = (bf16[128,2176]{1,0:T(8,128)(2,1)S(1)}, bf16[112,2176]{1,0:T(8,128)(2,1)S(1)}, s32[2]{0:T(128)S(1)}) custom-call(s32[2]{0:T(128)S(1)} %get-tuple-element.60._.experts_ref, f32[240,1536]{1,0:T(8,128)S(1)} %get-tuple-element.61.p0_ref, f32[240,1536]{1,0:T(8,128)S(1)} %get-tuple-element.62.p1_ref, ...), custom_call_target="tpu_custom_call" | custom-call | flops 1358954496 | bytes 1024 | tf_op jit(solution)/shard_map/pallas_call | solution.py:213
  64.9 1.8 %collective-permute-start.19 = (bf16[112,2176]{1,0:T(8,128)(2,1)S(1)}, bf16[112,2176]{1,0:T(8,128)(2,1)S(1)}, u32[]{:S(2)}, u32[]{:S(2)}) collective-permute-start(bf16[112,2176]{1,0:T(8,128)(2,1)S(1)} %get-tuple-element.83), channel_id=1, source_target_pairs={{0,2},{1,3},{2,0},{3,1},{4,6},{5,7},{6,4},{7,5},{8,10},{9,11},{10,... | collective-permute-start | bytes 1462280 | tf_op jit(solution)/shard_map/ppermute | solution.py:235
  69.2 1.8 %collective-permute-start.15 = (bf16[112,2176]{1,0:T(8,128)(2,1)S(1)}, bf16[112,2176]{1,0:T(8,128)(2,1)S(1)}, u32[]{:S(2)}, u32[]{:S(2)}) collective-permute-start(bf16[112,2176]{1,0:T(8,128)(2,1)S(1)} %get-tuple-element.68._), channel_id=1, source_target_pairs={{0,2},{1,3},{2,0},{3,1},{4,6},{5,7},{6,4},{7,5},{8,10},{9,11},{10,... | collective-permute-start | bytes 1462280 | tf_op jit(solution)/shard_map/ppermute | solution.py:235
  71.0 3.8 %shard_map.90 = (f32[240,1536]{1,0:T(8,128)S(1)}, f32[240,1536]{1,0:T(8,128)S(1)}, s32[2]{0:T(128)S(1)}) custom-call(s32[2]{0:T(128)S(1)} %get-tuple-element.66._.ticket_ref, bf16[128,2176]{1,0:T(8,128)(2,1)S(1)} %get-tuple-element.67.own_ref.tok_own, bf16[112,2176]{1,0:T(8,128)(2,1)S(1)} %collective-permute-done.11.far_ref.tok_far, ...), custom_call_target="tpu_custom_call" | custom-call | flops 905969664 | bytes 1024 | tf_op jit(solution)/shard_map/pallas_call | solution.py:157
  74.8 4.3 %collective-permute-done.19.back_ref = bf16[112,2176]{1,0:T(8,128)(2,1)S(1)} collective-permute-done((bf16[112,2176]{1,0:T(8,128)(2,1)S(1)}, bf16[112,2176]{1,0:T(8,128)(2,1)S(1)}, u32[]{:S(2)}, u32[]{:S(2)}) %collective-permute-start.19) | collective-permute-done | bytes 487456 | tf_op jit(solution)/shard_map/ppermute | solution.py:235
  80.9 7.9 %collective-permute-done.13.far_ref = bf16[112,2048]{1,0:T(8,128)(2,1)S(1)} collective-permute-done((bf16[112,2048]{1,0:T(8,128)(2,1)S(1)}, bf16[112,2048]{1,0:T(8,128)(2,1)S(1)}, u32[]{:S(2)}, u32[]{:S(2)}) %collective-permute-start.13) | collective-permute-done | bytes 458784 | tf_op jit(solution)/shard_map/ppermute | solution.py:235
  88.9 6.6 %shard_map.92 = (bf16[128,2176]{1,0:T(8,128)(2,1)S(1)}, bf16[112,2176]{1,0:T(8,128)(2,1)S(1)}, s32[2]{0:T(128)S(1)}) custom-call(s32[2]{0:T(128)S(1)} %get-tuple-element.69._.experts_ref, f32[240,1536]{1,0:T(8,128)S(1)} %get-tuple-element.70.p0_ref, f32[240,1536]{1,0:T(8,128)S(1)} %get-tuple-element.71.p1_ref, ...), custom_call_target="tpu_custom_call" | custom-call | flops 1358954496 | bytes 1024 | tf_op jit(solution)/shard_map/pallas_call | solution.py:213
  95.5 1.8 %collective-permute-start.18 = (bf16[112,2176]{1,0:T(8,128)(2,1)S(1)}, bf16[112,2176]{1,0:T(8,128)(2,1)S(1)}, u32[]{:S(2)}, u32[]{:S(2)}) collective-permute-start(bf16[112,2176]{1,0:T(8,128)(2,1)S(1)} %get-tuple-element.81), channel_id=1, source_target_pairs={{0,2},{1,3},{2,0},{3,1},{4,6},{5,7},{6,4},{7,5},{8,10},{9,11},{10,... | collective-permute-start | bytes 1462280 | tf_op jit(solution)/shard_map/ppermute | solution.py:235
  97.6 1.7 %collective-permute-done.15.far_ref.tok_far = bf16[112,2176]{1,0:T(8,128)(2,1)S(1)} collective-permute-done((bf16[112,2176]{1,0:T(8,128)(2,1)S(1)}, bf16[112,2176]{1,0:T(8,128)(2,1)S(1)}, u32[]{:S(2)}, u32[]{:S(2)}) %collective-permute-start.15) | collective-permute-done | bytes 487456 | tf_op jit(solution)/shard_map/ppermute | solution.py:235
  99.3 3.8 %shard_map.93 = (f32[240,1536]{1,0:T(8,128)S(1)}, f32[240,1536]{1,0:T(8,128)S(1)}, s32[2]{0:T(128)S(1)}) custom-call(s32[2]{0:T(128)S(1)} %get-tuple-element.74.ticket_ref, bf16[128,2176]{1,0:T(8,128)(2,1)S(1)} %collective-permute-done.12.x_ref.own_ref.tok_own, bf16[112,2176]{1,0:T(8,128)(2,1)S(1)} %collective-permute-done.15.far_ref.tok_far, ...), custom_call_target="tpu_custom_call" | custom-call | flops 905969664 | bytes 1024 | tf_op jit(solution)/shard_map/pallas_call | solution.py:157
  103.1 6.7 %collective-permute-done.18.back_ref = bf16[112,2176]{1,0:T(8,128)(2,1)S(1)} collective-permute-done((bf16[112,2176]{1,0:T(8,128)(2,1)S(1)}, bf16[112,2176]{1,0:T(8,128)(2,1)S(1)}, u32[]{:S(2)}, u32[]{:S(2)}) %collective-permute-start.18) | collective-permute-done | bytes 487456 | tf_op jit(solution)/shard_map/ppermute | solution.py:235
  110.7 5.8 %collective-permute-done.16.far_ref = bf16[112,2048]{1,0:T(8,128)(2,1)S(1)} collective-permute-done((bf16[112,2048]{1,0:T(8,128)(2,1)S(1)}, bf16[112,2048]{1,0:T(8,128)(2,1)S(1)}, u32[]{:S(2)}, u32[]{:S(2)}) %collective-permute-start.16) | collective-permute-done | bytes 458784 | tf_op jit(solution)/shard_map/ppermute | solution.py:235
  116.4 6.5 %shard_map.94 = (bf16[128,2176]{1,0:T(8,128)(2,1)S(1)}, bf16[112,2176]{1,0:T(8,128)(2,1)S(1)}, s32[2]{0:T(128)}) custom-call(s32[2]{0:T(128)S(1)} %get-tuple-element.75.experts_ref, f32[240,1536]{1,0:T(8,128)S(1)} %get-tuple-element.76.p0_ref, f32[240,1536]{1,0:T(8,128)S(1)} %get-tuple-element.77.p1_ref, ...), custom_call_target="tpu_custom_call" | custom-call | flops 1358954496 | bytes 1024 | tf_op jit(solution)/shard_map/pallas_call | solution.py:213
  124.4 8.8 %collective-permute-done.17.back_ref = bf16[112,2176]{1,0:T(8,128)(2,1)S(1)} collective-permute-done((bf16[112,2176]{1,0:T(8,128)(2,1)S(1)}, bf16[112,2176]{1,0:T(8,128)(2,1)S(1)}, u32[]{:S(2)}, u32[]{:S(2)}) %collective-permute-start.17) | collective-permute-done | bytes 487456 | tf_op jit(solution)/shard_map/ppermute | solution.py:235
  134.4 1.5 %collective-permute-start.6 = (bf16[112,2176]{1,0:T(8,128)(2,1)S(1)}, bf16[112,2176]{1,0:T(8,128)(2,1)S(1)}, u32[]{:S(2)}, u32[]{:S(2)}) collective-permute-start(bf16[112,2176]{1,0:T(8,128)(2,1)S(1)} %get-tuple-element.56), channel_id=1, source_target_pairs={{0,2},{1,3},{2,0},{3,1},{4,6},{5,7},{6,4},{7,5},{8,10},{9,11},{10,... | collective-permute-start | bytes 1462280 | tf_op jit(solution)/shard_map/ppermute | solution.py:235
  136.0 7.5 %collective-permute-done.6.back_ref = bf16[112,2176]{1,0:T(8,128)(2,1)S(1)} collective-permute-done((bf16[112,2176]{1,0:T(8,128)(2,1)S(1)}, bf16[112,2176]{1,0:T(8,128)(2,1)S(1)}, u32[]{:S(2)}, u32[]{:S(2)}) %collective-permute-start.6) | collective-permute-done | bytes 487456 | tf_op jit(solution)/shard_map/ppermute | solution.py:235
  143.5 4.0 %collective-permute-done.22.carried_ref = bf16[128,2176]{1,0:T(8,128)(2,1)S(1)} collective-permute-done((bf16[128,2176]{1,0:T(8,128)(2,1)S(1)}, bf16[128,2176]{1,0:T(8,128)(2,1)S(1)}, u32[]{:S(2)}, u32[]{:S(2)}) %collective-permute-start.22) | collective-permute-done | bytes 557088 | tf_op jit(solution)/shard_map/ppermute | solution.py:235
  (49 shorter events, 20.7 us)
Async XLA Ops:
  0.6 8.4 %copy-start.2 = (bf16[128,2048]{1,0:T(8,128)(2,1)S(1)}, bf16[128,2048]{1,0:T(8,128)(2,1)}, u32[]{:S(2)}) copy-start(bf16[128,2048]{1,0:T(8,128)(2,1)} %own_ref.1) | copy-start | bytes 1572868
  0.6 29.4 %collective-permute-start.1 = (bf16[2048,1536]{1,0:T(8,128)(2,1)}, bf16[2048,1536]{1,0:T(8,128)(2,1)}, u32[]{:S(2)}, u32[]{:S(2)}) collective-permute-start(bf16[2048,1536]{1,0:T(8,128)(2,1)} %bitcast.4), channel_id=1, source_target_pairs={{0,1},{1,0},{2,3},{3,2},{4,5},{5,4},{6,7},{7,6},{8,9},{9,8},{10,11... | collective-permute-start | bytes 18874376 | tf_op jit(solution)/shard_map/ppermute | solution.py:235
  1.2 23.5 %collective-permute-start.2 = (bf16[768,2048]{1,0:T(8,128)(2,1)}, bf16[768,2048]{1,0:T(8,128)(2,1)}, u32[]{:S(2)}, u32[]{:S(2)}) collective-permute-start(bf16[768,2048]{1,0:T(8,128)(2,1)} %bitcast.6), channel_id=1, source_target_pairs={{0,1},{1,0},{2,3},{3,2},{4,5},{5,4},{6,7},{7,6},{8,9},{9,8},{10,11... | collective-permute-start | bytes 9437192 | tf_op jit(solution)/shard_map/ppermute | solution.py:235
  3.2 18.5 %collective-permute-start.3 = (bf16[128,2176]{1,0:T(8,128)(2,1)S(1)}, bf16[128,2176]{1,0:T(8,128)(2,1)S(1)}, u32[]{:S(2)}, u32[]{:S(2)}) collective-permute-start(bf16[128,2176]{1,0:T(8,128)(2,1)S(1)} %pad_maximum_fusion.x_ref.own_ref.tok_own), channel_id=1, source_target_pairs={{0,4},{1,5},{2,6},{3,7},{4,8},{5,9},{6,10},{7,11},{8,12},{9,13},{1... | collective-permute-start | bytes 1671176 | tf_op jit(solution)/shard_map/ppermute | solution.py:235
  7.4 26.7 %collective-permute-start = (bf16[112,2176]{1,0:T(8,128)(2,1)S(1)}, bf16[112,2176]{1,0:T(8,128)(2,1)S(1)}, u32[]{:S(2)}, u32[]{:S(2)}) collective-permute-start(bf16[112,2176]{1,0:T(8,128)(2,1)S(1)} %get-tuple-element.43), channel_id=1, source_target_pairs={{0,2},{1,3},{2,0},{3,1},{4,6},{5,7},{6,4},{7,5},{8,10},{9,11},{10,... | collective-permute-start | bytes 1462280 | tf_op jit(solution)/shard_map/ppermute | solution.py:235
  9.0 28.9 %collective-permute-start.5 = (bf16[128,2048]{1,0:T(8,128)(2,1)S(1)}, bf16[128,2048]{1,0:T(8,128)(2,1)S(1)}, u32[]{:S(2)}, u32[]{:S(2)}) collective-permute-start(bf16[128,2048]{1,0:T(8,128)(2,1)S(1)} %copy-done.2), channel_id=1, source_target_pairs={{0,4},{1,5},{2,6},{3,7},{4,8},{5,9},{6,10},{7,11},{8,12},{9,13},{1... | collective-permute-start | bytes 1572872 | tf_op jit(solution)/shard_map/ppermute | solution.py:235
  21.7 20.2 %collective-permute-start.4 = (bf16[112,2048]{1,0:T(8,128)(2,1)S(1)}, bf16[112,2048]{1,0:T(8,128)(2,1)S(1)}, u32[]{:S(2)}, u32[]{:S(2)}) collective-permute-start(bf16[112,2048]{1,0:T(8,128)(2,1)S(1)} %shard_map.82), channel_id=1, source_target_pairs={{0,2},{1,3},{2,0},{3,1},{4,6},{5,7},{6,4},{7,5},{8,10},{9,11},{10,... | collective-permute-start | bytes 1376264 | tf_op jit(solution)/shard_map/ppermute | solution.py:235
  24.6 23.8 %collective-permute-start.8 = (bf16[128,2176]{1,0:T(8,128)(2,1)S(1)}, bf16[128,2176]{1,0:T(8,128)(2,1)S(1)}, u32[]{:S(2)}, u32[]{:S(2)}) collective-permute-start(bf16[128,2176]{1,0:T(8,128)(2,1)S(1)} %get-tuple-element.58.own_ref.tok_own), channel_id=1, source_target_pairs={{0,4},{1,5},{2,6},{3,7},{4,8},{5,9},{6,10},{7,11},{8,12},{9,13},{1... | collective-permute-start | bytes 1671176 | tf_op jit(solution)/shard_map/ppermute | solution.py:235
  24.7 2.8 %copy-start = (bf16[1,2048,1536]{2,1,0:T(8,128)(2,1)S(1)}, bf16[1,2048,1536]{2,1,0:T(8,128)(2,1)}, u32[]{:S(2)}) copy-start(bf16[1,2048,1536]{2,1,0:T(8,128)(2,1)} %param.10) | copy-start | bytes 18874372
  27.5 1.9 %copy-start.1 = (bf16[1,768,2048]{2,1,0:T(8,128)(2,1)S(1)}, bf16[1,768,2048]{2,1,0:T(8,128)(2,1)}, u32[]{:S(2)}) copy-start(bf16[1,768,2048]{2,1,0:T(8,128)(2,1)} %param.11) | copy-start | bytes 9437188
  30.0 21.7 %collective-permute-start.7 = (bf16[112,2176]{1,0:T(8,128)(2,1)S(1)}, bf16[112,2176]{1,0:T(8,128)(2,1)S(1)}, u32[]{:S(2)}, u32[]{:S(2)}) collective-permute-start(bf16[112,2176]{1,0:T(8,128)(2,1)S(1)} %get-tuple-element.46._), channel_id=1, source_target_pairs={{0,2},{1,3},{2,0},{3,1},{4,6},{5,7},{6,4},{7,5},{8,10},{9,11},{10,... | collective-permute-start | bytes 1462280 | tf_op jit(solution)/shard_map/ppermute | solution.py:235
  38.7 17.4 %collective-permute-start.10 = (bf16[128,2048]{1,0:T(8,128)(2,1)S(1)}, bf16[128,2048]{1,0:T(8,128)(2,1)S(1)}, u32[]{:S(2)}, u32[]{:S(2)}) collective-permute-start(bf16[128,2048]{1,0:T(8,128)(2,1)S(1)} %get-tuple-element.63.own_ref), channel_id=1, source_target_pairs={{0,4},{1,5},{2,6},{3,7},{4,8},{5,9},{6,10},{7,11},{8,12},{9,13},{1... | collective-permute-start | bytes 1572872 | tf_op jit(solution)/shard_map/ppermute | solution.py:235
  40.4 18.0 %collective-permute-start.9 = (bf16[112,2048]{1,0:T(8,128)(2,1)S(1)}, bf16[112,2048]{1,0:T(8,128)(2,1)S(1)}, u32[]{:S(2)}, u32[]{:S(2)}) collective-permute-start(bf16[112,2048]{1,0:T(8,128)(2,1)S(1)} %get-tuple-element.54._), channel_id=1, source_target_pairs={{0,2},{1,3},{2,0},{3,1},{4,6},{5,7},{6,4},{7,5},{8,10},{9,11},{10,... | collective-permute-start | bytes 1376264 | tf_op jit(solution)/shard_map/ppermute | solution.py:235
  49.6 18.5 %collective-permute-start.12 = (bf16[128,2176]{1,0:T(8,128)(2,1)S(1)}, bf16[128,2176]{1,0:T(8,128)(2,1)S(1)}, u32[]{:S(2)}, u32[]{:S(2)}) collective-permute-start(bf16[128,2176]{1,0:T(8,128)(2,1)S(1)} %get-tuple-element.67.own_ref.tok_own), channel_id=1, source_target_pairs={{0,4},{1,5},{2,6},{3,7},{4,8},{5,9},{6,10},{7,11},{8,12},{9,13},{1... | collective-permute-start | bytes 1671176 | tf_op jit(solution)/shard_map/ppermute | solution.py:235
  51.2 19.8 %collective-permute-start.11 = (bf16[112,2176]{1,0:T(8,128)(2,1)S(1)}, bf16[112,2176]{1,0:T(8,128)(2,1)S(1)}, u32[]{:S(2)}, u32[]{:S(2)}) collective-permute-start(bf16[112,2176]{1,0:T(8,128)(2,1)S(1)} %get-tuple-element.59._), channel_id=1, source_target_pairs={{0,2},{1,3},{2,0},{3,1},{4,6},{5,7},{6,4},{7,5},{8,10},{9,11},{10,... | collective-permute-start | bytes 1462280 | tf_op jit(solution)/shard_map/ppermute | solution.py:235
  57.0 23.1 %collective-permute-start.14 = (bf16[128,2048]{1,0:T(8,128)(2,1)S(1)}, bf16[128,2048]{1,0:T(8,128)(2,1)S(1)}, u32[]{:S(2)}, u32[]{:S(2)}) collective-permute-start(bf16[128,2048]{1,0:T(8,128)(2,1)S(1)} %get-tuple-element.72.own_ref), channel_id=1, source_target_pairs={{0,4},{1,5},{2,6},{3,7},{4,8},{5,9},{6,10},{7,11},{8,12},{9,13},{1... | collective-permute-start | bytes 1572872 | tf_op jit(solution)/shard_map/ppermute | solution.py:235
  64.9 14.1 %collective-permute-start.19 = (bf16[112,2176]{1,0:T(8,128)(2,1)S(1)}, bf16[112,2176]{1,0:T(8,128)(2,1)S(1)}, u32[]{:S(2)}, u32[]{:S(2)}) collective-permute-start(bf16[112,2176]{1,0:T(8,128)(2,1)S(1)} %get-tuple-element.83), channel_id=1, source_target_pairs={{0,2},{1,3},{2,0},{3,1},{4,6},{5,7},{6,4},{7,5},{8,10},{9,11},{10,... | collective-permute-start | bytes 1462280 | tf_op jit(solution)/shard_map/ppermute | solution.py:235
  66.7 22.2 %collective-permute-start.13 = (bf16[112,2048]{1,0:T(8,128)(2,1)S(1)}, bf16[112,2048]{1,0:T(8,128)(2,1)S(1)}, u32[]{:S(2)}, u32[]{:S(2)}) collective-permute-start(bf16[112,2048]{1,0:T(8,128)(2,1)S(1)} %get-tuple-element.65._), channel_id=1, source_target_pairs={{0,2},{1,3},{2,0},{3,1},{4,6},{5,7},{6,4},{7,5},{8,10},{9,11},{10,... | collective-permute-start | bytes 1376264 | tf_op jit(solution)/shard_map/ppermute | solution.py:235
  69.2 30.1 %collective-permute-start.15 = (bf16[112,2176]{1,0:T(8,128)(2,1)S(1)}, bf16[112,2176]{1,0:T(8,128)(2,1)S(1)}, u32[]{:S(2)}, u32[]{:S(2)}) collective-permute-start(bf16[112,2176]{1,0:T(8,128)(2,1)S(1)} %get-tuple-element.68._), channel_id=1, source_target_pairs={{0,2},{1,3},{2,0},{3,1},{4,6},{5,7},{6,4},{7,5},{8,10},{9,11},{10,... | collective-permute-start | bytes 1462280 | tf_op jit(solution)/shard_map/ppermute | solution.py:235
  79.4 30.4 %collective-permute-start.20 = (bf16[128,2176]{1,0:T(8,128)(2,1)S(1)}, bf16[128,2176]{1,0:T(8,128)(2,1)S(1)}, u32[]{:S(2)}, u32[]{:S(2)}) collective-permute-start(bf16[128,2176]{1,0:T(8,128)(2,1)S(1)} %shard_map.95), channel_id=1, source_target_pairs={{0,4},{1,5},{2,6},{3,7},{4,8},{5,9},{6,10},{7,11},{8,12},{9,13},{1... | collective-permute-start | bytes 1671176 | tf_op jit(solution)/shard_map/ppermute | solution.py:235
  95.5 14.3 %collective-permute-start.18 = (bf16[112,2176]{1,0:T(8,128)(2,1)S(1)}, bf16[112,2176]{1,0:T(8,128)(2,1)S(1)}, u32[]{:S(2)}, u32[]{:S(2)}) collective-permute-start(bf16[112,2176]{1,0:T(8,128)(2,1)S(1)} %get-tuple-element.81), channel_id=1, source_target_pairs={{0,2},{1,3},{2,0},{3,1},{4,6},{5,7},{6,4},{7,5},{8,10},{9,11},{10,... | collective-permute-start | bytes 1462280 | tf_op jit(solution)/shard_map/ppermute | solution.py:235
  97.3 19.1 %collective-permute-start.16 = (bf16[112,2048]{1,0:T(8,128)(2,1)S(1)}, bf16[112,2048]{1,0:T(8,128)(2,1)S(1)}, u32[]{:S(2)}, u32[]{:S(2)}) collective-permute-start(bf16[112,2048]{1,0:T(8,128)(2,1)S(1)} %shard_map.91._), channel_id=1, source_target_pairs={{0,2},{1,3},{2,0},{3,1},{4,6},{5,7},{6,4},{7,5},{8,10},{9,11},{10,... | collective-permute-start | bytes 1376264 | tf_op jit(solution)/shard_map/ppermute | solution.py:235
  110.1 23.0 %collective-permute-start.21 = (bf16[128,2176]{1,0:T(8,128)(2,1)S(1)}, bf16[128,2176]{1,0:T(8,128)(2,1)S(1)}, u32[]{:S(2)}, u32[]{:S(2)}) collective-permute-start(bf16[128,2176]{1,0:T(8,128)(2,1)S(1)} %shard_map.96), channel_id=1, source_target_pairs={{0,4},{1,5},{2,6},{3,7},{4,8},{5,9},{6,10},{7,11},{8,12},{9,13},{1... | collective-permute-start | bytes 1671176 | tf_op jit(solution)/shard_map/ppermute | solution.py:235
  123.0 12.9 %copy-start.3 = (s32[128,4]{0,1:T(4,128)S(1)}, s32[128,4]{0,1:T(4,128)}, u32[]{:S(2)}) copy-start(s32[128,4]{0,1:T(4,128)} %param.8) | copy-start | bytes 6148
  123.0 10.2 %collective-permute-start.17 = (bf16[112,2176]{1,0:T(8,128)(2,1)S(1)}, bf16[112,2176]{1,0:T(8,128)(2,1)S(1)}, u32[]{:S(2)}, u32[]{:S(2)}) collective-permute-start(bf16[112,2176]{1,0:T(8,128)(2,1)S(1)} %get-tuple-element.79), channel_id=1, source_target_pairs={{0,2},{1,3},{2,0},{3,1},{4,6},{5,7},{6,4},{7,5},{8,10},{9,11},{10,... | collective-permute-start | bytes 1462280 | tf_op jit(solution)/shard_map/ppermute | solution.py:235
  133.6 14.0 %collective-permute-start.22 = (bf16[128,2176]{1,0:T(8,128)(2,1)S(1)}, bf16[128,2176]{1,0:T(8,128)(2,1)S(1)}, u32[]{:S(2)}, u32[]{:S(2)}) collective-permute-start(bf16[128,2176]{1,0:T(8,128)(2,1)S(1)} %shard_map.97), channel_id=1, source_target_pairs={{0,4},{1,5},{2,6},{3,7},{4,8},{5,9},{6,10},{7,11},{8,12},{9,13},{1... | collective-permute-start | bytes 1671176 | tf_op jit(solution)/shard_map/ppermute | solution.py:235
  134.4 9.1 %collective-permute-start.6 = (bf16[112,2176]{1,0:T(8,128)(2,1)S(1)}, bf16[112,2176]{1,0:T(8,128)(2,1)S(1)}, u32[]{:S(2)}, u32[]{:S(2)}) collective-permute-start(bf16[112,2176]{1,0:T(8,128)(2,1)S(1)} %get-tuple-element.56), channel_id=1, source_target_pairs={{0,2},{1,3},{2,0},{3,1},{4,6},{5,7},{6,4},{7,5},{8,10},{9,11},{10,... | collective-permute-start | bytes 1462280 | tf_op jit(solution)/shard_map/ppermute | solution.py:235

commit v3 on v2

v3 whole, which is shorter than its diff:
```python
import functools

import jax
import jax.numpy as jnp
from jax import lax
from jax.experimental import pallas as pl
from jax.experimental.pallas import tpu as pltpu
from jax.sharding import PartitionSpec as P

F32, BF16 = jnp.float32, jnp.bfloat16
LANES = 128
VMEM_BYTES = 16 * 2**20
COST = 30
HOLD = 8 * 10**9, 0, 8 * 10**9
NT = (((1,), (1,)), ((), ()))
LOCAL = pl.BlockSpec(memory_space=pltpu.VMEM)
SCALAR = pl.BlockSpec(memory_space=pltpu.SMEM)
ANYWHERE = pl.BlockSpec(memory_space=pl.ANY)


def array(*shape, dtype=BF16):
    return jax.ShapeDtypeStruct(shape, dtype)


class Queue:
    def __init__(self, ticket):
        self.ticket = ticket

    def run(self, kernel, operands, outs, scratch=(), flops=0, anywhere=0):
        def body(ticket_ref, *refs):
            n = len(operands) + len(outs)
            kernel(ticket_ref, *refs[:n], *refs[n + 1 :])
            for i in range(4):
                refs[n][i] = ticket_ref[i]

        *results, self.ticket = pl.pallas_call(
            body,
            in_specs=[SCALAR] + [ANYWHERE] * anywhere + [LOCAL] * (len(operands) - anywhere),
            out_specs=[LOCAL] * len(outs) + [SCALAR],
            out_shape=list(outs) + [array(4, dtype=jnp.int32)],
            scratch_shapes=list(scratch),
            compiler_params=pltpu.CompilerParams(vmem_limit_bytes=VMEM_BYTES),
            cost_estimate=pl.CostEstimate(flops=COST * flops // 100, bytes_accessed=0, transcendentals=0),
        )(self.ticket, *[pltpu.with_memory_space_constraint(a, pltpu.HBM if i < anywhere else pltpu.VMEM) for i, a in enumerate(operands)])
        return results[0] if len(results) == 1 else results


def load_kernel(count, pieces, _, *refs):
    sems = refs[-1]
    copies = []
    for i in range(count):
        rows = refs[i].shape[0] // pieces
        for j in range(pieces):
            at = pl.ds(j * rows, rows)
            copies.append(pltpu.make_async_copy(refs[i].at[at], refs[count + i].at[at], sems.at[i, j]))
            copies[-1].start()
    for c in copies:
        c.wait()


def load(queue, *arrays, pieces=4):
    n = len(arrays)
    return queue.run(
        functools.partial(load_kernel, n, pieces), arrays, [array(*a.shape) for a in arrays],
        [pltpu.SemaphoreType.DMA((n, pieces))], anywhere=n,
    )


def selection(table, ids_ref, near):
    rows = table.shape[0]
    lane = lax.broadcasted_iota(jnp.int32, (8, LANES), 1)
    pick = jnp.where((lane == ids_ref[2]) | (lane == ids_ref[3]), 1.0, 0.0)
    named = jnp.where(table > 0.0, 1.0, 0.0)
    need = jnp.minimum(lax.dot_general(pick, named, NT, preferred_element_type=F32), 1.0)
    before = lax.broadcasted_iota(jnp.int32, (rows, rows), 0) < lax.broadcasted_iota(jnp.int32, (rows, rows), 1)
    place = jnp.dot(need, jnp.where(before, 1.0, 0.0), preferred_element_type=F32)
    slot = lax.broadcasted_iota(jnp.int32, (near, rows), 0)
    return jnp.where((place[:1].astype(jnp.int32) == slot) & (need[:1] > 0.0), 1.0, 0.0).astype(BF16)


def choose_kernel(near, ids_ref, x_ref, out_ref, sel_ref, *same_ref):
    for ref in same_ref:
        ref[...] = x_ref[...]
    sel_ref[...] = selection(x_ref[:, x_ref.shape[1] - LANES :].astype(F32), ids_ref, near)
    out_ref[...] = jnp.dot(sel_ref[...], x_ref[...], preferred_element_type=F32).astype(BF16)


def choose(queue, x, near, again):
    rows, width = x.shape
    outs = [array(near, width), array(near, rows)] + [array(rows, width)] * again
    return queue.run(functools.partial(choose_kernel, near), [x], outs)


def prepare_kernel(near, ids_ref, tokens_ref, named_hbm, weight_hbm, x_ref, out_ref, sel_ref, named_ref, weight_ref, sems):
    rows, features = tokens_ref.shape
    copies = [
        pltpu.make_async_copy(named_hbm, named_ref, sems.at[0]),
        pltpu.make_async_copy(weight_hbm, weight_ref, sems.at[1]),
        pltpu.make_async_copy(tokens_ref, x_ref.at[:, pl.ds(0, features)], sems.at[2]),
    ]
    for c in copies:
        c.start()
    for c in copies[:2]:
        c.wait()
    expert = lax.broadcasted_iota(jnp.int32, (LANES, rows), 0)
    table = jnp.zeros((LANES, rows), F32)
    for k in range(named_ref.shape[0]):
        weight = weight_ref[k : k + 1, :].astype(F32)
        table += jnp.where(expert == named_ref[k : k + 1, :], weight, 0.0)
    row = lax.broadcasted_iota(jnp.int32, (LANES, rows), 1).astype(F32)
    table = jnp.where(expert == LANES - 1, row, table).T
    x_ref[:, features:] = table.astype(BF16)
    sel_ref[...] = selection(table, ids_ref, near)
    copies[2].wait()
    out_ref[...] = jnp.dot(sel_ref[...], x_ref[...], preferred_element_type=F32).astype(BF16)


def prepare(queue, tokens, ids, weights, near):
    rows, features = tokens.shape
    width = features + LANES
    return queue.run(
        functools.partial(prepare_kernel, near),
        [tokens, ids, weights],
        [array(rows, width), array(near, width), array(near, rows)],
        [pltpu.VMEM(ids.shape, jnp.int32), pltpu.VMEM(weights.shape, BF16), pltpu.SemaphoreType.DMA((3,))],
        anywhere=3,
    )


def pack_kernel(_, sel_ref, g_ref, out_ref, *same_ref):
    for ref in same_ref:
        ref[...] = g_ref[...]
    out_ref[...] = jnp.dot(sel_ref[...], g_ref[...], preferred_element_type=F32).astype(BF16)


def pack(queue, sel, g, again):
    outs = [array(sel.shape[0], g.shape[1])] + [array(*g.shape)] * again
    return queue.run(pack_kernel, [sel, g], outs)


def spread(sel_ref, back_ref):
    return lax.dot_general(
        sel_ref[...], back_ref[...], (((0,), (0,)), ((), ())), preferred_element_type=F32
    )


def place_kernel(cuts, _, far_ref, tok_ref, *refs):
    near, width = far_ref.shape
    rows = refs[-1].shape[0]
    row = tok_ref[:, width - 1 :].astype(F32).astype(jnp.int32)
    sel = jnp.where(lax.broadcasted_iota(jnp.int32, (near, rows), 1) == row, 1.0, 0.0).astype(BF16)
    total = lax.dot_general(sel, far_ref[...], (((0,), (0,)), ((), ())), preferred_element_type=F32)
    for ref in refs[: -len(cuts)]:
        total += ref[...].astype(F32)
    for (at, end), ref in zip(cuts, refs[-len(cuts) :]):
        ref[...] = total[:, at:end].astype(BF16)


def place(queue, far, tok, rows, *carried, cuts=None):
    cuts = cuts or [(0, far.shape[1])]
    outs = [array(rows, end - at) for at, end in cuts]
    return queue.run(functools.partial(place_kernel, cuts), [far, tok, *carried], outs)


def gather_kernel(cut, _, own_ref, back_ref, sel_ref, *refs):
    at, end = cut
    total = own_ref[:, at:end].astype(F32) + spread(sel_ref, back_ref)
    for ref in refs[:-1]:
        total += (ref[...] if ref.shape == total.shape else ref[:, at:end]).astype(F32)
    refs[-1][...] = total.astype(BF16)


def gather(queue, own, back, sel, cut, *carried, flops=0):
    return queue.run(
        functools.partial(gather_kernel, cut), [own, back, sel, *carried],
        [array(own.shape[0], cut[1] - cut[0])], flops=flops,
    )


def add_kernel(cut, kept, _, *refs):
    for ref, same_ref in zip(refs[:kept], refs[len(refs) - kept :]):
        same_ref[...] = ref[...]
    *block_refs, out_ref = refs[kept : len(refs) - kept]
    width = out_ref.shape[1]
    blocks = [ref[...] if ref.shape[1] == width else ref[:, cut[0] : cut[1]] for ref in block_refs]
    out_ref[...] = sum(block.astype(F32) for block in blocks).astype(BF16)


def add(queue, cut, *blocks, kept=()):
    outs = [array(blocks[0].shape[0], cut[1] - cut[0])] + [array(*a.shape) for a in kept]
    return queue.run(functools.partial(add_kernel, cut, len(kept)), [*kept, *blocks], outs)


def total(own_ref, back_ref, sel_ref, carried_ref, at):
    end = at + carried_ref.shape[1]
    return own_ref[:, at:end].astype(F32) + spread(sel_ref, back_ref.at[:, pl.ds(at, end - at)]) + carried_ref[...].astype(F32)


def front_kernel(_, own_ref, back_ref, sel_ref, carried_ref, out_ref):
    out_ref[...] = total(own_ref, back_ref, sel_ref, carried_ref, 0).astype(BF16)


def finish_kernel(_, own_ref, back_ref, sel_ref, carried_ref, front_ref, ids_ref, out_ref, gates_ref):
    features = out_ref.shape[1]
    at = front_ref.shape[1]
    out_ref[:, :at] = front_ref[...]
    rest = total(own_ref, back_ref, sel_ref, carried_ref, at)
    out_ref[:, at:] = rest[:, : features - at].astype(BF16)
    gates = rest[:, features - at :].T
    expert = lax.broadcasted_iota(jnp.int32, gates.shape, 0)
    for k in range(ids_ref.shape[0]):
        gates_ref[k : k + 1, :] = jnp.sum(jnp.where(expert == ids_ref[k : k + 1, :], gates, 0.0), axis=0, keepdims=True)


def finish(queue, own, back, sel, ids, first, second):
    rows, width = own.shape
    front = queue.run(front_kernel, [own, back, sel, first], [array(*first.shape)], flops=HOLD[2])
    return queue.run(
        finish_kernel, [own, back, sel, second, front, ids],
        [array(rows, width - LANES), array(*ids.shape, dtype=F32)],
    )


def project_kernel(tile, _, own_ref, far_ref, w0_ref, w1_ref, *refs):
    kept = (len(refs) - 3) // 2
    out0_ref, out1_ref = refs[kept : kept + 2]
    both = refs[-1]
    for ref, same_ref in zip(refs[:kept], refs[kept + 2 : -1]):
        same_ref[...] = ref[...]
    features, width = w0_ref.shape
    rows = own_ref.shape[0]
    both[:rows, :] = own_ref[:, :features]
    both[rows:, :] = far_ref[:, :features]
    for w_ref, out_ref in ((w0_ref, out0_ref), (w1_ref, out1_ref)):
        for j in range(width // tile):
            at = pl.ds(j * tile, tile)
            out_ref[:, at] = jnp.dot(both[...], w_ref[:, at], preferred_element_type=F32)


def project(queue, own, far, w0, w1, *kept, tile=512):
    rows = own.shape[0] + far.shape[0]
    features, width = w0.shape
    return queue.run(
        functools.partial(project_kernel, tile),
        [own, far, w0, w1, *kept],
        [array(rows, width, dtype=F32)] * 2 + [array(*a.shape) for a in kept],
        [pltpu.VMEM((rows, features), BF16)],
        flops=4 * rows * features * width,
    )


def backward_kernel(
    tile, split, ids_ref, p0_ref, p1_ref, own_ref, far_ref, tok_own, tok_far, d0_ref, d1_ref, w0_ref, w1_ref,
    out_own, *refs,
):
    hidden, features = d0_ref.shape
    parts, splits = hidden // tile, features // split
    rows = own_ref.shape[0]
    *out_fars, both, meta, grads = refs
    starts = [sum(ref.shape[1] for ref in out_fars[:i]) for i in range(len(out_fars))]
    both[:rows, :] = own_ref[...]
    both[rows:, :] = far_ref[...]
    meta[:rows, :] = tok_own[:, features:].astype(F32)
    meta[rows:, :] = tok_far[:, features:].astype(F32)
    lane = lax.broadcasted_iota(jnp.int32, meta.shape, 1)
    gates = jnp.zeros(meta.shape, F32)
    for e, (p_ref, d_ref) in enumerate(((p0_ref, d0_ref), (p1_ref, d1_ref))):
        here = lane == ids_ref[e]
        scale = jnp.sum(jnp.where(here, meta[...], 0.0), axis=1, keepdims=True)
        total = jnp.zeros((meta.shape[0], 1), F32)
        for j in range(parts):
            at = pl.ds(j * tile, tile)
            hidden_grad = lax.dot_general(both[...], d_ref[at], NT, preferred_element_type=F32)
            gate_pre = p_ref[:, at]
            up_pre = p_ref[:, pl.ds(hidden + j * tile, tile)]
            sigmoid = 1.0 / (1.0 + jnp.exp(-gate_pre))
            active = gate_pre * sigmoid
            total += jnp.sum(hidden_grad * active * up_pre, axis=1, keepdims=True)
            scaled = scale * hidden_grad
            base = 2 * e * hidden + j * tile
            grads[:, pl.ds(base, tile)] = (
                scaled * up_pre * sigmoid * (1.0 + gate_pre * (1.0 - sigmoid))
            ).astype(BF16)
            grads[:, pl.ds(base + hidden, tile)] = (scaled * active).astype(BF16)
        gates += jnp.where(here, total, 0.0)
    out_own[:, features:] = gates[:rows].astype(BF16)
    out_fars[-1][:, features - starts[-1] :] = gates[rows:].astype(BF16)
    for j in range(splits):
        at = pl.ds(j * split, split)
        out = lax.dot_general(grads[:, : 2 * hidden], w0_ref[at], NT, preferred_element_type=F32)
        out += lax.dot_general(grads[:, 2 * hidden :], w1_ref[at], NT, preferred_element_type=F32)
        out_own[:, at] = out[:rows].astype(BF16)
        i = sum(start <= j * split for start in starts) - 1
        out_fars[i][:, pl.ds(j * split - starts[i], split)] = out[rows:].astype(BF16)


def backward(queue, p0, p1, own, far, tok_own, tok_far, d0, d1, w0, w1, cuts, tile=256, split=512):
    rows = own.shape[0] + far.shape[0]
    hidden, features = d0.shape
    return queue.run(
        functools.partial(backward_kernel, tile, split),
        [p0, p1, own, far, tok_own, tok_far, d0, d1, w0, w1],
        [array(own.shape[0], features + LANES)] + [array(far.shape[0], end - at) for at, end in cuts],
        [pltpu.VMEM((rows, features), BF16), pltpu.VMEM((rows, LANES), F32), pltpu.VMEM((rows, 4 * hidden), BF16)],
        flops=12 * rows * features * hidden,
    )


def shards(lines, tokens, cotangent, expert_ids, gate_weights, w_gate_up, w_down):
    devices = lax.axis_size("expert")
    depth = devices // (2 * lines)
    rows, features = tokens.shape
    fanout = expert_ids.shape[1]
    capacity = 7 * rows * fanout // (4 * devices)
    near = min(rows, -(-2 * capacity // 16) * 16)
    index = lambda z, y, c: (z * lines + y) * 2 + c
    places = [(z, y, c) for z in range(depth) for y in range(lines) for c in range(2)]
    up = [(index(z, y, c), index((z + 1) % depth, y, c)) for z, y, c in places]
    across = [(index(z, y, c), index(z, 1 - y, c)) for z, y, c in places]
    twin = [(index(z, y, c), index(z, y, 1 - c)) for z, y, c in places]
    move = lambda a, pairs: lax.ppermute(a, "expert", pairs)

    me = lax.axis_index("expert")
    queue = Queue(jnp.stack([me, me ^ 1, me ^ 2, me ^ 3]).astype(jnp.int32))
    ids, weights = expert_ids.T, gate_weights.T
    w0, d0 = w_gate_up[0], w_down[0]
    w1, d1 = move(w0, twin), move(d0, twin)
    last = depth - 1
    xs, gs, sels, xf, gf = [], [], [], [], []
    own, far, back = [], [], []
    early = 1 if depth == 4 else depth
    whole = [(0, features + LANES)]
    halves = [(0, features // 2), (features // 2, features + LANES)]
    nx = ng = None

    def take_tokens(s):
        nonlocal nx
        if s:
            x, again = nx, s < last
            packed, sel, *kept = choose(queue, x, near, again)
        else:
            x, packed, sel = prepare(queue, tokens, ids, weights, near)
            again = False
        x = kept[0] if again else x
        if s < last:
            nx = move(x, up)
        xf.append(move(packed, across))
        sels.append(sel)
        xs.append(x)

    def take_grads(s):
        nonlocal ng
        g, again = ng if s else cotangent, 0 < s < last
        packed = pack(queue, sels[s], g, again)
        if again:
            packed, g = packed
        if s < last:
            ng = move(g, up)
        gf.append(move(packed, across))
        gs.append(g)

    take_tokens(0)
    take_grads(0)
    w0, d0 = load(queue, w0, d0)
    w1, d1 = load(queue, w1, d1)
    take_tokens(1)
    for s in range(depth):
        if s == 1:
            take_tokens(2)
        kept = own[early : early + 1] if s == early + 2 else []
        p0, p1, *kept = project(queue, xs[s], xf[s], w0, w1, *kept)
        own[early : early + len(kept)] = kept
        if 1 < s < last:
            take_tokens(s + 1)
        if s == early + 1:
            lifted = move(place(queue, far[early], xf[early], rows), up)
        if s == early + 2:
            lifted = place(queue, far[s - 1], xf[s - 1], rows, lifted, cuts=halves)
            back[s - 1] = [move(a, across) for a in lifted]
        if s < 2:
            take_grads(s + 1)
        cuts = halves if s == last else whole
        mine, *other = backward(queue, p0, p1, gs[s], gf[s], xs[s], xf[s], d0, d1, w0, w1, cuts)
        if 1 < s < last:
            take_grads(s + 1)
        own.append(mine)
        far.append(other[0])
        back.append(None if s in (0, early, early + 1) else [move(a, across) for a in other])
    carried = [move(own[1] if early == 1 else gather(queue, own[1], back[1][0], sels[1], *whole), up)]
    for s in range(2, depth):
        if s == early + 1:
            first = add(queue, halves[0], own[s], back[s][0], *carried)
            second, later = add(queue, halves[1], own[s], back[s][1], *carried, kept=[far[0]])
            back[0] = move(later, across)
            carried = [first, second]
        elif s < last:
            carried = [gather(queue, own[s], back[s][0], sels[s], whole[0], *carried)]
        else:
            if len(carried) == 1:
                carried, back[0] = carried * 2, move(far[0], across)
            carried = [
                gather(queue, own[s], part, sels[s], cut, before, flops=cost)
                for cut, part, before, cost in zip(halves, back[s], carried, HOLD)
            ]
        carried = [move(a, up) for a in carried]
    grad_tokens, grad_gates = finish(queue, own[0], back[0], sels[0], ids, *carried)
    return grad_tokens, grad_gates.T.astype(BF16)


def solution(mesh):
    row, cube = P(("parts", "expert"), None), P(("parts", "expert"), None, None)
    body = functools.partial(shards, 2)
    return jax.shard_map(
        body, mesh=mesh, in_specs=(row, row, row, row, cube, cube), out_specs=(row, row), check_vma=False
    )
```

time: 150 us -> 135 us (0.900)
  waiting for transfers between devices: 58.9 us -> 29.8 us
  Pallas kernels: 55.5 us -> 73.7 us
  local copies, waits for them, and re-layouts: 5.44 us -> 1.09 us
  starting transfers between devices: 26.6 us -> 28.9 us
    ppermute x23 -> x27, waiting for transfers between devices: 58.9 us -> 29.8 us  [shards(): move = lambda a, pairs: lax.ppermute(a, 'expert', pairs)]
    pallas_call x22 -> x26, Pallas kernels: 55.5 us -> 73.7 us  [run(): pl.pallas_call(body, in_specs=[SCALAR] + [ANYWHERE] * anywhere + [LOCAL]...]
    unnamed x9 -> x8, local copies, waits for them, and re-layouts: 4.79 us -> 1.09 us
    ppermute x23 -> x27, starting transfers between devices: 26.6 us -> 28.9 us  [shards(): move = lambda a, pairs: lax.ppermute(a, 'expert', pairs)]
  transfers between devices with their start and end apart: 23 -> 27, of which waited for: 11 -> 14; matrix products, arithmetic and copies ran while one was open for 1% -> 0% of each run, Pallas kernels for 36% -> 53%
where the time goes in v3:
time: 135 us
  Pallas kernels  73.7 us (55%)
  waiting for transfers between devices  29.8 us (22%)
  starting transfers between devices  28.9 us (21%)
    pallas_call x26, Pallas kernels, run(): pl.pallas_call(body, in_specs=[SCALAR] + [ANYWHERE] * anywhere + [LOCAL]...  73.7 us
    ppermute x27, waiting for transfers between devices, shards(): move = lambda a, pairs: lax.ppermute(a, 'expert', pairs)  29.8 us
    ppermute x27, starting transfers between devices, shards(): move = lambda a, pairs: lax.ppermute(a, 'expert', pairs)  28.9 us
  transfers between devices with their start and end apart: 27, of which 14 were waited for; matrix products, arithmetic and copies ran while one was open for 0% of the time, Pallas kernels for 53%

profile of v3, /device:TPU:0, one launch (start us, length us, event | category | flops | bytes accessed | tf_op | source)
XLA Modules:
  0.0 135.2 jit_solution(16816676926725206282)
XLA Ops:
  1.3 2.2 %shard_map.77 = (bf16[128,2176]{1,0:T(8,128)(2,1)S(1)}, bf16[112,2176]{1,0:T(8,128)(2,1)S(1)}, bf16[112,128]{1,0:T(8,128)(2,1)S(1)}, s32[4]{0:T(128)S(1)}) custom-call(s32[4]{0:T(128)S(1)} %pad_add_fusion.ticket_ref, bf16[128,2048]{1,0:T(8,128)(2,1)} %refs_0_.1, s32[4,128]{1,0:T(4,128)} %bitcast.10, bf16[4,128]{1,0:T(4,128)(2,1)} %bitcast.16), custom_call_target="tpu_custom_call" | custom-call | tf_op jit(solution)/shard_map/pallas_call | solution.py:36
  3.6 3.1 %collective-permute-start.2 = (bf16[128,2176]{1,0:T(8,128)(2,1)S(1)}, bf16[128,2176]{1,0:T(8,128)(2,1)S(1)}, u32[]{:S(2)}, u32[]{:S(2)}) collective-permute-start(bf16[128,2176]{1,0:T(8,128)(2,1)S(1)} %get-tuple-element.82.refs_0_.refs_4_), channel_id=1, source_target_pairs={{0,4},{1,5},{2,6},{3,7},{4,8},{5,9},{6,10},{7,11},{8,12},{9,13},{1... | collective-permute-start | bytes 1671176 | tf_op jit(solution)/shard_map/ppermute | solution.py:321
  6.6 1.5 %collective-permute-start.3 = (bf16[112,2176]{1,0:T(8,128)(2,1)S(1)}, bf16[112,2176]{1,0:T(8,128)(2,1)S(1)}, u32[]{:S(2)}, u32[]{:S(2)}) collective-permute-start(bf16[112,2176]{1,0:T(8,128)(2,1)S(1)} %get-tuple-element.84), channel_id=1, source_target_pairs={{0,2},{1,3},{2,0},{3,1},{4,6},{5,7},{6,4},{7,5},{8,10},{9,11},{10,... | collective-permute-start | bytes 1462280 | tf_op jit(solution)/shard_map/ppermute | solution.py:321
  8.1 1.6 %collective-permute-start.4 = (bf16[128,2048]{1,0:T(8,128)(2,1)}, bf16[128,2048]{1,0:T(8,128)(2,1)S(1)}, u32[]{:S(2)}, u32[]{:S(2)}) collective-permute-start(bf16[128,2048]{1,0:T(8,128)(2,1)} %refs_2_.1), channel_id=1, source_target_pairs={{0,4},{1,5},{2,6},{3,7},{4,8},{5,9},{6,10},{7,11},{8,12},{9,13},{1... | collective-permute-start | bytes 1572872 | tf_op jit(solution)/shard_map/ppermute | solution.py:321
  11.9 3.6 %collective-permute-done.1.refs_1_ = bf16[768,2048]{1,0:T(8,128)(2,1)S(1)} collective-permute-done((bf16[768,2048]{1,0:T(8,128)(2,1)}, bf16[768,2048]{1,0:T(8,128)(2,1)S(1)}, u32[]{:S(2)}, u32[]{:S(2)}) %collective-permute-start.1) | collective-permute-done | bytes 3145760 | tf_op jit(solution)/shard_map/ppermute | solution.py:321
  15.6 2.6 %collective-permute-start.5 = (bf16[112,2048]{1,0:T(8,128)(2,1)S(1)}, bf16[112,2048]{1,0:T(8,128)(2,1)S(1)}, u32[]{:S(2)}, u32[]{:S(2)}) collective-permute-start(bf16[112,2048]{1,0:T(8,128)(2,1)S(1)} %get-tuple-element.92), channel_id=1, source_target_pairs={{0,2},{1,3},{2,0},{3,1},{4,6},{5,7},{6,4},{7,5},{8,10},{9,11},{10,... | collective-permute-start | bytes 1376264 | tf_op jit(solution)/shard_map/ppermute | solution.py:321
  18.2 4.9 %shard_map.79 = (bf16[2048,1536]{1,0:T(8,128)(2,1)S(1)}, bf16[768,2048]{1,0:T(8,128)(2,1)S(1)}, s32[4]{0:T(128)S(1)}) custom-call(s32[4]{0:T(128)S(1)} %get-tuple-element.79.ticket_ref, bf16[2048,1536]{1,0:T(8,128)(2,1)} %bitcast.13, bf16[768,2048]{1,0:T(8,128)(2,1)} %bitcast.15), custom_call_target="tpu_custom_call" | custom-call | tf_op jit(solution)/shard_map/pallas_call | solution.py:36
  23.1 4.9 %shard_map.80 = (bf16[2048,1536]{1,0:T(8,128)(2,1)S(1)}, bf16[768,2048]{1,0:T(8,128)(2,1)S(1)}, s32[4]{0:T(128)S(1)}) custom-call(s32[4]{0:T(128)S(1)} %get-tuple-element.80.ticket_ref, bf16[2048,1536]{1,0:T(8,128)(2,1)} %collective-permute-done.refs_0_, bf16[768,2048]{1,0:T(8,128)(2,1)} %copy-done.3), custom_call_target="tpu_custom_call" | custom-call | tf_op jit(solution)/shard_map/pallas_call | solution.py:36
  29.4 1.6 %collective-permute-start.6 = (bf16[128,2176]{1,0:T(8,128)(2,1)S(1)}, bf16[128,2176]{1,0:T(8,128)(2,1)S(1)}, u32[]{:S(2)}, u32[]{:S(2)}) collective-permute-start(bf16[128,2176]{1,0:T(8,128)(2,1)S(1)} %get-tuple-element.96.refs_0_.refs_4_), channel_id=1, source_target_pairs={{0,4},{1,5},{2,6},{3,7},{4,8},{5,9},{6,10},{7,11},{8,12},{9,13},{1... | collective-permute-start | bytes 1671176 | tf_op jit(solution)/shard_map/ppermute | solution.py:321
  31.6 4.1 %shard_map.82 = (f32[240,1536]{1,0:T(8,128)S(1)}, f32[240,1536]{1,0:T(8,128)S(1)}, s32[4]{0:T(128)S(1)}) custom-call(s32[4]{0:T(128)S(1)} %get-tuple-element.83.ticket_ref, bf16[128,2176]{1,0:T(8,128)(2,1)S(1)} %get-tuple-element.82.refs_0_.refs_4_, bf16[112,2176]{1,0:T(8,128)(2,1)S(1)} %collective-permute-done.3.refs_1_.refs_5_, ...), custom_call_target="tpu_custom_call" | custom-call | flops 905969664 | tf_op jit(solution)/shard_map/pallas_call | solution.py:36
  36.9 1.6 %collective-permute-start.8 = (bf16[128,2048]{1,0:T(8,128)(2,1)S(1)}, bf16[128,2048]{1,0:T(8,128)(2,1)S(1)}, u32[]{:S(2)}, u32[]{:S(2)}) collective-permute-start(bf16[128,2048]{1,0:T(8,128)(2,1)S(1)} %get-tuple-element.101.refs_2_), channel_id=1, source_target_pairs={{0,4},{1,5},{2,6},{3,7},{4,8},{5,9},{6,10},{7,11},{8,12},{9,13},{1... | collective-permute-start | bytes 1572872 | tf_op jit(solution)/shard_map/ppermute | solution.py:321
  38.5 1.5 %collective-permute-start.9 = (bf16[112,2048]{1,0:T(8,128)(2,1)S(1)}, bf16[112,2048]{1,0:T(8,128)(2,1)S(1)}, u32[]{:S(2)}, u32[]{:S(2)}) collective-permute-start(bf16[112,2048]{1,0:T(8,128)(2,1)S(1)} %get-tuple-element.105), channel_id=1, source_target_pairs={{0,2},{1,3},{2,0},{3,1},{4,6},{5,7},{6,4},{7,5},{8,10},{9,11},{10,... | collective-permute-start | bytes 1376264 | tf_op jit(solution)/shard_map/ppermute | solution.py:321
  40.0 6.7 %shard_map.84 = (bf16[128,2176]{1,0:T(8,128)(2,1)S(1)}, bf16[112,2176]{1,0:T(8,128)(2,1)S(1)}, s32[4]{0:T(128)S(1)}) custom-call(s32[4]{0:T(128)S(1)} %get-tuple-element.89.ticket_ref, f32[240,1536]{1,0:T(8,128)S(1)} %get-tuple-element.90.refs_0_, f32[240,1536]{1,0:T(8,128)S(1)} %get-tuple-element.91.refs_1_, bf16[128,2048]{1,0:T(8,128)(2,1)S(1)} %copy-done.1, ...), custom_call_target="tpu_custom_call" | custom-call | flops 1358954496 | tf_op jit(solution)/shard_map/pallas_call | solution.py:36
  50.3 4.1 %shard_map.86 = (f32[240,1536]{1,0:T(8,128)S(1)}, f32[240,1536]{1,0:T(8,128)S(1)}, s32[4]{0:T(128)S(1)}) custom-call(s32[4]{0:T(128)S(1)} %get-tuple-element.97.ticket_ref, bf16[128,2176]{1,0:T(8,128)(2,1)S(1)} %get-tuple-element.96.refs_0_.refs_4_, bf16[112,2176]{1,0:T(8,128)(2,1)S(1)} %collective-permute-done.7.refs_1_.refs_5_, ...), custom_call_target="tpu_custom_call" | custom-call | flops 905969664 | tf_op jit(solution)/shard_map/pallas_call | solution.py:36
  54.5 3.5 %collective-permute-done.8.refs_1_ = bf16[128,2048]{1,0:T(8,128)(2,1)S(1)} collective-permute-done((bf16[128,2048]{1,0:T(8,128)(2,1)S(1)}, bf16[128,2048]{1,0:T(8,128)(2,1)S(1)}, u32[]{:S(2)}, u32[]{:S(2)}) %collective-permute-start.8) | collective-permute-done | bytes 524320 | tf_op jit(solution)/shard_map/ppermute | solution.py:321
  59.7 6.6 %shard_map.88 = (bf16[128,2176]{1,0:T(8,128)(2,1)S(1)}, bf16[112,2176]{1,0:T(8,128)(2,1)S(1)}, s32[4]{0:T(128)S(1)}) custom-call(s32[4]{0:T(128)S(1)} %get-tuple-element.102.ticket_ref, f32[240,1536]{1,0:T(8,128)S(1)} %get-tuple-element.103.refs_0_, f32[240,1536]{1,0:T(8,128)S(1)} %get-tuple-element.104.refs_1_, ...), custom_call_target="tpu_custom_call" | custom-call | flops 1358954496 | tf_op jit(solution)/shard_map/pallas_call | solution.py:36
  66.4 4.1 %shard_map.89 = (f32[240,1536]{1,0:T(8,128)S(1)}, f32[240,1536]{1,0:T(8,128)S(1)}, s32[4]{0:T(128)S(1)}) custom-call(s32[4]{0:T(128)S(1)} %get-tuple-element.106.ticket_ref, bf16[128,2176]{1,0:T(8,128)(2,1)S(1)} %get-tuple-element.107.refs_0_.refs_4_, bf16[112,2176]{1,0:T(8,128)(2,1)S(1)} %collective-permute-done.10.refs_1_.refs_5_, ...), custom_call_target="tpu_custom_call" | custom-call | flops 905969664 | tf_op jit(solution)/shard_map/pallas_call | solution.py:36
  72.0 1.6 %collective-permute-start.14 = (bf16[112,2176]{1,0:T(8,128)(2,1)S(1)}, bf16[112,2176]{1,0:T(8,128)(2,1)S(1)}, u32[]{:S(2)}, u32[]{:S(2)}) collective-permute-start(bf16[112,2176]{1,0:T(8,128)(2,1)S(1)} %get-tuple-element.120), channel_id=1, source_target_pairs={{0,2},{1,3},{2,0},{3,1},{4,6},{5,7},{6,4},{7,5},{8,10},{9,11},{10,... | collective-permute-start | bytes 1462280 | tf_op jit(solution)/shard_map/ppermute | solution.py:321
  74.7 1.6 %collective-permute-start.15 = (bf16[128,2176]{1,0:T(8,128)(2,1)S(1)}, bf16[128,2176]{1,0:T(8,128)(2,1)S(1)}, u32[]{:S(2)}, u32[]{:S(2)}) collective-permute-start(bf16[128,2176]{1,0:T(8,128)(2,1)S(1)} %get-tuple-element.124), channel_id=1, source_target_pairs={{0,4},{1,5},{2,6},{3,7},{4,8},{5,9},{6,10},{7,11},{8,12},{9,13},{1... | collective-permute-start | bytes 1671176 | tf_op jit(solution)/shard_map/ppermute | solution.py:321
  76.3 6.5 %shard_map.92 = (bf16[128,2176]{1,0:T(8,128)(2,1)S(1)}, bf16[112,2176]{1,0:T(8,128)(2,1)S(1)}, s32[4]{0:T(128)S(1)}) custom-call(s32[4]{0:T(128)S(1)} %get-tuple-element.112.ticket_ref, f32[240,1536]{1,0:T(8,128)S(1)} %get-tuple-element.113.refs_0_, f32[240,1536]{1,0:T(8,128)S(1)} %get-tuple-element.114.refs_1_, ...), custom_call_target="tpu_custom_call" | custom-call | flops 1358954496 | tf_op jit(solution)/shard_map/pallas_call | solution.py:36
  84.9 4.2 %shard_map.94 = (f32[240,1536]{1,0:T(8,128)S(1)}, f32[240,1536]{1,0:T(8,128)S(1)}, bf16[128,2176]{1,0:T(8,128)(2,1)S(1)}, s32[4]{0:T(128)S(1)}) custom-call(s32[4]{0:T(128)S(1)} %get-tuple-element.119.ticket_ref, bf16[128,2176]{1,0:T(8,128)(2,1)S(1)} %collective-permute-done.11.refs_0_.refs_4_, ...), custom_call_target="tpu_custom_call" | custom-call | flops 905969664 | tf_op jit(solution)/shard_map/pallas_call | solution.py:36
  89.1 1.6 %collective-permute-start.18 = (bf16[128,2176]{1,0:T(8,128)(2,1)S(1)}, bf16[128,2176]{1,0:T(8,128)(2,1)S(1)}, u32[]{:S(2)}, u32[]{:S(2)}) collective-permute-start(bf16[128,2176]{1,0:T(8,128)(2,1)S(1)} %get-tuple-element.132), channel_id=1, source_target_pairs={{0,4},{1,5},{2,6},{3,7},{4,8},{5,9},{6,10},{7,11},{8,12},{9,13},{1... | collective-permute-start | bytes 1671176 | tf_op jit(solution)/shard_map/ppermute | solution.py:321
  90.8 2.2 %collective-permute-done.15.refs_2_ = bf16[128,2176]{1,0:T(8,128)(2,1)S(1)} collective-permute-done((bf16[128,2176]{1,0:T(8,128)(2,1)S(1)}, bf16[128,2176]{1,0:T(8,128)(2,1)S(1)}, u32[]{:S(2)}, u32[]{:S(2)}) %collective-permute-start.15) | collective-permute-done | bytes 557088 | tf_op jit(solution)/shard_map/ppermute | solution.py:321
  96.4 6.6 %shard_map.96 = (bf16[128,2176]{1,0:T(8,128)(2,1)S(1)}, bf16[112,1024]{1,0:T(8,128)(2,1)S(1)}, bf16[112,1152]{1,0:T(8,128)(2,1)S(1)}, s32[4]{0:T(128)S(1)}) custom-call(s32[4]{0:T(128)S(1)} %get-tuple-element.125.ticket_ref, f32[240,1536]{1,0:T(8,128)S(1)} %get-tuple-element.126.refs_0_, f32[240,1536]{1,0:T(8,128)S(1)} %get-tuple-element.127.refs_1_, ...), custom_call_target="tpu_custom_call" | custom-call | flops 1358954496 | tf_op jit(solution)/shard_map/pallas_call | solution.py:36
  107.6 1.6 %collective-permute-done.19.refs_2_ = bf16[128,1152]{1,0:T(8,128)(2,1)S(1)} collective-permute-done((bf16[128,1152]{1,0:T(8,128)(2,1)S(1)}, bf16[128,1152]{1,0:T(8,128)(2,1)S(1)}, u32[]{:S(2)}, u32[]{:S(2)}) %collective-permute-start.19) | collective-permute-done | bytes 294944 | tf_op jit(solution)/shard_map/ppermute | solution.py:321
  110.3 1.5 %collective-permute-start.24 = (bf16[112,2176]{1,0:T(8,128)(2,1)S(1)}, bf16[112,2176]{1,0:T(8,128)(2,1)S(1)}, u32[]{:S(2)}, u32[]{:S(2)}) collective-permute-start(bf16[112,2176]{1,0:T(8,128)(2,1)S(1)} %get-tuple-element.145), channel_id=1, source_target_pairs={{0,2},{1,3},{2,0},{3,1},{4,6},{5,7},{6,4},{7,5},{8,10},{9,11},{10,... | collective-permute-start | bytes 1462280 | tf_op jit(solution)/shard_map/ppermute | solution.py:321
  111.9 2.2 %collective-permute-done.20.refs_1_ = bf16[112,1024]{1,0:T(8,128)(2,1)S(1)} collective-permute-done((bf16[112,1024]{1,0:T(8,128)(2,1)S(1)}, bf16[112,1024]{1,0:T(8,128)(2,1)S(1)}, u32[]{:S(2)}, u32[]{:S(2)}) %collective-permute-start.20) | collective-permute-done | bytes 229408 | tf_op jit(solution)/shard_map/ppermute | solution.py:321
  116.5 3.1 %collective-permute-done.22.refs_1_ = bf16[112,1152]{1,0:T(8,128)(2,1)S(1)} collective-permute-done((bf16[112,1152]{1,0:T(8,128)(2,1)S(1)}, bf16[112,1152]{1,0:T(8,128)(2,1)S(1)}, u32[]{:S(2)}, u32[]{:S(2)}) %collective-permute-start.22) | collective-permute-done | bytes 258080 | tf_op jit(solution)/shard_map/ppermute | solution.py:321
  119.6 3.7 %collective-permute-done.23.refs_3_ = bf16[128,1152]{1,0:T(8,128)(2,1)S(1)} collective-permute-done((bf16[128,1152]{1,0:T(8,128)(2,1)S(1)}, bf16[128,1152]{1,0:T(8,128)(2,1)S(1)}, u32[]{:S(2)}, u32[]{:S(2)}) %collective-permute-start.23) | collective-permute-done | bytes 294944 | tf_op jit(solution)/shard_map/ppermute | solution.py:321
  124.5 4.0 %collective-permute-done.24.refs_1_ = bf16[112,2176]{1,0:T(8,128)(2,1)S(1)} collective-permute-done((bf16[112,2176]{1,0:T(8,128)(2,1)S(1)}, bf16[112,2176]{1,0:T(8,128)(2,1)S(1)}, u32[]{:S(2)}, u32[]{:S(2)}) %collective-permute-start.24) | collective-permute-done | bytes 487456 | tf_op jit(solution)/shard_map/ppermute | solution.py:321
  129.9 3.1 %collective-permute-done.26.refs_3_ = bf16[128,1152]{1,0:T(8,128)(2,1)S(1)} collective-permute-done((bf16[128,1152]{1,0:T(8,128)(2,1)S(1)}, bf16[128,1152]{1,0:T(8,128)(2,1)S(1)}, u32[]{:S(2)}, u32[]{:S(2)}) %collective-permute-start.26) | collective-permute-done | bytes 294944 | tf_op jit(solution)/shard_map/ppermute | solution.py:321
  133.0 1.6 %shard_map.102 = (bf16[128,2048]{1,0:T(8,128)(2,1)}, f32[4,128]{1,0:T(4,128)S(1)}, s32[4]{0:T(128)}) custom-call(s32[4]{0:T(128)S(1)} %get-tuple-element.147.ticket_ref, bf16[128,2176]{1,0:T(8,128)(2,1)S(1)} %get-tuple-element.144.refs_0_, bf16[112,2176]{1,0:T(8,128)(2,1)S(1)} %collective-permute-done.24.refs_1_, ...), custom_call_target="tpu_custom_call" | custom-call | tf_op jit(solution)/shard_map/pallas_call | solution.py:36
  (58 shorter events, 30.7 us)
Async XLA Ops:
  0.6 22.5 %collective-permute-start = (bf16[2048,1536]{1,0:T(8,128)(2,1)}, bf16[2048,1536]{1,0:T(8,128)(2,1)}, u32[]{:S(2)}, u32[]{:S(2)}) collective-permute-start(bf16[2048,1536]{1,0:T(8,128)(2,1)} %bitcast.12), channel_id=1, source_target_pairs={{0,1},{1,0},{2,3},{3,2},{4,5},{5,4},{6,7},{7,6},{8,9},{9,8},{10,11... | collective-permute-start | bytes 18874376 | tf_op jit(solution)/shard_map/ppermute | solution.py:321
  1.1 14.4 %collective-permute-start.1 = (bf16[768,2048]{1,0:T(8,128)(2,1)}, bf16[768,2048]{1,0:T(8,128)(2,1)S(1)}, u32[]{:S(2)}, u32[]{:S(2)}) collective-permute-start(bf16[768,2048]{1,0:T(8,128)(2,1)} %bitcast.14), channel_id=1, source_target_pairs={{0,1},{1,0},{2,3},{3,2},{4,5},{5,4},{6,7},{7,6},{8,9},{9,8},{10,11... | collective-permute-start | bytes 9437192 | tf_op jit(solution)/shard_map/ppermute | solution.py:321
  3.6 24.4 %collective-permute-start.2 = (bf16[128,2176]{1,0:T(8,128)(2,1)S(1)}, bf16[128,2176]{1,0:T(8,128)(2,1)S(1)}, u32[]{:S(2)}, u32[]{:S(2)}) collective-permute-start(bf16[128,2176]{1,0:T(8,128)(2,1)S(1)} %get-tuple-element.82.refs_0_.refs_4_), channel_id=1, source_target_pairs={{0,4},{1,5},{2,6},{3,7},{4,8},{5,9},{6,10},{7,11},{8,12},{9,13},{1... | collective-permute-start | bytes 1671176 | tf_op jit(solution)/shard_map/ppermute | solution.py:321
  6.6 25.0 %collective-permute-start.3 = (bf16[112,2176]{1,0:T(8,128)(2,1)S(1)}, bf16[112,2176]{1,0:T(8,128)(2,1)S(1)}, u32[]{:S(2)}, u32[]{:S(2)}) collective-permute-start(bf16[112,2176]{1,0:T(8,128)(2,1)S(1)} %get-tuple-element.84), channel_id=1, source_target_pairs={{0,2},{1,3},{2,0},{3,1},{4,6},{5,7},{6,4},{7,5},{8,10},{9,11},{10,... | collective-permute-start | bytes 1462280 | tf_op jit(solution)/shard_map/ppermute | solution.py:321
  8.1 27.6 %collective-permute-start.4 = (bf16[128,2048]{1,0:T(8,128)(2,1)}, bf16[128,2048]{1,0:T(8,128)(2,1)S(1)}, u32[]{:S(2)}, u32[]{:S(2)}) collective-permute-start(bf16[128,2048]{1,0:T(8,128)(2,1)} %refs_2_.1), channel_id=1, source_target_pairs={{0,4},{1,5},{2,6},{3,7},{4,8},{5,9},{6,10},{7,11},{8,12},{9,13},{1... | collective-permute-start | bytes 1572872 | tf_op jit(solution)/shard_map/ppermute | solution.py:321
  9.7 1.1 copy-start
  15.6 7.5 %copy-start.3 = (bf16[768,2048]{1,0:T(8,128)(2,1)}, bf16[768,2048]{1,0:T(8,128)(2,1)S(1)}, u32[]{:S(2)}) copy-start(bf16[768,2048]{1,0:T(8,128)(2,1)S(1)} %collective-permute-done.1.refs_1_) | copy-start | bytes 9437188
  15.6 24.5 %collective-permute-start.5 = (bf16[112,2048]{1,0:T(8,128)(2,1)S(1)}, bf16[112,2048]{1,0:T(8,128)(2,1)S(1)}, u32[]{:S(2)}, u32[]{:S(2)}) collective-permute-start(bf16[112,2048]{1,0:T(8,128)(2,1)S(1)} %get-tuple-element.92), channel_id=1, source_target_pairs={{0,2},{1,3},{2,0},{3,1},{4,6},{5,7},{6,4},{7,5},{8,10},{9,11},{10,... | collective-permute-start | bytes 1376264 | tf_op jit(solution)/shard_map/ppermute | solution.py:321
  29.4 17.3 %collective-permute-start.6 = (bf16[128,2176]{1,0:T(8,128)(2,1)S(1)}, bf16[128,2176]{1,0:T(8,128)(2,1)S(1)}, u32[]{:S(2)}, u32[]{:S(2)}) collective-permute-start(bf16[128,2176]{1,0:T(8,128)(2,1)S(1)} %get-tuple-element.96.refs_0_.refs_4_), channel_id=1, source_target_pairs={{0,4},{1,5},{2,6},{3,7},{4,8},{5,9},{6,10},{7,11},{8,12},{9,13},{1... | collective-permute-start | bytes 1671176 | tf_op jit(solution)/shard_map/ppermute | solution.py:321
  31.1 19.3 %collective-permute-start.7 = (bf16[112,2176]{1,0:T(8,128)(2,1)S(1)}, bf16[112,2176]{1,0:T(8,128)(2,1)S(1)}, u32[]{:S(2)}, u32[]{:S(2)}) collective-permute-start(bf16[112,2176]{1,0:T(8,128)(2,1)S(1)} %get-tuple-element.98), channel_id=1, source_target_pairs={{0,2},{1,3},{2,0},{3,1},{4,6},{5,7},{6,4},{7,5},{8,10},{9,11},{10,... | collective-permute-start | bytes 1462280 | tf_op jit(solution)/shard_map/ppermute | solution.py:321
  31.6 8.4 %copy-start.1 = (bf16[128,2048]{1,0:T(8,128)(2,1)S(1)}, bf16[128,2048]{1,0:T(8,128)(2,1)}, u32[]{:S(2)}) copy-start(bf16[128,2048]{1,0:T(8,128)(2,1)} %refs_2_.1) | copy-start | bytes 1572868
  36.9 21.1 %collective-permute-start.8 = (bf16[128,2048]{1,0:T(8,128)(2,1)S(1)}, bf16[128,2048]{1,0:T(8,128)(2,1)S(1)}, u32[]{:S(2)}, u32[]{:S(2)}) collective-permute-start(bf16[128,2048]{1,0:T(8,128)(2,1)S(1)} %get-tuple-element.101.refs_2_), channel_id=1, source_target_pairs={{0,4},{1,5},{2,6},{3,7},{4,8},{5,9},{6,10},{7,11},{8,12},{9,13},{1... | collective-permute-start | bytes 1572872 | tf_op jit(solution)/shard_map/ppermute | solution.py:321
  38.5 21.2 %collective-permute-start.9 = (bf16[112,2048]{1,0:T(8,128)(2,1)S(1)}, bf16[112,2048]{1,0:T(8,128)(2,1)S(1)}, u32[]{:S(2)}, u32[]{:S(2)}) collective-permute-start(bf16[112,2048]{1,0:T(8,128)(2,1)S(1)} %get-tuple-element.105), channel_id=1, source_target_pairs={{0,2},{1,3},{2,0},{3,1},{4,6},{5,7},{6,4},{7,5},{8,10},{9,11},{10,... | collective-permute-start | bytes 1376264 | tf_op jit(solution)/shard_map/ppermute | solution.py:321
  48.2 18.2 %collective-permute-start.10 = (bf16[112,2176]{1,0:T(8,128)(2,1)S(1)}, bf16[112,2176]{1,0:T(8,128)(2,1)S(1)}, u32[]{:S(2)}, u32[]{:S(2)}) collective-permute-start(bf16[112,2176]{1,0:T(8,128)(2,1)S(1)} %get-tuple-element.108), channel_id=1, source_target_pairs={{0,2},{1,3},{2,0},{3,1},{4,6},{5,7},{6,4},{7,5},{8,10},{9,11},{10,... | collective-permute-start | bytes 1462280 | tf_op jit(solution)/shard_map/ppermute | solution.py:321
  48.8 21.7 %collective-permute-start.11 = (bf16[128,2176]{1,0:T(8,128)(2,1)S(1)}, bf16[128,2176]{1,0:T(8,128)(2,1)S(1)}, u32[]{:S(2)}, u32[]{:S(2)}) collective-permute-start(bf16[128,2176]{1,0:T(8,128)(2,1)S(1)} %get-tuple-element.107.refs_0_.refs_4_), channel_id=1, source_target_pairs={{0,4},{1,5},{2,6},{3,7},{4,8},{5,9},{6,10},{7,11},{8,12},{9,13},{1... | collective-permute-start | bytes 1671176 | tf_op jit(solution)/shard_map/ppermute | solution.py:321
  59.1 17.2 %collective-permute-start.12 = (bf16[112,2048]{1,0:T(8,128)(2,1)S(1)}, bf16[112,2048]{1,0:T(8,128)(2,1)S(1)}, u32[]{:S(2)}, u32[]{:S(2)}) collective-permute-start(bf16[112,2048]{1,0:T(8,128)(2,1)S(1)} %get-tuple-element.116), channel_id=1, source_target_pairs={{0,2},{1,3},{2,0},{3,1},{4,6},{5,7},{6,4},{7,5},{8,10},{9,11},{10,... | collective-permute-start | bytes 1376264 | tf_op jit(solution)/shard_map/ppermute | solution.py:321
  59.7 23.1 %collective-permute-start.13 = (bf16[128,2048]{1,0:T(8,128)(2,1)S(1)}, bf16[128,2048]{1,0:T(8,128)(2,1)S(1)}, u32[]{:S(2)}, u32[]{:S(2)}) collective-permute-start(bf16[128,2048]{1,0:T(8,128)(2,1)S(1)} %get-tuple-element.115.refs_2_), channel_id=1, source_target_pairs={{0,4},{1,5},{2,6},{3,7},{4,8},{5,9},{6,10},{7,11},{8,12},{9,13},{1... | collective-permute-start | bytes 1572872 | tf_op jit(solution)/shard_map/ppermute | solution.py:321
  72.0 13.0 %collective-permute-start.14 = (bf16[112,2176]{1,0:T(8,128)(2,1)S(1)}, bf16[112,2176]{1,0:T(8,128)(2,1)S(1)}, u32[]{:S(2)}, u32[]{:S(2)}) collective-permute-start(bf16[112,2176]{1,0:T(8,128)(2,1)S(1)} %get-tuple-element.120), channel_id=1, source_target_pairs={{0,2},{1,3},{2,0},{3,1},{4,6},{5,7},{6,4},{7,5},{8,10},{9,11},{10,... | collective-permute-start | bytes 1462280 | tf_op jit(solution)/shard_map/ppermute | solution.py:321
  74.7 18.3 %collective-permute-start.15 = (bf16[128,2176]{1,0:T(8,128)(2,1)S(1)}, bf16[128,2176]{1,0:T(8,128)(2,1)S(1)}, u32[]{:S(2)}, u32[]{:S(2)}) collective-permute-start(bf16[128,2176]{1,0:T(8,128)(2,1)S(1)} %get-tuple-element.124), channel_id=1, source_target_pairs={{0,4},{1,5},{2,6},{3,7},{4,8},{5,9},{6,10},{7,11},{8,12},{9,13},{1... | collective-permute-start | bytes 1671176 | tf_op jit(solution)/shard_map/ppermute | solution.py:321
  84.0 12.4 %collective-permute-start.16 = (bf16[112,2048]{1,0:T(8,128)(2,1)S(1)}, bf16[112,2048]{1,0:T(8,128)(2,1)S(1)}, u32[]{:S(2)}, u32[]{:S(2)}) collective-permute-start(bf16[112,2048]{1,0:T(8,128)(2,1)S(1)} %get-tuple-element.128), channel_id=1, source_target_pairs={{0,2},{1,3},{2,0},{3,1},{4,6},{5,7},{6,4},{7,5},{8,10},{9,11},{10,... | collective-permute-start | bytes 1376264 | tf_op jit(solution)/shard_map/ppermute | solution.py:321
  89.1 15.1 %collective-permute-start.18 = (bf16[128,2176]{1,0:T(8,128)(2,1)S(1)}, bf16[128,2176]{1,0:T(8,128)(2,1)S(1)}, u32[]{:S(2)}, u32[]{:S(2)}) collective-permute-start(bf16[128,2176]{1,0:T(8,128)(2,1)S(1)} %get-tuple-element.132), channel_id=1, source_target_pairs={{0,4},{1,5},{2,6},{3,7},{4,8},{5,9},{6,10},{7,11},{8,12},{9,13},{1... | collective-permute-start | bytes 1671176 | tf_op jit(solution)/shard_map/ppermute | solution.py:321
  94.3 9.3 %collective-permute-start.17 = (bf16[128,1024]{1,0:T(8,128)(2,1)S(1)}, bf16[128,1024]{1,0:T(8,128)(2,1)S(1)}, u32[]{:S(2)}, u32[]{:S(2)}) collective-permute-start(bf16[128,1024]{1,0:T(8,128)(2,1)S(1)} %get-tuple-element.131), channel_id=1, source_target_pairs={{0,2},{1,3},{2,0},{3,1},{4,6},{5,7},{6,4},{7,5},{8,10},{9,11},{10,... | collective-permute-start | bytes 786440 | tf_op jit(solution)/shard_map/ppermute | solution.py:321
  95.0 14.1 %collective-permute-start.19 = (bf16[128,1152]{1,0:T(8,128)(2,1)S(1)}, bf16[128,1152]{1,0:T(8,128)(2,1)S(1)}, u32[]{:S(2)}, u32[]{:S(2)}) collective-permute-start(bf16[128,1152]{1,0:T(8,128)(2,1)S(1)} %get-tuple-element.135), channel_id=1, source_target_pairs={{0,2},{1,3},{2,0},{3,1},{4,6},{5,7},{6,4},{7,5},{8,10},{9,11},{10,... | collective-permute-start | bytes 884744 | tf_op jit(solution)/shard_map/ppermute | solution.py:321
  105.4 9.6 %collective-permute-start.21 = (bf16[128,1024]{1,0:T(8,128)(2,1)S(1)}, bf16[128,1024]{1,0:T(8,128)(2,1)S(1)}, u32[]{:S(2)}, u32[]{:S(2)}) collective-permute-start(bf16[128,1024]{1,0:T(8,128)(2,1)S(1)} %get-tuple-element.139), channel_id=1, source_target_pairs={{0,4},{1,5},{2,6},{3,7},{4,8},{5,9},{6,10},{7,11},{8,12},{9,13},{1... | collective-permute-start | bytes 786440 | tf_op jit(solution)/shard_map/ppermute | solution.py:321
  105.5 8.6 %collective-permute-start.20 = (bf16[112,1024]{1,0:T(8,128)(2,1)S(1)}, bf16[112,1024]{1,0:T(8,128)(2,1)S(1)}, u32[]{:S(2)}, u32[]{:S(2)}) collective-permute-start(bf16[112,1024]{1,0:T(8,128)(2,1)S(1)} %get-tuple-element.138), channel_id=1, source_target_pairs={{0,2},{1,3},{2,0},{3,1},{4,6},{5,7},{6,4},{7,5},{8,10},{9,11},{10,... | collective-permute-start | bytes 688136 | tf_op jit(solution)/shard_map/ppermute | solution.py:321
  106.4 13.2 %collective-permute-start.22 = (bf16[112,1152]{1,0:T(8,128)(2,1)S(1)}, bf16[112,1152]{1,0:T(8,128)(2,1)S(1)}, u32[]{:S(2)}, u32[]{:S(2)}) collective-permute-start(bf16[112,1152]{1,0:T(8,128)(2,1)S(1)} %get-tuple-element.141), channel_id=1, source_target_pairs={{0,2},{1,3},{2,0},{3,1},{4,6},{5,7},{6,4},{7,5},{8,10},{9,11},{10,... | collective-permute-start | bytes 774152 | tf_op jit(solution)/shard_map/ppermute | solution.py:321
  110.3 18.1 %collective-permute-start.24 = (bf16[112,2176]{1,0:T(8,128)(2,1)S(1)}, bf16[112,2176]{1,0:T(8,128)(2,1)S(1)}, u32[]{:S(2)}, u32[]{:S(2)}) collective-permute-start(bf16[112,2176]{1,0:T(8,128)(2,1)S(1)} %get-tuple-element.145), channel_id=1, source_target_pairs={{0,2},{1,3},{2,0},{3,1},{4,6},{5,7},{6,4},{7,5},{8,10},{9,11},{10,... | collective-permute-start | bytes 1462280 | tf_op jit(solution)/shard_map/ppermute | solution.py:321
  111.9 11.4 %collective-permute-start.23 = (bf16[128,1152]{1,0:T(8,128)(2,1)S(1)}, bf16[128,1152]{1,0:T(8,128)(2,1)S(1)}, u32[]{:S(2)}, u32[]{:S(2)}) collective-permute-start(bf16[128,1152]{1,0:T(8,128)(2,1)S(1)} %get-tuple-element.142), channel_id=1, source_target_pairs={{0,4},{1,5},{2,6},{3,7},{4,8},{5,9},{6,10},{7,11},{8,12},{9,13},{1... | collective-permute-start | bytes 884744 | tf_op jit(solution)/shard_map/ppermute | solution.py:321
  116.1 12.6 %collective-permute-start.25 = (bf16[128,1024]{1,0:T(8,128)(2,1)S(1)}, bf16[128,1024]{1,0:T(8,128)(2,1)S(1)}, u32[]{:S(2)}, u32[]{:S(2)}) collective-permute-start(bf16[128,1024]{1,0:T(8,128)(2,1)S(1)} %get-tuple-element.146), channel_id=1, source_target_pairs={{0,4},{1,5},{2,6},{3,7},{4,8},{5,9},{6,10},{7,11},{8,12},{9,13},{1... | collective-permute-start | bytes 786440 | tf_op jit(solution)/shard_map/ppermute | solution.py:321
  124.4 8.6 %collective-permute-start.26 = (bf16[128,1152]{1,0:T(8,128)(2,1)S(1)}, bf16[128,1152]{1,0:T(8,128)(2,1)S(1)}, u32[]{:S(2)}, u32[]{:S(2)}) collective-permute-start(bf16[128,1152]{1,0:T(8,128)(2,1)S(1)} %get-tuple-element.148), channel_id=1, source_target_pairs={{0,4},{1,5},{2,6},{3,7},{4,8},{5,9},{6,10},{7,11},{8,12},{9,13},{1... | collective-permute-start | bytes 884744 | tf_op jit(solution)/shard_map/ppermute | solution.py:321
  128.7 4.2 %copy-start.2 = (s32[128,4]{0,1:T(4,128)S(1)}, s32[128,4]{0,1:T(4,128)}, u32[]{:S(2)}) copy-start(s32[128,4]{0,1:T(4,128)} %param.8) | copy-start | bytes 6148

commit v4 on v3

--- a/solution.py
+++ b/solution.py
@@ -208,8 +208,11 @@
     out_ref[:, at:] = rest[:, : features - at].astype(BF16)
     gates = rest[:, features - at :].T
     expert = lax.broadcasted_iota(jnp.int32, gates.shape, 0)
-    for k in range(ids_ref.shape[0]):
-        gates_ref[k : k + 1, :] = jnp.sum(jnp.where(expert == ids_ref[k : k + 1, :], gates, 0.0), axis=0, keepdims=True)
+    chosen = [
+        jnp.sum(jnp.where(expert == ids_ref[k : k + 1, :], gates, 0.0), axis=0, keepdims=True)
+        for k in range(ids_ref.shape[0])
+    ]
+    gates_ref[...] = jnp.concatenate(chosen, axis=0).astype(BF16)
 
 
 def finish(queue, own, back, sel, ids, first, second):
@@ -217,7 +220,7 @@
     front = queue.run(front_kernel, [own, back, sel, first], [array(*first.shape)], flops=HOLD[2])
     return queue.run(
         finish_kernel, [own, back, sel, second, front, ids],
-        [array(rows, width - LANES), array(*ids.shape, dtype=F32)],
+        [array(rows, width - LANES), array(*ids.shape)],
     )
 
 
@@ -360,8 +363,8 @@
         gs.append(g)
 
     take_tokens(0)
+    w0, d0 = load(queue, w0, d0)
     take_grads(0)
-    w0, d0 = load(queue, w0, d0)
     w1, d1 = load(queue, w1, d1)
     take_tokens(1)
     for s in range(depth):
@@ -377,11 +380,11 @@
         if s == early + 2:
             lifted = place(queue, far[s - 1], xf[s - 1], rows, lifted, cuts=halves)
             back[s - 1] = [move(a, across) for a in lifted]
-        if s < 2:
-            take_grads(s + 1)
+        if s == 0:
+            take_grads(1)
         cuts = halves if s == last else whole
         mine, *other = backward(queue, p0, p1, gs[s], gf[s], xs[s], xf[s], d0, d1, w0, w1, cuts)
-        if 1 < s < last:
+        if 0 < s < last:
             take_grads(s + 1)
         own.append(mine)
         far.append(other[0])
@@ -404,7 +407,7 @@
             ]
         carried = [move(a, up) for a in carried]
     grad_tokens, grad_gates = finish(queue, own[0], back[0], sels[0], ids, *carried)
-    return grad_tokens, grad_gates.T.astype(BF16)
+    return grad_tokens, grad_gates.T
 
 
 def solution(mesh):

time: 135 us -> 133 us (0.985)
  transfers between devices with their start and end apart: 27 -> 27, of which waited for: 14 -> 13; matrix products, arithmetic and copies ran while one was open for 0% -> 0% of each run, Pallas kernels for 53% -> 54%
where the time goes in v4:
time: 133 us
  Pallas kernels  73.8 us (55%)
  waiting for transfers between devices  29.6 us (22%)
  starting transfers between devices  28.5 us (21%)
    pallas_call x26, Pallas kernels, run(): pl.pallas_call(body, in_specs=[SCALAR] + [ANYWHERE] * anywhere + [LOCAL]...  73.8 us
    ppermute x27, waiting for transfers between devices, shards(): move = lambda a, pairs: lax.ppermute(a, 'expert', pairs)  29.6 us
    ppermute x27, starting transfers between devices, shards(): move = lambda a, pairs: lax.ppermute(a, 'expert', pairs)  28.5 us
  transfers between devices with their start and end apart: 27, of which 13 were waited for; matrix products, arithmetic and copies ran while one was open for 0% of the time, Pallas kernels for 54%

profile of v4, /device:TPU:0, one launch (start us, length us, event | category | flops | bytes accessed | tf_op | source)
XLA Modules:
  0.0 133.1 jit_solution(10762939142338656320)
XLA Ops:
  1.3 2.3 %shard_map.77 = (bf16[128,2176]{1,0:T(8,128)(2,1)S(1)}, bf16[112,2176]{1,0:T(8,128)(2,1)S(1)}, bf16[112,128]{1,0:T(8,128)(2,1)S(1)}, s32[4]{0:T(128)S(1)}) custom-call(s32[4]{0:T(128)S(1)} %pad_add_fusion.ticket_ref, bf16[128,2048]{1,0:T(8,128)(2,1)} %refs_0_.1, s32[4,128]{1,0:T(4,128)} %bitcast.9, bf16[4,128]{1,0:T(4,128)(2,1)} %bitcast.15), custom_call_target="tpu_custom_call" | custom-call | tf_op jit(solution)/shard_map/pallas_call | solution.py:36
  3.6 3.1 %collective-permute-start.2 = (bf16[128,2176]{1,0:T(8,128)(2,1)S(1)}, bf16[128,2176]{1,0:T(8,128)(2,1)S(1)}, u32[]{:S(2)}, u32[]{:S(2)}) collective-permute-start(bf16[128,2176]{1,0:T(8,128)(2,1)S(1)} %get-tuple-element.82.refs_0_.refs_4_), channel_id=1, source_target_pairs={{0,4},{1,5},{2,6},{3,7},{4,8},{5,9},{6,10},{7,11},{8,12},{9,13},{1... | collective-permute-start | bytes 1671176 | tf_op jit(solution)/shard_map/ppermute | solution.py:324
  6.6 1.5 %collective-permute-start.3 = (bf16[112,2176]{1,0:T(8,128)(2,1)S(1)}, bf16[112,2176]{1,0:T(8,128)(2,1)S(1)}, u32[]{:S(2)}, u32[]{:S(2)}) collective-permute-start(bf16[112,2176]{1,0:T(8,128)(2,1)S(1)} %get-tuple-element.84), channel_id=1, source_target_pairs={{0,2},{1,3},{2,0},{3,1},{4,6},{5,7},{6,4},{7,5},{8,10},{9,11},{10,... | collective-permute-start | bytes 1462280 | tf_op jit(solution)/shard_map/ppermute | solution.py:324
  8.1 1.6 %collective-permute-start.4 = (bf16[128,2048]{1,0:T(8,128)(2,1)}, bf16[128,2048]{1,0:T(8,128)(2,1)S(1)}, u32[]{:S(2)}, u32[]{:S(2)}) collective-permute-start(bf16[128,2048]{1,0:T(8,128)(2,1)} %refs_2_.1), channel_id=1, source_target_pairs={{0,4},{1,5},{2,6},{3,7},{4,8},{5,9},{6,10},{7,11},{8,12},{9,13},{1... | collective-permute-start | bytes 1572872 | tf_op jit(solution)/shard_map/ppermute | solution.py:324
  9.7 4.9 %shard_map.78 = (bf16[2048,1536]{1,0:T(8,128)(2,1)S(1)}, bf16[768,2048]{1,0:T(8,128)(2,1)S(1)}, s32[4]{0:T(128)S(1)}) custom-call(s32[4]{0:T(128)S(1)} %get-tuple-element.77.ticket_ref, bf16[2048,1536]{1,0:T(8,128)(2,1)} %bitcast.12, bf16[768,2048]{1,0:T(8,128)(2,1)} %bitcast.14), custom_call_target="tpu_custom_call" | custom-call | tf_op jit(solution)/shard_map/pallas_call | solution.py:36
  15.8 2.4 %collective-permute-start.5 = (bf16[112,2048]{1,0:T(8,128)(2,1)S(1)}, bf16[112,2048]{1,0:T(8,128)(2,1)S(1)}, u32[]{:S(2)}, u32[]{:S(2)}) collective-permute-start(bf16[112,2048]{1,0:T(8,128)(2,1)S(1)} %get-tuple-element.92), channel_id=1, source_target_pairs={{0,2},{1,3},{2,0},{3,1},{4,6},{5,7},{6,4},{7,5},{8,10},{9,11},{10,... | collective-permute-start | bytes 1376264 | tf_op jit(solution)/shard_map/ppermute | solution.py:324
  18.2 4.9 %shard_map.80 = (bf16[2048,1536]{1,0:T(8,128)(2,1)S(1)}, bf16[768,2048]{1,0:T(8,128)(2,1)S(1)}, s32[4]{0:T(128)S(1)}) custom-call(s32[4]{0:T(128)S(1)} %get-tuple-element.80.ticket_ref, bf16[2048,1536]{1,0:T(8,128)(2,1)} %collective-permute-done.refs_0_, bf16[768,2048]{1,0:T(8,128)(2,1)} %copy-done.2), custom_call_target="tpu_custom_call" | custom-call | tf_op jit(solution)/shard_map/pallas_call | solution.py:36
  24.5 1.8 %collective-permute-start.6 = (bf16[128,2176]{1,0:T(8,128)(2,1)S(1)}, bf16[128,2176]{1,0:T(8,128)(2,1)S(1)}, u32[]{:S(2)}, u32[]{:S(2)}) collective-permute-start(bf16[128,2176]{1,0:T(8,128)(2,1)S(1)} %get-tuple-element.96.refs_0_.refs_4_), channel_id=1, source_target_pairs={{0,4},{1,5},{2,6},{3,7},{4,8},{5,9},{6,10},{7,11},{8,12},{9,13},{1... | collective-permute-start | bytes 1671176 | tf_op jit(solution)/shard_map/ppermute | solution.py:324
  27.9 4.1 %shard_map.82 = (f32[240,1536]{1,0:T(8,128)S(1)}, f32[240,1536]{1,0:T(8,128)S(1)}, s32[4]{0:T(128)S(1)}) custom-call(s32[4]{0:T(128)S(1)} %get-tuple-element.83.ticket_ref, bf16[128,2176]{1,0:T(8,128)(2,1)S(1)} %get-tuple-element.82.refs_0_.refs_4_, bf16[112,2176]{1,0:T(8,128)(2,1)S(1)} %collective-permute-done.3.refs_1_.refs_5_, ...), custom_call_target="tpu_custom_call" | custom-call | flops 905969664 | tf_op jit(solution)/shard_map/pallas_call | solution.py:36
  34.4 1.8 %collective-permute-start.8 = (bf16[112,2048]{1,0:T(8,128)(2,1)S(1)}, bf16[112,2048]{1,0:T(8,128)(2,1)S(1)}, u32[]{:S(2)}, u32[]{:S(2)}) collective-permute-start(bf16[112,2048]{1,0:T(8,128)(2,1)S(1)} %get-tuple-element.103), channel_id=1, source_target_pairs={{0,2},{1,3},{2,0},{3,1},{4,6},{5,7},{6,4},{7,5},{8,10},{9,11},{10,... | collective-permute-start | bytes 1376264 | tf_op jit(solution)/shard_map/ppermute | solution.py:324
  36.3 6.6 %shard_map.84 = (bf16[128,2176]{1,0:T(8,128)(2,1)S(1)}, bf16[112,2176]{1,0:T(8,128)(2,1)S(1)}, s32[4]{0:T(128)S(1)}) custom-call(s32[4]{0:T(128)S(1)} %get-tuple-element.89.ticket_ref, f32[240,1536]{1,0:T(8,128)S(1)} %get-tuple-element.90.refs_0_, f32[240,1536]{1,0:T(8,128)S(1)} %get-tuple-element.91.refs_1_, bf16[128,2048]{1,0:T(8,128)(2,1)S(1)} %copy-done, ...), custom_call_target="tpu_custom_call" | custom-call | flops 1358954496 | tf_op jit(solution)/shard_map/pallas_call | solution.py:36
  42.9 2.3 %collective-permute-done.6.refs_0_ = bf16[128,2176]{1,0:T(8,128)(2,1)S(1)} collective-permute-done((bf16[128,2176]{1,0:T(8,128)(2,1)S(1)}, bf16[128,2176]{1,0:T(8,128)(2,1)S(1)}, u32[]{:S(2)}, u32[]{:S(2)}) %collective-permute-start.6) | collective-permute-done | bytes 557088 | tf_op jit(solution)/shard_map/ppermute | solution.py:324
  46.7 1.8 %collective-permute-start.10 = (bf16[112,2176]{1,0:T(8,128)(2,1)S(1)}, bf16[112,2176]{1,0:T(8,128)(2,1)S(1)}, u32[]{:S(2)}, u32[]{:S(2)}) collective-permute-start(bf16[112,2176]{1,0:T(8,128)(2,1)S(1)} %get-tuple-element.108), channel_id=1, source_target_pairs={{0,2},{1,3},{2,0},{3,1},{4,6},{5,7},{6,4},{7,5},{8,10},{9,11},{10,... | collective-permute-start | bytes 1462280 | tf_op jit(solution)/shard_map/ppermute | solution.py:324
  48.5 4.1 %shard_map.86 = (f32[240,1536]{1,0:T(8,128)S(1)}, f32[240,1536]{1,0:T(8,128)S(1)}, s32[4]{0:T(128)S(1)}) custom-call(s32[4]{0:T(128)S(1)} %get-tuple-element.97.ticket_ref, bf16[128,2176]{1,0:T(8,128)(2,1)S(1)} %get-tuple-element.96.refs_0_.refs_4_, bf16[112,2176]{1,0:T(8,128)(2,1)S(1)} %collective-permute-done.7.refs_1_.refs_5_, ...), custom_call_target="tpu_custom_call" | custom-call | flops 905969664 | tf_op jit(solution)/shard_map/pallas_call | solution.py:36
  52.7 6.6 %shard_map.87 = (bf16[128,2176]{1,0:T(8,128)(2,1)S(1)}, bf16[112,2176]{1,0:T(8,128)(2,1)S(1)}, s32[4]{0:T(128)S(1)}) custom-call(s32[4]{0:T(128)S(1)} %get-tuple-element.99.ticket_ref, f32[240,1536]{1,0:T(8,128)S(1)} %get-tuple-element.100.refs_0_, f32[240,1536]{1,0:T(8,128)S(1)} %get-tuple-element.101.refs_1_, ...), custom_call_target="tpu_custom_call" | custom-call | flops 1358954496 | tf_op jit(solution)/shard_map/pallas_call | solution.py:36
  60.8 1.6 %collective-permute-start.13 = (bf16[128,2048]{1,0:T(8,128)(2,1)S(1)}, bf16[128,2048]{1,0:T(8,128)(2,1)S(1)}, u32[]{:S(2)}, u32[]{:S(2)}) collective-permute-start(bf16[128,2048]{1,0:T(8,128)(2,1)S(1)} %get-tuple-element.115.refs_2_), channel_id=1, source_target_pairs={{0,4},{1,5},{2,6},{3,7},{4,8},{5,9},{6,10},{7,11},{8,12},{9,13},{1... | collective-permute-start | bytes 1572872 | tf_op jit(solution)/shard_map/ppermute | solution.py:324
  62.4 4.1 %shard_map.89 = (f32[240,1536]{1,0:T(8,128)S(1)}, f32[240,1536]{1,0:T(8,128)S(1)}, s32[4]{0:T(128)S(1)}) custom-call(s32[4]{0:T(128)S(1)} %get-tuple-element.106.ticket_ref, bf16[128,2176]{1,0:T(8,128)(2,1)S(1)} %get-tuple-element.107.refs_0_.refs_4_, bf16[112,2176]{1,0:T(8,128)(2,1)S(1)} %collective-permute-done.10.refs_1_.refs_5_, ...), custom_call_target="tpu_custom_call" | custom-call | flops 905969664 | tf_op jit(solution)/shard_map/pallas_call | solution.py:36
  66.6 1.9 %collective-permute-done.11.refs_0_.refs_4_ = bf16[128,2176]{1,0:T(8,128)(2,1)S(1)} collective-permute-done((bf16[128,2176]{1,0:T(8,128)(2,1)S(1)}, bf16[128,2176]{1,0:T(8,128)(2,1)S(1)}, u32[]{:S(2)}, u32[]{:S(2)}) %collective-permute-start.11) | collective-permute-done | bytes 557088 | tf_op jit(solution)/shard_map/ppermute | solution.py:324
  69.8 1.8 %collective-permute-start.14 = (bf16[112,2176]{1,0:T(8,128)(2,1)S(1)}, bf16[112,2176]{1,0:T(8,128)(2,1)S(1)}, u32[]{:S(2)}, u32[]{:S(2)}) collective-permute-start(bf16[112,2176]{1,0:T(8,128)(2,1)S(1)} %get-tuple-element.120), channel_id=1, source_target_pairs={{0,2},{1,3},{2,0},{3,1},{4,6},{5,7},{6,4},{7,5},{8,10},{9,11},{10,... | collective-permute-start | bytes 1462280 | tf_op jit(solution)/shard_map/ppermute | solution.py:324
  73.1 6.6 %shard_map.92 = (bf16[128,2176]{1,0:T(8,128)(2,1)S(1)}, bf16[112,2176]{1,0:T(8,128)(2,1)S(1)}, s32[4]{0:T(128)S(1)}) custom-call(s32[4]{0:T(128)S(1)} %get-tuple-element.112.ticket_ref, f32[240,1536]{1,0:T(8,128)S(1)} %get-tuple-element.113.refs_0_, f32[240,1536]{1,0:T(8,128)S(1)} %get-tuple-element.114.refs_1_, ...), custom_call_target="tpu_custom_call" | custom-call | flops 1358954496 | tf_op jit(solution)/shard_map/pallas_call | solution.py:36
  80.9 1.8 %collective-permute-start.16 = (bf16[112,2048]{1,0:T(8,128)(2,1)S(1)}, bf16[112,2048]{1,0:T(8,128)(2,1)S(1)}, u32[]{:S(2)}, u32[]{:S(2)}) collective-permute-start(bf16[112,2048]{1,0:T(8,128)(2,1)S(1)} %get-tuple-element.128), channel_id=1, source_target_pairs={{0,2},{1,3},{2,0},{3,1},{4,6},{5,7},{6,4},{7,5},{8,10},{9,11},{10,... | collective-permute-start | bytes 1376264 | tf_op jit(solution)/shard_map/ppermute | solution.py:324
  82.6 4.2 %shard_map.94 = (f32[240,1536]{1,0:T(8,128)S(1)}, f32[240,1536]{1,0:T(8,128)S(1)}, bf16[128,2176]{1,0:T(8,128)(2,1)S(1)}, s32[4]{0:T(128)S(1)}) custom-call(s32[4]{0:T(128)S(1)} %get-tuple-element.119.ticket_ref, bf16[128,2176]{1,0:T(8,128)(2,1)S(1)} %collective-permute-done.11.refs_0_.refs_4_, ...), custom_call_target="tpu_custom_call" | custom-call | flops 905969664 | tf_op jit(solution)/shard_map/pallas_call | solution.py:36
  87.0 4.6 %collective-permute-done.15.refs_2_ = bf16[128,2176]{1,0:T(8,128)(2,1)S(1)} collective-permute-done((bf16[128,2176]{1,0:T(8,128)(2,1)S(1)}, bf16[128,2176]{1,0:T(8,128)(2,1)S(1)}, u32[]{:S(2)}, u32[]{:S(2)}) %collective-permute-start.15) | collective-permute-done | bytes 557088 | tf_op jit(solution)/shard_map/ppermute | solution.py:324
  92.9 1.8 %collective-permute-start.17 = (bf16[128,1024]{1,0:T(8,128)(2,1)S(1)}, bf16[128,1024]{1,0:T(8,128)(2,1)S(1)}, u32[]{:S(2)}, u32[]{:S(2)}) collective-permute-start(bf16[128,1024]{1,0:T(8,128)(2,1)S(1)} %get-tuple-element.131), channel_id=1, source_target_pairs={{0,2},{1,3},{2,0},{3,1},{4,6},{5,7},{6,4},{7,5},{8,10},{9,11},{10,... | collective-permute-start | bytes 786440 | tf_op jit(solution)/shard_map/ppermute | solution.py:324
  95.0 6.7 %shard_map.96 = (bf16[128,2176]{1,0:T(8,128)(2,1)S(1)}, bf16[112,1024]{1,0:T(8,128)(2,1)S(1)}, bf16[112,1152]{1,0:T(8,128)(2,1)S(1)}, s32[4]{0:T(128)S(1)}) custom-call(s32[4]{0:T(128)S(1)} %get-tuple-element.125.ticket_ref, f32[240,1536]{1,0:T(8,128)S(1)} %get-tuple-element.126.refs_0_, f32[240,1536]{1,0:T(8,128)S(1)} %get-tuple-element.127.refs_1_, ...), custom_call_target="tpu_custom_call" | custom-call | flops 1358954496 | tf_op jit(solution)/shard_map/pallas_call | solution.py:36
  104.2 1.6 %collective-permute-start.20 = (bf16[112,1024]{1,0:T(8,128)(2,1)S(1)}, bf16[112,1024]{1,0:T(8,128)(2,1)S(1)}, u32[]{:S(2)}, u32[]{:S(2)}) collective-permute-start(bf16[112,1024]{1,0:T(8,128)(2,1)S(1)} %get-tuple-element.138), channel_id=1, source_target_pairs={{0,2},{1,3},{2,0},{3,1},{4,6},{5,7},{6,4},{7,5},{8,10},{9,11},{10,... | collective-permute-start | bytes 688136 | tf_op jit(solution)/shard_map/ppermute | solution.py:324
  110.3 2.5 %collective-permute-done.20.refs_1_ = bf16[112,1024]{1,0:T(8,128)(2,1)S(1)} collective-permute-done((bf16[112,1024]{1,0:T(8,128)(2,1)S(1)}, bf16[112,1024]{1,0:T(8,128)(2,1)S(1)}, u32[]{:S(2)}, u32[]{:S(2)}) %collective-permute-start.20) | collective-permute-done | bytes 229408 | tf_op jit(solution)/shard_map/ppermute | solution.py:324
  115.3 3.1 %collective-permute-done.22.refs_1_ = bf16[112,1152]{1,0:T(8,128)(2,1)S(1)} collective-permute-done((bf16[112,1152]{1,0:T(8,128)(2,1)S(1)}, bf16[112,1152]{1,0:T(8,128)(2,1)S(1)}, u32[]{:S(2)}, u32[]{:S(2)}) %collective-permute-start.22) | collective-permute-done | bytes 258080 | tf_op jit(solution)/shard_map/ppermute | solution.py:324
  118.3 2.5 %collective-permute-done.23.refs_3_ = bf16[128,1152]{1,0:T(8,128)(2,1)S(1)} collective-permute-done((bf16[128,1152]{1,0:T(8,128)(2,1)S(1)}, bf16[128,1152]{1,0:T(8,128)(2,1)S(1)}, u32[]{:S(2)}, u32[]{:S(2)}) %collective-permute-start.23) | collective-permute-done | bytes 294944 | tf_op jit(solution)/shard_map/ppermute | solution.py:324
  122.1 5.4 %collective-permute-done.24.refs_1_ = bf16[112,2176]{1,0:T(8,128)(2,1)S(1)} collective-permute-done((bf16[112,2176]{1,0:T(8,128)(2,1)S(1)}, bf16[112,2176]{1,0:T(8,128)(2,1)S(1)}, u32[]{:S(2)}, u32[]{:S(2)}) %collective-permute-start.24) | collective-permute-done | bytes 487456 | tf_op jit(solution)/shard_map/ppermute | solution.py:324
  128.6 2.7 %collective-permute-done.26.refs_3_ = bf16[128,1152]{1,0:T(8,128)(2,1)S(1)} collective-permute-done((bf16[128,1152]{1,0:T(8,128)(2,1)S(1)}, bf16[128,1152]{1,0:T(8,128)(2,1)S(1)}, u32[]{:S(2)}, u32[]{:S(2)}) %collective-permute-start.26) | collective-permute-done | bytes 294944 | tf_op jit(solution)/shard_map/ppermute | solution.py:324
  131.3 1.6 %shard_map.102 = (bf16[128,2048]{1,0:T(8,128)(2,1)}, bf16[4,128]{1,0:T(4,128)(2,1)}, s32[4]{0:T(128)}) custom-call(s32[4]{0:T(128)S(1)} %get-tuple-element.147.ticket_ref, bf16[128,2176]{1,0:T(8,128)(2,1)S(1)} %get-tuple-element.144.refs_0_, bf16[112,2176]{1,0:T(8,128)(2,1)S(1)} %collective-permute-done.24.refs_1_, ...), custom_call_target="tpu_custom_call" | custom-call | tf_op jit(solution)/shard_map/pallas_call | solution.py:36
  (55 shorter events, 27.7 us)
Async XLA Ops:
  0.6 17.6 %collective-permute-start = (bf16[2048,1536]{1,0:T(8,128)(2,1)}, bf16[2048,1536]{1,0:T(8,128)(2,1)}, u32[]{:S(2)}, u32[]{:S(2)}) collective-permute-start(bf16[2048,1536]{1,0:T(8,128)(2,1)} %bitcast.11), channel_id=1, source_target_pairs={{0,1},{1,0},{2,3},{3,2},{4,5},{5,4},{6,7},{7,6},{8,9},{9,8},{10,11... | collective-permute-start | bytes 18874376 | tf_op jit(solution)/shard_map/ppermute | solution.py:324
  1.1 14.6 %collective-permute-start.1 = (bf16[768,2048]{1,0:T(8,128)(2,1)}, bf16[768,2048]{1,0:T(8,128)(2,1)S(1)}, u32[]{:S(2)}, u32[]{:S(2)}) collective-permute-start(bf16[768,2048]{1,0:T(8,128)(2,1)} %bitcast.13), channel_id=1, source_target_pairs={{0,1},{1,0},{2,3},{3,2},{4,5},{5,4},{6,7},{7,6},{8,9},{9,8},{10,11... | collective-permute-start | bytes 9437192 | tf_op jit(solution)/shard_map/ppermute | solution.py:324
  3.6 19.5 %collective-permute-start.2 = (bf16[128,2176]{1,0:T(8,128)(2,1)S(1)}, bf16[128,2176]{1,0:T(8,128)(2,1)S(1)}, u32[]{:S(2)}, u32[]{:S(2)}) collective-permute-start(bf16[128,2176]{1,0:T(8,128)(2,1)S(1)} %get-tuple-element.82.refs_0_.refs_4_), channel_id=1, source_target_pairs={{0,4},{1,5},{2,6},{3,7},{4,8},{5,9},{6,10},{7,11},{8,12},{9,13},{1... | collective-permute-start | bytes 1671176 | tf_op jit(solution)/shard_map/ppermute | solution.py:324
  6.6 21.3 %collective-permute-start.3 = (bf16[112,2176]{1,0:T(8,128)(2,1)S(1)}, bf16[112,2176]{1,0:T(8,128)(2,1)S(1)}, u32[]{:S(2)}, u32[]{:S(2)}) collective-permute-start(bf16[112,2176]{1,0:T(8,128)(2,1)S(1)} %get-tuple-element.84), channel_id=1, source_target_pairs={{0,2},{1,3},{2,0},{3,1},{4,6},{5,7},{6,4},{7,5},{8,10},{9,11},{10,... | collective-permute-start | bytes 1462280 | tf_op jit(solution)/shard_map/ppermute | solution.py:324
  8.1 25.2 %collective-permute-start.4 = (bf16[128,2048]{1,0:T(8,128)(2,1)}, bf16[128,2048]{1,0:T(8,128)(2,1)S(1)}, u32[]{:S(2)}, u32[]{:S(2)}) collective-permute-start(bf16[128,2048]{1,0:T(8,128)(2,1)} %refs_2_.1), channel_id=1, source_target_pairs={{0,4},{1,5},{2,6},{3,7},{4,8},{5,9},{6,10},{7,11},{8,12},{9,13},{1... | collective-permute-start | bytes 1572872 | tf_op jit(solution)/shard_map/ppermute | solution.py:324
  9.7 4.9 %copy-start = (bf16[128,2048]{1,0:T(8,128)(2,1)S(1)}, bf16[128,2048]{1,0:T(8,128)(2,1)}, u32[]{:S(2)}) copy-start(bf16[128,2048]{1,0:T(8,128)(2,1)} %refs_2_.1) | copy-start | bytes 1572868
  15.8 2.4 %copy-start.2 = (bf16[768,2048]{1,0:T(8,128)(2,1)}, bf16[768,2048]{1,0:T(8,128)(2,1)S(1)}, u32[]{:S(2)}) copy-start(bf16[768,2048]{1,0:T(8,128)(2,1)S(1)} %collective-permute-done.1.refs_1_) | copy-start | bytes 9437188
  15.8 20.5 %collective-permute-start.5 = (bf16[112,2048]{1,0:T(8,128)(2,1)S(1)}, bf16[112,2048]{1,0:T(8,128)(2,1)S(1)}, u32[]{:S(2)}, u32[]{:S(2)}) collective-permute-start(bf16[112,2048]{1,0:T(8,128)(2,1)S(1)} %get-tuple-element.92), channel_id=1, source_target_pairs={{0,2},{1,3},{2,0},{3,1},{4,6},{5,7},{6,4},{7,5},{8,10},{9,11},{10,... | collective-permute-start | bytes 1376264 | tf_op jit(solution)/shard_map/ppermute | solution.py:324
  24.5 20.7 %collective-permute-start.6 = (bf16[128,2176]{1,0:T(8,128)(2,1)S(1)}, bf16[128,2176]{1,0:T(8,128)(2,1)S(1)}, u32[]{:S(2)}, u32[]{:S(2)}) collective-permute-start(bf16[128,2176]{1,0:T(8,128)(2,1)S(1)} %get-tuple-element.96.refs_0_.refs_4_), channel_id=1, source_target_pairs={{0,4},{1,5},{2,6},{3,7},{4,8},{5,9},{6,10},{7,11},{8,12},{9,13},{1... | collective-permute-start | bytes 1671176 | tf_op jit(solution)/shard_map/ppermute | solution.py:324
  26.4 22.2 %collective-permute-start.7 = (bf16[112,2176]{1,0:T(8,128)(2,1)S(1)}, bf16[112,2176]{1,0:T(8,128)(2,1)S(1)}, u32[]{:S(2)}, u32[]{:S(2)}) collective-permute-start(bf16[112,2176]{1,0:T(8,128)(2,1)S(1)} %get-tuple-element.98), channel_id=1, source_target_pairs={{0,2},{1,3},{2,0},{3,1},{4,6},{5,7},{6,4},{7,5},{8,10},{9,11},{10,... | collective-permute-start | bytes 1462280 | tf_op jit(solution)/shard_map/ppermute | solution.py:324
  34.4 18.2 %collective-permute-start.8 = (bf16[112,2048]{1,0:T(8,128)(2,1)S(1)}, bf16[112,2048]{1,0:T(8,128)(2,1)S(1)}, u32[]{:S(2)}, u32[]{:S(2)}) collective-permute-start(bf16[112,2048]{1,0:T(8,128)(2,1)S(1)} %get-tuple-element.103), channel_id=1, source_target_pairs={{0,2},{1,3},{2,0},{3,1},{4,6},{5,7},{6,4},{7,5},{8,10},{9,11},{10,... | collective-permute-start | bytes 1376264 | tf_op jit(solution)/shard_map/ppermute | solution.py:324
  36.3 23.1 %collective-permute-start.9 = (bf16[128,2048]{1,0:T(8,128)(2,1)S(1)}, bf16[128,2048]{1,0:T(8,128)(2,1)S(1)}, u32[]{:S(2)}, u32[]{:S(2)}) collective-permute-start(bf16[128,2048]{1,0:T(8,128)(2,1)S(1)} %get-tuple-element.102.refs_2_), channel_id=1, source_target_pairs={{0,4},{1,5},{2,6},{3,7},{4,8},{5,9},{6,10},{7,11},{8,12},{9,13},{1... | collective-permute-start | bytes 1572872 | tf_op jit(solution)/shard_map/ppermute | solution.py:324
  46.7 15.7 %collective-permute-start.10 = (bf16[112,2176]{1,0:T(8,128)(2,1)S(1)}, bf16[112,2176]{1,0:T(8,128)(2,1)S(1)}, u32[]{:S(2)}, u32[]{:S(2)}) collective-permute-start(bf16[112,2176]{1,0:T(8,128)(2,1)S(1)} %get-tuple-element.108), channel_id=1, source_target_pairs={{0,2},{1,3},{2,0},{3,1},{4,6},{5,7},{6,4},{7,5},{8,10},{9,11},{10,... | collective-permute-start | bytes 1462280 | tf_op jit(solution)/shard_map/ppermute | solution.py:324
  48.5 19.9 %collective-permute-start.11 = (bf16[128,2176]{1,0:T(8,128)(2,1)S(1)}, bf16[128,2176]{1,0:T(8,128)(2,1)S(1)}, u32[]{:S(2)}, u32[]{:S(2)}) collective-permute-start(bf16[128,2176]{1,0:T(8,128)(2,1)S(1)} %get-tuple-element.107.refs_0_.refs_4_), channel_id=1, source_target_pairs={{0,4},{1,5},{2,6},{3,7},{4,8},{5,9},{6,10},{7,11},{8,12},{9,13},{1... | collective-permute-start | bytes 1671176 | tf_op jit(solution)/shard_map/ppermute | solution.py:324
  60.5 12.6 %collective-permute-start.12 = (bf16[112,2048]{1,0:T(8,128)(2,1)S(1)}, bf16[112,2048]{1,0:T(8,128)(2,1)S(1)}, u32[]{:S(2)}, u32[]{:S(2)}) collective-permute-start(bf16[112,2048]{1,0:T(8,128)(2,1)S(1)} %get-tuple-element.116), channel_id=1, source_target_pairs={{0,2},{1,3},{2,0},{3,1},{4,6},{5,7},{6,4},{7,5},{8,10},{9,11},{10,... | collective-permute-start | bytes 1376264 | tf_op jit(solution)/shard_map/ppermute | solution.py:324
  60.8 18.9 %collective-permute-start.13 = (bf16[128,2048]{1,0:T(8,128)(2,1)S(1)}, bf16[128,2048]{1,0:T(8,128)(2,1)S(1)}, u32[]{:S(2)}, u32[]{:S(2)}) collective-permute-start(bf16[128,2048]{1,0:T(8,128)(2,1)S(1)} %get-tuple-element.115.refs_2_), channel_id=1, source_target_pairs={{0,4},{1,5},{2,6},{3,7},{4,8},{5,9},{6,10},{7,11},{8,12},{9,13},{1... | collective-permute-start | bytes 1572872 | tf_op jit(solution)/shard_map/ppermute | solution.py:324
  69.8 12.8 %collective-permute-start.14 = (bf16[112,2176]{1,0:T(8,128)(2,1)S(1)}, bf16[112,2176]{1,0:T(8,128)(2,1)S(1)}, u32[]{:S(2)}, u32[]{:S(2)}) collective-permute-start(bf16[112,2176]{1,0:T(8,128)(2,1)S(1)} %get-tuple-element.120), channel_id=1, source_target_pairs={{0,2},{1,3},{2,0},{3,1},{4,6},{5,7},{6,4},{7,5},{8,10},{9,11},{10,... | collective-permute-start | bytes 1462280 | tf_op jit(solution)/shard_map/ppermute | solution.py:324
  72.8 18.8 %collective-permute-start.15 = (bf16[128,2176]{1,0:T(8,128)(2,1)S(1)}, bf16[128,2176]{1,0:T(8,128)(2,1)S(1)}, u32[]{:S(2)}, u32[]{:S(2)}) collective-permute-start(bf16[128,2176]{1,0:T(8,128)(2,1)S(1)} %get-tuple-element.124), channel_id=1, source_target_pairs={{0,4},{1,5},{2,6},{3,7},{4,8},{5,9},{6,10},{7,11},{8,12},{9,13},{1... | collective-permute-start | bytes 1671176 | tf_op jit(solution)/shard_map/ppermute | solution.py:324
  80.9 14.2 %collective-permute-start.16 = (bf16[112,2048]{1,0:T(8,128)(2,1)S(1)}, bf16[112,2048]{1,0:T(8,128)(2,1)S(1)}, u32[]{:S(2)}, u32[]{:S(2)}) collective-permute-start(bf16[112,2048]{1,0:T(8,128)(2,1)S(1)} %get-tuple-element.128), channel_id=1, source_target_pairs={{0,2},{1,3},{2,0},{3,1},{4,6},{5,7},{6,4},{7,5},{8,10},{9,11},{10,... | collective-permute-start | bytes 1376264 | tf_op jit(solution)/shard_map/ppermute | solution.py:324
  86.8 16.1 %collective-permute-start.18 = (bf16[128,2176]{1,0:T(8,128)(2,1)S(1)}, bf16[128,2176]{1,0:T(8,128)(2,1)S(1)}, u32[]{:S(2)}, u32[]{:S(2)}) collective-permute-start(bf16[128,2176]{1,0:T(8,128)(2,1)S(1)} %get-tuple-element.132), channel_id=1, source_target_pairs={{0,4},{1,5},{2,6},{3,7},{4,8},{5,9},{6,10},{7,11},{8,12},{9,13},{1... | collective-permute-start | bytes 1671176 | tf_op jit(solution)/shard_map/ppermute | solution.py:324
  92.9 9.3 %collective-permute-start.17 = (bf16[128,1024]{1,0:T(8,128)(2,1)S(1)}, bf16[128,1024]{1,0:T(8,128)(2,1)S(1)}, u32[]{:S(2)}, u32[]{:S(2)}) collective-permute-start(bf16[128,1024]{1,0:T(8,128)(2,1)S(1)} %get-tuple-element.131), channel_id=1, source_target_pairs={{0,2},{1,3},{2,0},{3,1},{4,6},{5,7},{6,4},{7,5},{8,10},{9,11},{10,... | collective-permute-start | bytes 786440 | tf_op jit(solution)/shard_map/ppermute | solution.py:324
  94.8 12.3 %collective-permute-start.19 = (bf16[128,1152]{1,0:T(8,128)(2,1)S(1)}, bf16[128,1152]{1,0:T(8,128)(2,1)S(1)}, u32[]{:S(2)}, u32[]{:S(2)}) collective-permute-start(bf16[128,1152]{1,0:T(8,128)(2,1)S(1)} %get-tuple-element.135), channel_id=1, source_target_pairs={{0,2},{1,3},{2,0},{3,1},{4,6},{5,7},{6,4},{7,5},{8,10},{9,11},{10,... | collective-permute-start | bytes 884744 | tf_op jit(solution)/shard_map/ppermute | solution.py:324
  104.1 9.9 %collective-permute-start.21 = (bf16[128,1024]{1,0:T(8,128)(2,1)S(1)}, bf16[128,1024]{1,0:T(8,128)(2,1)S(1)}, u32[]{:S(2)}, u32[]{:S(2)}) collective-permute-start(bf16[128,1024]{1,0:T(8,128)(2,1)S(1)} %get-tuple-element.139), channel_id=1, source_target_pairs={{0,4},{1,5},{2,6},{3,7},{4,8},{5,9},{6,10},{7,11},{8,12},{9,13},{1... | collective-permute-start | bytes 786440 | tf_op jit(solution)/shard_map/ppermute | solution.py:324
  104.2 8.6 %collective-permute-start.20 = (bf16[112,1024]{1,0:T(8,128)(2,1)S(1)}, bf16[112,1024]{1,0:T(8,128)(2,1)S(1)}, u32[]{:S(2)}, u32[]{:S(2)}) collective-permute-start(bf16[112,1024]{1,0:T(8,128)(2,1)S(1)} %get-tuple-element.138), channel_id=1, source_target_pairs={{0,2},{1,3},{2,0},{3,1},{4,6},{5,7},{6,4},{7,5},{8,10},{9,11},{10,... | collective-permute-start | bytes 688136 | tf_op jit(solution)/shard_map/ppermute | solution.py:324
  105.8 12.6 %collective-permute-start.22 = (bf16[112,1152]{1,0:T(8,128)(2,1)S(1)}, bf16[112,1152]{1,0:T(8,128)(2,1)S(1)}, u32[]{:S(2)}, u32[]{:S(2)}) collective-permute-start(bf16[112,1152]{1,0:T(8,128)(2,1)S(1)} %get-tuple-element.141), channel_id=1, source_target_pairs={{0,2},{1,3},{2,0},{3,1},{4,6},{5,7},{6,4},{7,5},{8,10},{9,11},{10,... | collective-permute-start | bytes 774152 | tf_op jit(solution)/shard_map/ppermute | solution.py:324
  108.2 19.2 %collective-permute-start.24 = (bf16[112,2176]{1,0:T(8,128)(2,1)S(1)}, bf16[112,2176]{1,0:T(8,128)(2,1)S(1)}, u32[]{:S(2)}, u32[]{:S(2)}) collective-permute-start(bf16[112,2176]{1,0:T(8,128)(2,1)S(1)} %get-tuple-element.145), channel_id=1, source_target_pairs={{0,2},{1,3},{2,0},{3,1},{4,6},{5,7},{6,4},{7,5},{8,10},{9,11},{10,... | collective-permute-start | bytes 1462280 | tf_op jit(solution)/shard_map/ppermute | solution.py:324
  109.1 11.7 %collective-permute-start.23 = (bf16[128,1152]{1,0:T(8,128)(2,1)S(1)}, bf16[128,1152]{1,0:T(8,128)(2,1)S(1)}, u32[]{:S(2)}, u32[]{:S(2)}) collective-permute-start(bf16[128,1152]{1,0:T(8,128)(2,1)S(1)} %get-tuple-element.142), channel_id=1, source_target_pairs={{0,4},{1,5},{2,6},{3,7},{4,8},{5,9},{6,10},{7,11},{8,12},{9,13},{1... | collective-permute-start | bytes 884744 | tf_op jit(solution)/shard_map/ppermute | solution.py:324
  115.2 12.2 %collective-permute-start.25 = (bf16[128,1024]{1,0:T(8,128)(2,1)S(1)}, bf16[128,1024]{1,0:T(8,128)(2,1)S(1)}, u32[]{:S(2)}, u32[]{:S(2)}) collective-permute-start(bf16[128,1024]{1,0:T(8,128)(2,1)S(1)} %get-tuple-element.146), channel_id=1, source_target_pairs={{0,4},{1,5},{2,6},{3,7},{4,8},{5,9},{6,10},{7,11},{8,12},{9,13},{1... | collective-permute-start | bytes 786440 | tf_op jit(solution)/shard_map/ppermute | solution.py:324
  122.0 9.3 %collective-permute-start.26 = (bf16[128,1152]{1,0:T(8,128)(2,1)S(1)}, bf16[128,1152]{1,0:T(8,128)(2,1)S(1)}, u32[]{:S(2)}, u32[]{:S(2)}) collective-permute-start(bf16[128,1152]{1,0:T(8,128)(2,1)S(1)} %get-tuple-element.148), channel_id=1, source_target_pairs={{0,4},{1,5},{2,6},{3,7},{4,8},{5,9},{6,10},{7,11},{8,12},{9,13},{1... | collective-permute-start | bytes 884744 | tf_op jit(solution)/shard_map/ppermute | solution.py:324
  127.4 3.9 %copy-start.1 = (s32[128,4]{0,1:T(4,128)S(1)}, s32[128,4]{0,1:T(4,128)}, u32[]{:S(2)}) copy-start(s32[128,4]{0,1:T(4,128)} %param.8) | copy-start | bytes 6148

commit v5 on v4

--- a/solution.py
+++ b/solution.py
@@ -191,22 +191,20 @@
     return queue.run(functools.partial(add_kernel, cut, len(kept)), [*kept, *blocks], outs)
 
 
-def total(own_ref, back_ref, sel_ref, carried_ref, at):
-    end = at + carried_ref.shape[1]
-    return own_ref[:, at:end].astype(F32) + spread(sel_ref, back_ref.at[:, pl.ds(at, end - at)]) + carried_ref[...].astype(F32)
-
-
-def front_kernel(_, own_ref, back_ref, sel_ref, carried_ref, out_ref):
-    out_ref[...] = total(own_ref, back_ref, sel_ref, carried_ref, 0).astype(BF16)
-
-
-def finish_kernel(_, own_ref, back_ref, sel_ref, carried_ref, front_ref, ids_ref, out_ref, gates_ref):
+def front_kernel(_, own_ref, back_ref, sel_ref, carried_ref, out_ref, rest_ref):
+    at = carried_ref.shape[1]
+    settled = own_ref[...].astype(F32) + spread(sel_ref, back_ref)
+    out_ref[...] = (settled[:, :at] + carried_ref[...].astype(F32)).astype(BF16)
+    rest_ref[...] = settled[:, at:]
+
+
+def finish_kernel(_, front_ref, rest_ref, carried_ref, ids_ref, out_ref, gates_ref):
     features = out_ref.shape[1]
     at = front_ref.shape[1]
     out_ref[:, :at] = front_ref[...]
-    rest = total(own_ref, back_ref, sel_ref, carried_ref, at)
-    out_ref[:, at:] = rest[:, : features - at].astype(BF16)
-    gates = rest[:, features - at :].T
+    total = rest_ref[...] + carried_ref[...].astype(F32)
+    out_ref[:, at:] = total[:, : features - at].astype(BF16)
+    gates = total[:, features - at :].T
     expert = lax.broadcasted_iota(jnp.int32, gates.shape, 0)
     chosen = [
         jnp.sum(jnp.where(expert == ids_ref[k : k + 1, :], gates, 0.0), axis=0, keepdims=True)
@@ -217,10 +215,12 @@
 
 def finish(queue, own, back, sel, ids, first, second):
     rows, width = own.shape
-    front = queue.run(front_kernel, [own, back, sel, first], [array(*first.shape)], flops=HOLD[2])
-    return queue.run(
-        finish_kernel, [own, back, sel, second, front, ids],
-        [array(rows, width - LANES), array(*ids.shape)],
+    front, rest = queue.run(
+        front_kernel, [own, back, sel, first],
+        [array(*first.shape), array(*second.shape, dtype=F32)], flops=HOLD[2],
+    )
+    return queue.run(
+        finish_kernel, [front, rest, second, ids], [array(rows, width - LANES), array(*ids.shape)]
     )
 
 
@@ -318,7 +318,9 @@
     near = min(rows, -(-2 * capacity // 16) * 16)
     index = lambda z, y, c: (z * lines + y) * 2 + c
     places = [(z, y, c) for z in range(depth) for y in range(lines) for c in range(2)]
-    up = [(index(z, y, c), index((z + 1) % depth, y, c)) for z, y, c in places]
+    ring = [z for z in range(depth) if z == 0 or z % 2] + [z for z in range(depth - 1, 0, -1) if z % 2 == 0]
+    after = {z: ring[(i + 1) % depth] for i, z in enumerate(ring)}
+    up = [(index(z, y, c), index(after[z], y, c)) for z, y, c in places]
     across = [(index(z, y, c), index(z, 1 - y, c)) for z, y, c in places]
     twin = [(index(z, y, c), index(z, y, 1 - c)) for z, y, c in places]
     move = lambda a, pairs: lax.ppermute(a, "expert", pairs)

time: 133 us -> 132 us (level)
  waiting for transfers between devices: 29.6 us -> 13.5 us
  starting transfers between devices: 28.5 us -> 43.2 us
    ppermute x27, waiting for transfers between devices: 29.6 us -> 13.5 us  [shards(): move = lambda a, pairs: lax.ppermute(a, 'expert', pairs)]
    ppermute x27, starting transfers between devices: 28.5 us -> 43.2 us  [shards(): move = lambda a, pairs: lax.ppermute(a, 'expert', pairs)]
  transfers between devices with their start and end apart: 27 -> 27, of which waited for: 13 -> 11; matrix products, arithmetic and copies ran while one was open for 0% -> 0% of each run, Pallas kernels for 54% -> 55%
where the time goes in v5:
time: 132 us
  Pallas kernels  73.7 us (56%)
  starting transfers between devices  43.2 us (33%)
  waiting for transfers between devices  13.5 us (10%)
    pallas_call x26, Pallas kernels, run(): pl.pallas_call(body, in_specs=[SCALAR] + [ANYWHERE] * anywhere + [LOCAL]...  73.7 us
    ppermute x27, starting transfers between devices, shards(): move = lambda a, pairs: lax.ppermute(a, 'expert', pairs)  43.2 us
    ppermute x27, waiting for transfers between devices, shards(): move = lambda a, pairs: lax.ppermute(a, 'expert', pairs)  13.5 us
  transfers between devices with their start and end apart: 27, of which 11 were waited for; matrix products, arithmetic and copies ran while one was open for 0% of the time, Pallas kernels for 55%

profile of v5, /device:TPU:0, one launch (start us, length us, event | category | flops | bytes accessed | tf_op | source)
XLA Modules:
  0.0 131.8 jit_solution(10852653498985139106)
XLA Ops:
  1.3 2.2 %shard_map.77 = (bf16[128,2176]{1,0:T(8,128)(2,1)S(1)}, bf16[112,2176]{1,0:T(8,128)(2,1)S(1)}, bf16[112,128]{1,0:T(8,128)(2,1)S(1)}, s32[4]{0:T(128)S(1)}) custom-call(s32[4]{0:T(128)S(1)} %pad_add_fusion.ticket_ref, bf16[128,2048]{1,0:T(8,128)(2,1)} %refs_0_.1, s32[4,128]{1,0:T(4,128)} %bitcast.9, bf16[4,128]{1,0:T(4,128)(2,1)} %bitcast.15), custom_call_target="tpu_custom_call" | custom-call | tf_op jit(solution)/shard_map/pallas_call | solution.py:36
  3.6 3.1 %collective-permute-start.2 = (bf16[128,2176]{1,0:T(8,128)(2,1)S(1)}, bf16[128,2176]{1,0:T(8,128)(2,1)S(1)}, u32[]{:S(2)}, u32[]{:S(2)}) collective-permute-start(bf16[128,2176]{1,0:T(8,128)(2,1)S(1)} %get-tuple-element.83.refs_0_.refs_4_), channel_id=1, source_target_pairs={{0,4},{1,5},{2,6},{3,7},{4,12},{5,13},{6,14},{7,15},{8,0},{9,1},{1... | collective-permute-start | bytes 1671176 | tf_op jit(solution)/shard_map/ppermute | solution.py:326
  6.6 1.5 %collective-permute-start.3 = (bf16[112,2176]{1,0:T(8,128)(2,1)S(1)}, bf16[112,2176]{1,0:T(8,128)(2,1)S(1)}, u32[]{:S(2)}, u32[]{:S(2)}) collective-permute-start(bf16[112,2176]{1,0:T(8,128)(2,1)S(1)} %get-tuple-element.85), channel_id=1, source_target_pairs={{0,2},{1,3},{2,0},{3,1},{4,6},{5,7},{6,4},{7,5},{8,10},{9,11},{10,... | collective-permute-start | bytes 1462280 | tf_op jit(solution)/shard_map/ppermute | solution.py:326
  8.1 2.6 %collective-permute-start.4 = (bf16[128,2048]{1,0:T(8,128)(2,1)}, bf16[128,2048]{1,0:T(8,128)(2,1)S(1)}, u32[]{:S(2)}, u32[]{:S(2)}) collective-permute-start(bf16[128,2048]{1,0:T(8,128)(2,1)} %refs_2_.1), channel_id=1, source_target_pairs={{0,4},{1,5},{2,6},{3,7},{4,12},{5,13},{6,14},{7,15},{8,0},{9,1},{1... | collective-permute-start | bytes 1572872 | tf_op jit(solution)/shard_map/ppermute | solution.py:326
  10.7 4.9 %shard_map.78 = (bf16[2048,1536]{1,0:T(8,128)(2,1)S(1)}, bf16[768,2048]{1,0:T(8,128)(2,1)S(1)}, s32[4]{0:T(128)S(1)}) custom-call(s32[4]{0:T(128)S(1)} %get-tuple-element.78.ticket_ref, bf16[2048,1536]{1,0:T(8,128)(2,1)} %bitcast.12, bf16[768,2048]{1,0:T(8,128)(2,1)} %bitcast.14), custom_call_target="tpu_custom_call" | custom-call | tf_op jit(solution)/shard_map/pallas_call | solution.py:36
  18.5 4.9 %shard_map.80 = (bf16[2048,1536]{1,0:T(8,128)(2,1)S(1)}, bf16[768,2048]{1,0:T(8,128)(2,1)S(1)}, s32[4]{0:T(128)S(1)}) custom-call(s32[4]{0:T(128)S(1)} %get-tuple-element.81.ticket_ref, bf16[2048,1536]{1,0:T(8,128)(2,1)} %collective-permute-done.refs_0_, bf16[768,2048]{1,0:T(8,128)(2,1)} %copy-done.2), custom_call_target="tpu_custom_call" | custom-call | tf_op jit(solution)/shard_map/pallas_call | solution.py:36
  23.4 1.4 %shard_map.81 = (bf16[112,2176]{1,0:T(8,128)(2,1)S(1)}, bf16[112,128]{1,0:T(8,128)(2,1)S(1)}, bf16[128,2176]{1,0:T(8,128)(2,1)S(1)}, s32[4]{0:T(128)S(1)}) custom-call(s32[4]{0:T(128)S(1)} %get-tuple-element.82.ticket_ref, bf16[128,2176]{1,0:T(8,128)(2,1)S(1)} %collective-permute-done.2.refs_0_), custom_call_target="tpu_custom_call" | custom-call | tf_op jit(solution)/shard_map/pallas_call | solution.py:36
  24.8 1.5 %collective-permute-start.6 = (bf16[128,2176]{1,0:T(8,128)(2,1)S(1)}, bf16[128,2176]{1,0:T(8,128)(2,1)S(1)}, u32[]{:S(2)}, u32[]{:S(2)}) collective-permute-start(bf16[128,2176]{1,0:T(8,128)(2,1)S(1)} %get-tuple-element.97.refs_0_.refs_4_), channel_id=1, source_target_pairs={{0,4},{1,5},{2,6},{3,7},{4,12},{5,13},{6,14},{7,15},{8,0},{9,1},{1... | collective-permute-start | bytes 1671176 | tf_op jit(solution)/shard_map/ppermute | solution.py:326
  26.4 1.5 %collective-permute-start.7 = (bf16[112,2176]{1,0:T(8,128)(2,1)S(1)}, bf16[112,2176]{1,0:T(8,128)(2,1)S(1)}, u32[]{:S(2)}, u32[]{:S(2)}) collective-permute-start(bf16[112,2176]{1,0:T(8,128)(2,1)S(1)} %get-tuple-element.99), channel_id=1, source_target_pairs={{0,2},{1,3},{2,0},{3,1},{4,6},{5,7},{6,4},{7,5},{8,10},{9,11},{10,... | collective-permute-start | bytes 1462280 | tf_op jit(solution)/shard_map/ppermute | solution.py:326
  27.9 4.1 %shard_map.82 = (f32[240,1536]{1,0:T(8,128)S(1)}, f32[240,1536]{1,0:T(8,128)S(1)}, s32[4]{0:T(128)S(1)}) custom-call(s32[4]{0:T(128)S(1)} %get-tuple-element.84.ticket_ref, bf16[128,2176]{1,0:T(8,128)(2,1)S(1)} %get-tuple-element.83.refs_0_.refs_4_, bf16[112,2176]{1,0:T(8,128)(2,1)S(1)} %collective-permute-done.3.refs_1_.refs_5_, ...), custom_call_target="tpu_custom_call" | custom-call | flops 905969664 | tf_op jit(solution)/shard_map/pallas_call | solution.py:36
  33.4 2.0 %collective-permute-start.8 = (bf16[112,2048]{1,0:T(8,128)(2,1)S(1)}, bf16[112,2048]{1,0:T(8,128)(2,1)S(1)}, u32[]{:S(2)}, u32[]{:S(2)}) collective-permute-start(bf16[112,2048]{1,0:T(8,128)(2,1)S(1)} %get-tuple-element.104), channel_id=1, source_target_pairs={{0,2},{1,3},{2,0},{3,1},{4,6},{5,7},{6,4},{7,5},{8,10},{9,11},{10,... | collective-permute-start | bytes 1376264 | tf_op jit(solution)/shard_map/ppermute | solution.py:326
  36.3 6.6 %shard_map.84 = (bf16[128,2176]{1,0:T(8,128)(2,1)S(1)}, bf16[112,2176]{1,0:T(8,128)(2,1)S(1)}, s32[4]{0:T(128)S(1)}) custom-call(s32[4]{0:T(128)S(1)} %get-tuple-element.90.ticket_ref, f32[240,1536]{1,0:T(8,128)S(1)} %get-tuple-element.91.refs_0_, f32[240,1536]{1,0:T(8,128)S(1)} %get-tuple-element.92.refs_1_, bf16[128,2048]{1,0:T(8,128)(2,1)S(1)} %copy-done, ...), custom_call_target="tpu_custom_call" | custom-call | flops 1358954496 | tf_op jit(solution)/shard_map/pallas_call | solution.py:36
  45.7 2.0 %collective-permute-start.10 = (bf16[112,2176]{1,0:T(8,128)(2,1)S(1)}, bf16[112,2176]{1,0:T(8,128)(2,1)S(1)}, u32[]{:S(2)}, u32[]{:S(2)}) collective-permute-start(bf16[112,2176]{1,0:T(8,128)(2,1)S(1)} %get-tuple-element.109), channel_id=1, source_target_pairs={{0,2},{1,3},{2,0},{3,1},{4,6},{5,7},{6,4},{7,5},{8,10},{9,11},{10,... | collective-permute-start | bytes 1462280 | tf_op jit(solution)/shard_map/ppermute | solution.py:326
  48.4 4.1 %shard_map.86 = (f32[240,1536]{1,0:T(8,128)S(1)}, f32[240,1536]{1,0:T(8,128)S(1)}, s32[4]{0:T(128)S(1)}) custom-call(s32[4]{0:T(128)S(1)} %get-tuple-element.98.ticket_ref, bf16[128,2176]{1,0:T(8,128)(2,1)S(1)} %get-tuple-element.97.refs_0_.refs_4_, bf16[112,2176]{1,0:T(8,128)(2,1)S(1)} %collective-permute-done.7.refs_1_.refs_5_, ...), custom_call_target="tpu_custom_call" | custom-call | flops 905969664 | tf_op jit(solution)/shard_map/pallas_call | solution.py:36
  52.6 6.6 %shard_map.87 = (bf16[128,2176]{1,0:T(8,128)(2,1)S(1)}, bf16[112,2176]{1,0:T(8,128)(2,1)S(1)}, s32[4]{0:T(128)S(1)}) custom-call(s32[4]{0:T(128)S(1)} %get-tuple-element.100.ticket_ref, f32[240,1536]{1,0:T(8,128)S(1)} %get-tuple-element.101.refs_0_, f32[240,1536]{1,0:T(8,128)S(1)} %get-tuple-element.102.refs_1_, ...), custom_call_target="tpu_custom_call" | custom-call | flops 1358954496 | tf_op jit(solution)/shard_map/pallas_call | solution.py:36
  61.8 2.6 %collective-permute-start.13 = (bf16[128,2048]{1,0:T(8,128)(2,1)S(1)}, bf16[128,2048]{1,0:T(8,128)(2,1)S(1)}, u32[]{:S(2)}, u32[]{:S(2)}) collective-permute-start(bf16[128,2048]{1,0:T(8,128)(2,1)S(1)} %get-tuple-element.116.refs_2_), channel_id=1, source_target_pairs={{0,4},{1,5},{2,6},{3,7},{4,12},{5,13},{6,14},{7,15},{8,0},{9,1},{1... | collective-permute-start | bytes 1572872 | tf_op jit(solution)/shard_map/ppermute | solution.py:326
  64.3 4.1 %shard_map.89 = (f32[240,1536]{1,0:T(8,128)S(1)}, f32[240,1536]{1,0:T(8,128)S(1)}, s32[4]{0:T(128)S(1)}) custom-call(s32[4]{0:T(128)S(1)} %get-tuple-element.107.ticket_ref, bf16[128,2176]{1,0:T(8,128)(2,1)S(1)} %get-tuple-element.108.refs_0_.refs_4_, bf16[112,2176]{1,0:T(8,128)(2,1)S(1)} %collective-permute-done.10.refs_1_.refs_5_, ...), custom_call_target="tpu_custom_call" | custom-call | flops 905969664 | tf_op jit(solution)/shard_map/pallas_call | solution.py:36
  69.9 1.6 %collective-permute-start.14 = (bf16[112,2176]{1,0:T(8,128)(2,1)S(1)}, bf16[112,2176]{1,0:T(8,128)(2,1)S(1)}, u32[]{:S(2)}, u32[]{:S(2)}) collective-permute-start(bf16[112,2176]{1,0:T(8,128)(2,1)S(1)} %get-tuple-element.121), channel_id=1, source_target_pairs={{0,2},{1,3},{2,0},{3,1},{4,6},{5,7},{6,4},{7,5},{8,10},{9,11},{10,... | collective-permute-start | bytes 1462280 | tf_op jit(solution)/shard_map/ppermute | solution.py:326
  73.0 6.6 %shard_map.92 = (bf16[128,2176]{1,0:T(8,128)(2,1)S(1)}, bf16[112,2176]{1,0:T(8,128)(2,1)S(1)}, s32[4]{0:T(128)S(1)}) custom-call(s32[4]{0:T(128)S(1)} %get-tuple-element.113.ticket_ref, f32[240,1536]{1,0:T(8,128)S(1)} %get-tuple-element.114.refs_0_, f32[240,1536]{1,0:T(8,128)S(1)} %get-tuple-element.115.refs_1_, ...), custom_call_target="tpu_custom_call" | custom-call | flops 1358954496 | tf_op jit(solution)/shard_map/pallas_call | solution.py:36
  81.7 4.2 %shard_map.94 = (f32[240,1536]{1,0:T(8,128)S(1)}, f32[240,1536]{1,0:T(8,128)S(1)}, bf16[128,2176]{1,0:T(8,128)(2,1)S(1)}, s32[4]{0:T(128)S(1)}) custom-call(s32[4]{0:T(128)S(1)} %get-tuple-element.120.ticket_ref, bf16[128,2176]{1,0:T(8,128)(2,1)S(1)} %collective-permute-done.11.refs_0_.refs_4_, ...), custom_call_target="tpu_custom_call" | custom-call | flops 905969664 | tf_op jit(solution)/shard_map/pallas_call | solution.py:36
  85.9 3.2 %collective-permute-start.18 = (bf16[128,2176]{1,0:T(8,128)(2,1)S(1)}, bf16[128,2176]{1,0:T(8,128)(2,1)S(1)}, u32[]{:S(2)}, u32[]{:S(2)}) collective-permute-start(bf16[128,2176]{1,0:T(8,128)(2,1)S(1)} %get-tuple-element.133), channel_id=1, source_target_pairs={{0,4},{1,5},{2,6},{3,7},{4,12},{5,13},{6,14},{7,15},{8,0},{9,1},{1... | collective-permute-start | bytes 1671176 | tf_op jit(solution)/shard_map/ppermute | solution.py:326
  91.9 2.0 %collective-permute-start.17 = (bf16[128,1024]{1,0:T(8,128)(2,1)S(1)}, bf16[128,1024]{1,0:T(8,128)(2,1)S(1)}, u32[]{:S(2)}, u32[]{:S(2)}) collective-permute-start(bf16[128,1024]{1,0:T(8,128)(2,1)S(1)} %get-tuple-element.132), channel_id=1, source_target_pairs={{0,2},{1,3},{2,0},{3,1},{4,6},{5,7},{6,4},{7,5},{8,10},{9,11},{10,... | collective-permute-start | bytes 786440 | tf_op jit(solution)/shard_map/ppermute | solution.py:326
  94.0 6.7 %shard_map.96 = (bf16[128,2176]{1,0:T(8,128)(2,1)S(1)}, bf16[112,1024]{1,0:T(8,128)(2,1)S(1)}, bf16[112,1152]{1,0:T(8,128)(2,1)S(1)}, s32[4]{0:T(128)S(1)}) custom-call(s32[4]{0:T(128)S(1)} %get-tuple-element.126.ticket_ref, f32[240,1536]{1,0:T(8,128)S(1)} %get-tuple-element.127.refs_0_, f32[240,1536]{1,0:T(8,128)S(1)} %get-tuple-element.128.refs_1_, ...), custom_call_target="tpu_custom_call" | custom-call | flops 1358954496 | tf_op jit(solution)/shard_map/pallas_call | solution.py:36
  104.0 1.5 %collective-permute-start.20 = (bf16[112,1024]{1,0:T(8,128)(2,1)S(1)}, bf16[112,1024]{1,0:T(8,128)(2,1)S(1)}, u32[]{:S(2)}, u32[]{:S(2)}) collective-permute-start(bf16[112,1024]{1,0:T(8,128)(2,1)S(1)} %get-tuple-element.139), channel_id=1, source_target_pairs={{0,2},{1,3},{2,0},{3,1},{4,6},{5,7},{6,4},{7,5},{8,10},{9,11},{10,... | collective-permute-start | bytes 688136 | tf_op jit(solution)/shard_map/ppermute | solution.py:326
  107.2 1.6 %collective-permute-start.24 = (bf16[112,2176]{1,0:T(8,128)(2,1)S(1)}, bf16[112,2176]{1,0:T(8,128)(2,1)S(1)}, u32[]{:S(2)}, u32[]{:S(2)}) collective-permute-start(bf16[112,2176]{1,0:T(8,128)(2,1)S(1)} %get-tuple-element.146), channel_id=1, source_target_pairs={{0,2},{1,3},{2,0},{3,1},{4,6},{5,7},{6,4},{7,5},{8,10},{9,11},{10,... | collective-permute-start | bytes 1462280 | tf_op jit(solution)/shard_map/ppermute | solution.py:326
  108.8 3.4 %collective-permute-start.23 = (bf16[128,1152]{1,0:T(8,128)(2,1)S(1)}, bf16[128,1152]{1,0:T(8,128)(2,1)S(1)}, u32[]{:S(2)}, u32[]{:S(2)}) collective-permute-start(bf16[128,1152]{1,0:T(8,128)(2,1)S(1)} %get-tuple-element.143), channel_id=1, source_target_pairs={{0,4},{1,5},{2,6},{3,7},{4,12},{5,13},{6,14},{7,15},{8,0},{9,1},{1... | collective-permute-start | bytes 884744 | tf_op jit(solution)/shard_map/ppermute | solution.py:326
  114.3 2.8 %collective-permute-start.25 = (bf16[128,1024]{1,0:T(8,128)(2,1)S(1)}, bf16[128,1024]{1,0:T(8,128)(2,1)S(1)}, u32[]{:S(2)}, u32[]{:S(2)}) collective-permute-start(bf16[128,1024]{1,0:T(8,128)(2,1)S(1)} %get-tuple-element.147), channel_id=1, source_target_pairs={{0,4},{1,5},{2,6},{3,7},{4,12},{5,13},{6,14},{7,15},{8,0},{9,1},{1... | collective-permute-start | bytes 786440 | tf_op jit(solution)/shard_map/ppermute | solution.py:326
  118.1 1.6 %collective-permute-done.23.refs_3_ = bf16[128,1152]{1,0:T(8,128)(2,1)S(1)} collective-permute-done((bf16[128,1152]{1,0:T(8,128)(2,1)S(1)}, bf16[128,1152]{1,0:T(8,128)(2,1)S(1)}, u32[]{:S(2)}, u32[]{:S(2)}) %collective-permute-start.23) | collective-permute-done | bytes 294944 | tf_op jit(solution)/shard_map/ppermute | solution.py:326
  120.8 2.5 %collective-permute-start.26 = (bf16[128,1152]{1,0:T(8,128)(2,1)S(1)}, bf16[128,1152]{1,0:T(8,128)(2,1)S(1)}, u32[]{:S(2)}, u32[]{:S(2)}) collective-permute-start(bf16[128,1152]{1,0:T(8,128)(2,1)S(1)} %get-tuple-element.151), channel_id=1, source_target_pairs={{0,4},{1,5},{2,6},{3,7},{4,12},{5,13},{6,14},{7,15},{8,0},{9,1},{1... | collective-permute-start | bytes 884744 | tf_op jit(solution)/shard_map/ppermute | solution.py:326
  123.3 3.1 %collective-permute-done.24.refs_1_ = bf16[112,2176]{1,0:T(8,128)(2,1)S(1)} collective-permute-done((bf16[112,2176]{1,0:T(8,128)(2,1)S(1)}, bf16[112,2176]{1,0:T(8,128)(2,1)S(1)}, u32[]{:S(2)}, u32[]{:S(2)}) %collective-permute-start.24) | collective-permute-done | bytes 487456 | tf_op jit(solution)/shard_map/ppermute | solution.py:326
  127.6 2.5 %collective-permute-done.26.refs_2_ = bf16[128,1152]{1,0:T(8,128)(2,1)S(1)} collective-permute-done((bf16[128,1152]{1,0:T(8,128)(2,1)S(1)}, bf16[128,1152]{1,0:T(8,128)(2,1)S(1)}, u32[]{:S(2)}, u32[]{:S(2)}) %collective-permute-start.26) | collective-permute-done | bytes 294944 | tf_op jit(solution)/shard_map/ppermute | solution.py:326
  130.1 1.5 %shard_map.102 = (bf16[128,2048]{1,0:T(8,128)(2,1)}, bf16[4,128]{1,0:T(4,128)(2,1)}, s32[4]{0:T(128)}) custom-call(s32[4]{0:T(128)S(1)} %get-tuple-element.148.ticket_ref, bf16[128,1024]{1,0:T(8,128)(2,1)S(1)} %get-tuple-element.149.refs_0_, f32[128,1152]{1,0:T(8,128)S(1)} %get-tuple-element.150.refs_1_, ...), custom_call_target="tpu_custom_call" | custom-call | tf_op jit(solution)/shard_map/pallas_call | solution.py:36
  (55 shorter events, 30.3 us)
Async XLA Ops:
  0.6 17.6 %collective-permute-start = (bf16[2048,1536]{1,0:T(8,128)(2,1)}, bf16[2048,1536]{1,0:T(8,128)(2,1)}, u32[]{:S(2)}, u32[]{:S(2)}) collective-permute-start(bf16[2048,1536]{1,0:T(8,128)(2,1)} %bitcast.11), channel_id=1, source_target_pairs={{0,1},{1,0},{2,3},{3,2},{4,5},{5,4},{6,7},{7,6},{8,9},{9,8},{10,11... | collective-permute-start | bytes 18874376 | tf_op jit(solution)/shard_map/ppermute | solution.py:326
  1.1 15.6 %collective-permute-start.1 = (bf16[768,2048]{1,0:T(8,128)(2,1)}, bf16[768,2048]{1,0:T(8,128)(2,1)S(1)}, u32[]{:S(2)}, u32[]{:S(2)}) collective-permute-start(bf16[768,2048]{1,0:T(8,128)(2,1)} %bitcast.13), channel_id=1, source_target_pairs={{0,1},{1,0},{2,3},{3,2},{4,5},{5,4},{6,7},{7,6},{8,9},{9,8},{10,11... | collective-permute-start | bytes 9437192 | tf_op jit(solution)/shard_map/ppermute | solution.py:326
  3.6 19.8 %collective-permute-start.2 = (bf16[128,2176]{1,0:T(8,128)(2,1)S(1)}, bf16[128,2176]{1,0:T(8,128)(2,1)S(1)}, u32[]{:S(2)}, u32[]{:S(2)}) collective-permute-start(bf16[128,2176]{1,0:T(8,128)(2,1)S(1)} %get-tuple-element.83.refs_0_.refs_4_), channel_id=1, source_target_pairs={{0,4},{1,5},{2,6},{3,7},{4,12},{5,13},{6,14},{7,15},{8,0},{9,1},{1... | collective-permute-start | bytes 1671176 | tf_op jit(solution)/shard_map/ppermute | solution.py:326
  6.6 21.3 %collective-permute-start.3 = (bf16[112,2176]{1,0:T(8,128)(2,1)S(1)}, bf16[112,2176]{1,0:T(8,128)(2,1)S(1)}, u32[]{:S(2)}, u32[]{:S(2)}) collective-permute-start(bf16[112,2176]{1,0:T(8,128)(2,1)S(1)} %get-tuple-element.85), channel_id=1, source_target_pairs={{0,2},{1,3},{2,0},{3,1},{4,6},{5,7},{6,4},{7,5},{8,10},{9,11},{10,... | collective-permute-start | bytes 1462280 | tf_op jit(solution)/shard_map/ppermute | solution.py:326
  8.1 24.1 %collective-permute-start.4 = (bf16[128,2048]{1,0:T(8,128)(2,1)}, bf16[128,2048]{1,0:T(8,128)(2,1)S(1)}, u32[]{:S(2)}, u32[]{:S(2)}) collective-permute-start(bf16[128,2048]{1,0:T(8,128)(2,1)} %refs_2_.1), channel_id=1, source_target_pairs={{0,4},{1,5},{2,6},{3,7},{4,12},{5,13},{6,14},{7,15},{8,0},{9,1},{1... | collective-permute-start | bytes 1572872 | tf_op jit(solution)/shard_map/ppermute | solution.py:326
  10.7 4.9 %copy-start = (bf16[128,2048]{1,0:T(8,128)(2,1)S(1)}, bf16[128,2048]{1,0:T(8,128)(2,1)}, u32[]{:S(2)}) copy-start(bf16[128,2048]{1,0:T(8,128)(2,1)} %refs_2_.1) | copy-start | bytes 1572868
  16.8 1.7 %copy-start.2 = (bf16[768,2048]{1,0:T(8,128)(2,1)}, bf16[768,2048]{1,0:T(8,128)(2,1)S(1)}, u32[]{:S(2)}) copy-start(bf16[768,2048]{1,0:T(8,128)(2,1)S(1)} %collective-permute-done.1.refs_1_) | copy-start | bytes 9437188
  16.8 19.5 %collective-permute-start.5 = (bf16[112,2048]{1,0:T(8,128)(2,1)S(1)}, bf16[112,2048]{1,0:T(8,128)(2,1)S(1)}, u32[]{:S(2)}, u32[]{:S(2)}) collective-permute-start(bf16[112,2048]{1,0:T(8,128)(2,1)S(1)} %get-tuple-element.93), channel_id=1, source_target_pairs={{0,2},{1,3},{2,0},{3,1},{4,6},{5,7},{6,4},{7,5},{8,10},{9,11},{10,... | collective-permute-start | bytes 1376264 | tf_op jit(solution)/shard_map/ppermute | solution.py:326
  24.8 19.4 %collective-permute-start.6 = (bf16[128,2176]{1,0:T(8,128)(2,1)S(1)}, bf16[128,2176]{1,0:T(8,128)(2,1)S(1)}, u32[]{:S(2)}, u32[]{:S(2)}) collective-permute-start(bf16[128,2176]{1,0:T(8,128)(2,1)S(1)} %get-tuple-element.97.refs_0_.refs_4_), channel_id=1, source_target_pairs={{0,4},{1,5},{2,6},{3,7},{4,12},{5,13},{6,14},{7,15},{8,0},{9,1},{1... | collective-permute-start | bytes 1671176 | tf_op jit(solution)/shard_map/ppermute | solution.py:326
  26.4 22.1 %collective-permute-start.7 = (bf16[112,2176]{1,0:T(8,128)(2,1)S(1)}, bf16[112,2176]{1,0:T(8,128)(2,1)S(1)}, u32[]{:S(2)}, u32[]{:S(2)}) collective-permute-start(bf16[112,2176]{1,0:T(8,128)(2,1)S(1)} %get-tuple-element.99), channel_id=1, source_target_pairs={{0,2},{1,3},{2,0},{3,1},{4,6},{5,7},{6,4},{7,5},{8,10},{9,11},{10,... | collective-permute-start | bytes 1462280 | tf_op jit(solution)/shard_map/ppermute | solution.py:326
  33.4 19.1 %collective-permute-start.8 = (bf16[112,2048]{1,0:T(8,128)(2,1)S(1)}, bf16[112,2048]{1,0:T(8,128)(2,1)S(1)}, u32[]{:S(2)}, u32[]{:S(2)}) collective-permute-start(bf16[112,2048]{1,0:T(8,128)(2,1)S(1)} %get-tuple-element.104), channel_id=1, source_target_pairs={{0,2},{1,3},{2,0},{3,1},{4,6},{5,7},{6,4},{7,5},{8,10},{9,11},{10,... | collective-permute-start | bytes 1376264 | tf_op jit(solution)/shard_map/ppermute | solution.py:326
  35.4 23.8 %collective-permute-start.9 = (bf16[128,2048]{1,0:T(8,128)(2,1)S(1)}, bf16[128,2048]{1,0:T(8,128)(2,1)S(1)}, u32[]{:S(2)}, u32[]{:S(2)}) collective-permute-start(bf16[128,2048]{1,0:T(8,128)(2,1)S(1)} %get-tuple-element.103.refs_2_), channel_id=1, source_target_pairs={{0,4},{1,5},{2,6},{3,7},{4,12},{5,13},{6,14},{7,15},{8,0},{9,1},{1... | collective-permute-start | bytes 1572872 | tf_op jit(solution)/shard_map/ppermute | solution.py:326
  45.7 18.7 %collective-permute-start.10 = (bf16[112,2176]{1,0:T(8,128)(2,1)S(1)}, bf16[112,2176]{1,0:T(8,128)(2,1)S(1)}, u32[]{:S(2)}, u32[]{:S(2)}) collective-permute-start(bf16[112,2176]{1,0:T(8,128)(2,1)S(1)} %get-tuple-element.109), channel_id=1, source_target_pairs={{0,2},{1,3},{2,0},{3,1},{4,6},{5,7},{6,4},{7,5},{8,10},{9,11},{10,... | collective-permute-start | bytes 1462280 | tf_op jit(solution)/shard_map/ppermute | solution.py:326
  47.6 20.8 %collective-permute-start.11 = (bf16[128,2176]{1,0:T(8,128)(2,1)S(1)}, bf16[128,2176]{1,0:T(8,128)(2,1)S(1)}, u32[]{:S(2)}, u32[]{:S(2)}) collective-permute-start(bf16[128,2176]{1,0:T(8,128)(2,1)S(1)} %get-tuple-element.108.refs_0_.refs_4_), channel_id=1, source_target_pairs={{0,4},{1,5},{2,6},{3,7},{4,12},{5,13},{6,14},{7,15},{8,0},{9,1},{1... | collective-permute-start | bytes 1671176 | tf_op jit(solution)/shard_map/ppermute | solution.py:326
  60.4 12.6 %collective-permute-start.12 = (bf16[112,2048]{1,0:T(8,128)(2,1)S(1)}, bf16[112,2048]{1,0:T(8,128)(2,1)S(1)}, u32[]{:S(2)}, u32[]{:S(2)}) collective-permute-start(bf16[112,2048]{1,0:T(8,128)(2,1)S(1)} %get-tuple-element.117), channel_id=1, source_target_pairs={{0,2},{1,3},{2,0},{3,1},{4,6},{5,7},{6,4},{7,5},{8,10},{9,11},{10,... | collective-permute-start | bytes 1376264 | tf_op jit(solution)/shard_map/ppermute | solution.py:326
  61.8 17.8 %collective-permute-start.13 = (bf16[128,2048]{1,0:T(8,128)(2,1)S(1)}, bf16[128,2048]{1,0:T(8,128)(2,1)S(1)}, u32[]{:S(2)}, u32[]{:S(2)}) collective-permute-start(bf16[128,2048]{1,0:T(8,128)(2,1)S(1)} %get-tuple-element.116.refs_2_), channel_id=1, source_target_pairs={{0,4},{1,5},{2,6},{3,7},{4,12},{5,13},{6,14},{7,15},{8,0},{9,1},{1... | collective-permute-start | bytes 1572872 | tf_op jit(solution)/shard_map/ppermute | solution.py:326
  69.9 11.8 %collective-permute-start.14 = (bf16[112,2176]{1,0:T(8,128)(2,1)S(1)}, bf16[112,2176]{1,0:T(8,128)(2,1)S(1)}, u32[]{:S(2)}, u32[]{:S(2)}) collective-permute-start(bf16[112,2176]{1,0:T(8,128)(2,1)S(1)} %get-tuple-element.121), channel_id=1, source_target_pairs={{0,2},{1,3},{2,0},{3,1},{4,6},{5,7},{6,4},{7,5},{8,10},{9,11},{10,... | collective-permute-start | bytes 1462280 | tf_op jit(solution)/shard_map/ppermute | solution.py:326
  72.6 17.9 %collective-permute-start.15 = (bf16[128,2176]{1,0:T(8,128)(2,1)S(1)}, bf16[128,2176]{1,0:T(8,128)(2,1)S(1)}, u32[]{:S(2)}, u32[]{:S(2)}) collective-permute-start(bf16[128,2176]{1,0:T(8,128)(2,1)S(1)} %get-tuple-element.125), channel_id=1, source_target_pairs={{0,4},{1,5},{2,6},{3,7},{4,12},{5,13},{6,14},{7,15},{8,0},{9,1},{1... | collective-permute-start | bytes 1671176 | tf_op jit(solution)/shard_map/ppermute | solution.py:326
  80.7 13.3 %collective-permute-start.16 = (bf16[112,2048]{1,0:T(8,128)(2,1)S(1)}, bf16[112,2048]{1,0:T(8,128)(2,1)S(1)}, u32[]{:S(2)}, u32[]{:S(2)}) collective-permute-start(bf16[112,2048]{1,0:T(8,128)(2,1)S(1)} %get-tuple-element.129), channel_id=1, source_target_pairs={{0,2},{1,3},{2,0},{3,1},{4,6},{5,7},{6,4},{7,5},{8,10},{9,11},{10,... | collective-permute-start | bytes 1376264 | tf_op jit(solution)/shard_map/ppermute | solution.py:326
  85.9 16.0 %collective-permute-start.18 = (bf16[128,2176]{1,0:T(8,128)(2,1)S(1)}, bf16[128,2176]{1,0:T(8,128)(2,1)S(1)}, u32[]{:S(2)}, u32[]{:S(2)}) collective-permute-start(bf16[128,2176]{1,0:T(8,128)(2,1)S(1)} %get-tuple-element.133), channel_id=1, source_target_pairs={{0,4},{1,5},{2,6},{3,7},{4,12},{5,13},{6,14},{7,15},{8,0},{9,1},{1... | collective-permute-start | bytes 1671176 | tf_op jit(solution)/shard_map/ppermute | solution.py:326
  91.9 9.3 %collective-permute-start.17 = (bf16[128,1024]{1,0:T(8,128)(2,1)S(1)}, bf16[128,1024]{1,0:T(8,128)(2,1)S(1)}, u32[]{:S(2)}, u32[]{:S(2)}) collective-permute-start(bf16[128,1024]{1,0:T(8,128)(2,1)S(1)} %get-tuple-element.132), channel_id=1, source_target_pairs={{0,2},{1,3},{2,0},{3,1},{4,6},{5,7},{6,4},{7,5},{8,10},{9,11},{10,... | collective-permute-start | bytes 786440 | tf_op jit(solution)/shard_map/ppermute | solution.py:326
  93.9 12.2 %collective-permute-start.19 = (bf16[128,1152]{1,0:T(8,128)(2,1)S(1)}, bf16[128,1152]{1,0:T(8,128)(2,1)S(1)}, u32[]{:S(2)}, u32[]{:S(2)}) collective-permute-start(bf16[128,1152]{1,0:T(8,128)(2,1)S(1)} %get-tuple-element.136), channel_id=1, source_target_pairs={{0,2},{1,3},{2,0},{3,1},{4,6},{5,7},{6,4},{7,5},{8,10},{9,11},{10,... | collective-permute-start | bytes 884744 | tf_op jit(solution)/shard_map/ppermute | solution.py:326
  103.1 10.1 %collective-permute-start.21 = (bf16[128,1024]{1,0:T(8,128)(2,1)S(1)}, bf16[128,1024]{1,0:T(8,128)(2,1)S(1)}, u32[]{:S(2)}, u32[]{:S(2)}) collective-permute-start(bf16[128,1024]{1,0:T(8,128)(2,1)S(1)} %get-tuple-element.140), channel_id=1, source_target_pairs={{0,4},{1,5},{2,6},{3,7},{4,12},{5,13},{6,14},{7,15},{8,0},{9,1},{1... | collective-permute-start | bytes 786440 | tf_op jit(solution)/shard_map/ppermute | solution.py:326
  104.0 8.5 %collective-permute-start.20 = (bf16[112,1024]{1,0:T(8,128)(2,1)S(1)}, bf16[112,1024]{1,0:T(8,128)(2,1)S(1)}, u32[]{:S(2)}, u32[]{:S(2)}) collective-permute-start(bf16[112,1024]{1,0:T(8,128)(2,1)S(1)} %get-tuple-element.139), channel_id=1, source_target_pairs={{0,2},{1,3},{2,0},{3,1},{4,6},{5,7},{6,4},{7,5},{8,10},{9,11},{10,... | collective-permute-start | bytes 688136 | tf_op jit(solution)/shard_map/ppermute | solution.py:326
  105.5 12.6 %collective-permute-start.22 = (bf16[112,1152]{1,0:T(8,128)(2,1)S(1)}, bf16[112,1152]{1,0:T(8,128)(2,1)S(1)}, u32[]{:S(2)}, u32[]{:S(2)}) collective-permute-start(bf16[112,1152]{1,0:T(8,128)(2,1)S(1)} %get-tuple-element.142), channel_id=1, source_target_pairs={{0,2},{1,3},{2,0},{3,1},{4,6},{5,7},{6,4},{7,5},{8,10},{9,11},{10,... | collective-permute-start | bytes 774152 | tf_op jit(solution)/shard_map/ppermute | solution.py:326
  107.2 19.2 %collective-permute-start.24 = (bf16[112,2176]{1,0:T(8,128)(2,1)S(1)}, bf16[112,2176]{1,0:T(8,128)(2,1)S(1)}, u32[]{:S(2)}, u32[]{:S(2)}) collective-permute-start(bf16[112,2176]{1,0:T(8,128)(2,1)S(1)} %get-tuple-element.146), channel_id=1, source_target_pairs={{0,2},{1,3},{2,0},{3,1},{4,6},{5,7},{6,4},{7,5},{8,10},{9,11},{10,... | collective-permute-start | bytes 1462280 | tf_op jit(solution)/shard_map/ppermute | solution.py:326
  108.8 10.8 %collective-permute-start.23 = (bf16[128,1152]{1,0:T(8,128)(2,1)S(1)}, bf16[128,1152]{1,0:T(8,128)(2,1)S(1)}, u32[]{:S(2)}, u32[]{:S(2)}) collective-permute-start(bf16[128,1152]{1,0:T(8,128)(2,1)S(1)} %get-tuple-element.143), channel_id=1, source_target_pairs={{0,4},{1,5},{2,6},{3,7},{4,12},{5,13},{6,14},{7,15},{8,0},{9,1},{1... | collective-permute-start | bytes 884744 | tf_op jit(solution)/shard_map/ppermute | solution.py:326
  114.3 12.1 %collective-permute-start.25 = (bf16[128,1024]{1,0:T(8,128)(2,1)S(1)}, bf16[128,1024]{1,0:T(8,128)(2,1)S(1)}, u32[]{:S(2)}, u32[]{:S(2)}) collective-permute-start(bf16[128,1024]{1,0:T(8,128)(2,1)S(1)} %get-tuple-element.147), channel_id=1, source_target_pairs={{0,4},{1,5},{2,6},{3,7},{4,12},{5,13},{6,14},{7,15},{8,0},{9,1},{1... | collective-permute-start | bytes 786440 | tf_op jit(solution)/shard_map/ppermute | solution.py:326
  120.8 9.3 %collective-permute-start.26 = (bf16[128,1152]{1,0:T(8,128)(2,1)S(1)}, bf16[128,1152]{1,0:T(8,128)(2,1)S(1)}, u32[]{:S(2)}, u32[]{:S(2)}) collective-permute-start(bf16[128,1152]{1,0:T(8,128)(2,1)S(1)} %get-tuple-element.151), channel_id=1, source_target_pairs={{0,4},{1,5},{2,6},{3,7},{4,12},{5,13},{6,14},{7,15},{8,0},{9,1},{1... | collective-permute-start | bytes 884744 | tf_op jit(solution)/shard_map/ppermute | solution.py:326
  126.4 3.6 %copy-start.1 = (s32[128,4]{0,1:T(4,128)S(1)}, s32[128,4]{0,1:T(4,128)}, u32[]{:S(2)}) copy-start(s32[128,4]{0,1:T(4,128)} %param.8) | copy-start | bytes 6148

commit v6 on v5

--- a/solution.py
+++ b/solution.py
@@ -144,22 +144,20 @@
     )
 
 
-def place_kernel(cuts, _, far_ref, tok_ref, *refs):
-    near, width = far_ref.shape
+def place_kernel(cuts, _, *refs):
     rows = refs[-1].shape[0]
-    row = tok_ref[:, width - 1 :].astype(F32).astype(jnp.int32)
-    sel = jnp.where(lax.broadcasted_iota(jnp.int32, (near, rows), 1) == row, 1.0, 0.0).astype(BF16)
-    total = lax.dot_general(sel, far_ref[...], (((0,), (0,)), ((), ())), preferred_element_type=F32)
+    total = 0.0
     for ref in refs[: -len(cuts)]:
-        total += ref[...].astype(F32)
+        near, width = ref.shape
+        row = ref[:, width - 1 :].astype(F32).astype(jnp.int32)
+        sel = jnp.where(lax.broadcasted_iota(jnp.int32, (near, rows), 1) == row, 1.0, 0.0).astype(BF16)
+        total += lax.dot_general(sel, ref[...], (((0,), (0,)), ((), ())), preferred_element_type=F32)
     for (at, end), ref in zip(cuts, refs[-len(cuts) :]):
         ref[...] = total[:, at:end].astype(BF16)
 
 
-def place(queue, far, tok, rows, *carried, cuts=None):
-    cuts = cuts or [(0, far.shape[1])]
-    outs = [array(rows, end - at) for at, end in cuts]
-    return queue.run(functools.partial(place_kernel, cuts), [far, tok, *carried], outs)
+def place(queue, rows, cuts, *packed):
+    return queue.run(functools.partial(place_kernel, cuts), packed, [array(rows, end - at) for at, end in cuts])
 
 
 def gather_kernel(cut, _, own_ref, back_ref, sel_ref, *refs):
@@ -287,6 +285,7 @@
             grads[:, pl.ds(base + hidden, tile)] = (scaled * active).astype(BF16)
         gates += jnp.where(here, total, 0.0)
     out_own[:, features:] = gates[:rows].astype(BF16)
+    gates = jnp.where(lane == LANES - 1, meta[...], gates)
     out_fars[-1][:, features - starts[-1] :] = gates[rows:].astype(BF16)
     for j in range(splits):
         at = pl.ds(j * split, split)
@@ -372,15 +371,16 @@
     for s in range(depth):
         if s == 1:
             take_tokens(2)
-        kept = own[early : early + 1] if s == early + 2 else []
+        kept = far[early : early + 1] if s == early + 1 else own[early : early + 1] if s == early + 2 else []
         p0, p1, *kept = project(queue, xs[s], xf[s], w0, w1, *kept)
-        own[early : early + len(kept)] = kept
+        if s == early + 1:
+            lifted = move(kept[0], up)
+        if s == early + 2:
+            own[early] = kept[0]
         if 1 < s < last:
             take_tokens(s + 1)
-        if s == early + 1:
-            lifted = move(place(queue, far[early], xf[early], rows), up)
         if s == early + 2:
-            lifted = place(queue, far[s - 1], xf[s - 1], rows, lifted, cuts=halves)
+            lifted = place(queue, rows, halves, far[s - 1], lifted)
             back[s - 1] = [move(a, across) for a in lifted]
         if s == 0:
             take_grads(1)

time: 132 us -> 129 us (0.977)
  waiting for transfers between devices: 13.5 us -> 11.4 us
    ppermute x27, waiting for transfers between devices: 13.5 us -> 11.4 us  [shards(): move = lambda a, pairs: lax.ppermute(a, 'expert', pairs)]
    pallas_call x26 -> x25, Pallas kernels: 73.7 us -> 72.5 us  [run(): pl.pallas_call(body, in_specs=[SCALAR] + [ANYWHERE] * anywhere + [LOCAL]...]
  transfers between devices with their start and end apart: 27 -> 27, of which waited for: 11 -> 8; matrix products, arithmetic and copies ran while one was open for 0% -> 0% of each run, Pallas kernels for 55% -> 55%
where the time goes in v6:
time: 129 us
  Pallas kernels  72.5 us (56%)
  starting transfers between devices  43.6 us (34%)
  waiting for transfers between devices  11.4 us (9%)
    pallas_call x25, Pallas kernels, run(): pl.pallas_call(body, in_specs=[SCALAR] + [ANYWHERE] * anywhere + [LOCAL]...  72.5 us
    ppermute x27, starting transfers between devices, shards(): move = lambda a, pairs: lax.ppermute(a, 'expert', pairs)  43.6 us
    ppermute x27, waiting for transfers between devices, shards(): move = lambda a, pairs: lax.ppermute(a, 'expert', pairs)  11.4 us
  transfers between devices with their start and end apart: 27, of which 8 were waited for; matrix products, arithmetic and copies ran while one was open for 0% of the time, Pallas kernels for 55%

profile of v6, /device:TPU:0, one launch (start us, length us, event | category | flops | bytes accessed | tf_op | source)
XLA Modules:
  0.0 129.0 jit_solution(6377673188835033812)
XLA Ops:
  1.3 2.3 %shard_map.77 = (bf16[128,2176]{1,0:T(8,128)(2,1)S(1)}, bf16[112,2176]{1,0:T(8,128)(2,1)S(1)}, bf16[112,128]{1,0:T(8,128)(2,1)S(1)}, s32[4]{0:T(128)S(1)}) custom-call(s32[4]{0:T(128)S(1)} %pad_add_fusion.ticket_ref, bf16[128,2048]{1,0:T(8,128)(2,1)} %refs_0_.1, s32[4,128]{1,0:T(4,128)} %bitcast.9, bf16[4,128]{1,0:T(4,128)(2,1)} %bitcast.15), custom_call_target="tpu_custom_call" | custom-call | tf_op jit(solution)/shard_map/pallas_call | solution.py:36
  3.6 3.1 %collective-permute-start.2 = (bf16[128,2176]{1,0:T(8,128)(2,1)S(1)}, bf16[128,2176]{1,0:T(8,128)(2,1)S(1)}, u32[]{:S(2)}, u32[]{:S(2)}) collective-permute-start(bf16[128,2176]{1,0:T(8,128)(2,1)S(1)} %get-tuple-element.82.refs_0_.refs_4_), channel_id=1, source_target_pairs={{0,4},{1,5},{2,6},{3,7},{4,12},{5,13},{6,14},{7,15},{8,0},{9,1},{1... | collective-permute-start | bytes 1671176 | tf_op jit(solution)/shard_map/ppermute | solution.py:325
  6.6 1.5 %collective-permute-start.3 = (bf16[112,2176]{1,0:T(8,128)(2,1)S(1)}, bf16[112,2176]{1,0:T(8,128)(2,1)S(1)}, u32[]{:S(2)}, u32[]{:S(2)}) collective-permute-start(bf16[112,2176]{1,0:T(8,128)(2,1)S(1)} %get-tuple-element.84), channel_id=1, source_target_pairs={{0,2},{1,3},{2,0},{3,1},{4,6},{5,7},{6,4},{7,5},{8,10},{9,11},{10,... | collective-permute-start | bytes 1462280 | tf_op jit(solution)/shard_map/ppermute | solution.py:325
  8.1 2.6 %collective-permute-start.4 = (bf16[128,2048]{1,0:T(8,128)(2,1)}, bf16[128,2048]{1,0:T(8,128)(2,1)S(1)}, u32[]{:S(2)}, u32[]{:S(2)}) collective-permute-start(bf16[128,2048]{1,0:T(8,128)(2,1)} %refs_2_.1), channel_id=1, source_target_pairs={{0,4},{1,5},{2,6},{3,7},{4,12},{5,13},{6,14},{7,15},{8,0},{9,1},{1... | collective-permute-start | bytes 1572872 | tf_op jit(solution)/shard_map/ppermute | solution.py:325
  10.7 4.9 %shard_map.78 = (bf16[2048,1536]{1,0:T(8,128)(2,1)S(1)}, bf16[768,2048]{1,0:T(8,128)(2,1)S(1)}, s32[4]{0:T(128)S(1)}) custom-call(s32[4]{0:T(128)S(1)} %get-tuple-element.77.ticket_ref, bf16[2048,1536]{1,0:T(8,128)(2,1)} %bitcast.12, bf16[768,2048]{1,0:T(8,128)(2,1)} %bitcast.14), custom_call_target="tpu_custom_call" | custom-call | tf_op jit(solution)/shard_map/pallas_call | solution.py:36
  18.5 4.9 %shard_map.80 = (bf16[2048,1536]{1,0:T(8,128)(2,1)S(1)}, bf16[768,2048]{1,0:T(8,128)(2,1)S(1)}, s32[4]{0:T(128)S(1)}) custom-call(s32[4]{0:T(128)S(1)} %get-tuple-element.80.ticket_ref, bf16[2048,1536]{1,0:T(8,128)(2,1)} %collective-permute-done.refs_0_, bf16[768,2048]{1,0:T(8,128)(2,1)} %copy-done.2), custom_call_target="tpu_custom_call" | custom-call | tf_op jit(solution)/shard_map/pallas_call | solution.py:36
  23.4 1.4 %shard_map.81 = (bf16[112,2176]{1,0:T(8,128)(2,1)S(1)}, bf16[112,128]{1,0:T(8,128)(2,1)S(1)}, bf16[128,2176]{1,0:T(8,128)(2,1)S(1)}, s32[4]{0:T(128)S(1)}) custom-call(s32[4]{0:T(128)S(1)} %get-tuple-element.81.ticket_ref, bf16[128,2176]{1,0:T(8,128)(2,1)S(1)} %collective-permute-done.2.refs_0_), custom_call_target="tpu_custom_call" | custom-call | tf_op jit(solution)/shard_map/pallas_call | solution.py:36
  24.8 1.5 %collective-permute-start.6 = (bf16[128,2176]{1,0:T(8,128)(2,1)S(1)}, bf16[128,2176]{1,0:T(8,128)(2,1)S(1)}, u32[]{:S(2)}, u32[]{:S(2)}) collective-permute-start(bf16[128,2176]{1,0:T(8,128)(2,1)S(1)} %get-tuple-element.96.refs_0_.refs_4_), channel_id=1, source_target_pairs={{0,4},{1,5},{2,6},{3,7},{4,12},{5,13},{6,14},{7,15},{8,0},{9,1},{1... | collective-permute-start | bytes 1671176 | tf_op jit(solution)/shard_map/ppermute | solution.py:325
  26.3 1.5 %collective-permute-start.7 = (bf16[112,2176]{1,0:T(8,128)(2,1)S(1)}, bf16[112,2176]{1,0:T(8,128)(2,1)S(1)}, u32[]{:S(2)}, u32[]{:S(2)}) collective-permute-start(bf16[112,2176]{1,0:T(8,128)(2,1)S(1)} %get-tuple-element.98), channel_id=1, source_target_pairs={{0,2},{1,3},{2,0},{3,1},{4,6},{5,7},{6,4},{7,5},{8,10},{9,11},{10,... | collective-permute-start | bytes 1462280 | tf_op jit(solution)/shard_map/ppermute | solution.py:325
  27.9 4.1 %shard_map.82 = (f32[240,1536]{1,0:T(8,128)S(1)}, f32[240,1536]{1,0:T(8,128)S(1)}, s32[4]{0:T(128)S(1)}) custom-call(s32[4]{0:T(128)S(1)} %get-tuple-element.83.ticket_ref, bf16[128,2176]{1,0:T(8,128)(2,1)S(1)} %get-tuple-element.82.refs_0_.refs_4_, bf16[112,2176]{1,0:T(8,128)(2,1)S(1)} %collective-permute-done.3.refs_1_.refs_5_, ...), custom_call_target="tpu_custom_call" | custom-call | flops 905969664 | tf_op jit(solution)/shard_map/pallas_call | solution.py:36
  33.4 2.0 %collective-permute-start.8 = (bf16[112,2048]{1,0:T(8,128)(2,1)S(1)}, bf16[112,2048]{1,0:T(8,128)(2,1)S(1)}, u32[]{:S(2)}, u32[]{:S(2)}) collective-permute-start(bf16[112,2048]{1,0:T(8,128)(2,1)S(1)} %get-tuple-element.103), channel_id=1, source_target_pairs={{0,2},{1,3},{2,0},{3,1},{4,6},{5,7},{6,4},{7,5},{8,10},{9,11},{10,... | collective-permute-start | bytes 1376264 | tf_op jit(solution)/shard_map/ppermute | solution.py:325
  36.3 6.7 %shard_map.84 = (bf16[128,2176]{1,0:T(8,128)(2,1)S(1)}, bf16[112,2176]{1,0:T(8,128)(2,1)S(1)}, s32[4]{0:T(128)S(1)}) custom-call(s32[4]{0:T(128)S(1)} %get-tuple-element.89.ticket_ref, f32[240,1536]{1,0:T(8,128)S(1)} %get-tuple-element.90.refs_0_, f32[240,1536]{1,0:T(8,128)S(1)} %get-tuple-element.91.refs_1_, bf16[128,2048]{1,0:T(8,128)(2,1)S(1)} %copy-done, ...), custom_call_target="tpu_custom_call" | custom-call | flops 1358954496 | tf_op jit(solution)/shard_map/pallas_call | solution.py:36
  45.7 2.0 %collective-permute-start.10 = (bf16[112,2176]{1,0:T(8,128)(2,1)S(1)}, bf16[112,2176]{1,0:T(8,128)(2,1)S(1)}, u32[]{:S(2)}, u32[]{:S(2)}) collective-permute-start(bf16[112,2176]{1,0:T(8,128)(2,1)S(1)} %get-tuple-element.108), channel_id=1, source_target_pairs={{0,2},{1,3},{2,0},{3,1},{4,6},{5,7},{6,4},{7,5},{8,10},{9,11},{10,... | collective-permute-start | bytes 1462280 | tf_op jit(solution)/shard_map/ppermute | solution.py:325
  48.4 4.2 %shard_map.86 = (f32[240,1536]{1,0:T(8,128)S(1)}, f32[240,1536]{1,0:T(8,128)S(1)}, s32[4]{0:T(128)S(1)}) custom-call(s32[4]{0:T(128)S(1)} %get-tuple-element.97.ticket_ref, bf16[128,2176]{1,0:T(8,128)(2,1)S(1)} %get-tuple-element.96.refs_0_.refs_4_, bf16[112,2176]{1,0:T(8,128)(2,1)S(1)} %collective-permute-done.7.refs_1_.refs_5_, ...), custom_call_target="tpu_custom_call" | custom-call | flops 905969664 | tf_op jit(solution)/shard_map/pallas_call | solution.py:36
  52.6 6.7 %shard_map.87 = (bf16[128,2176]{1,0:T(8,128)(2,1)S(1)}, bf16[112,2176]{1,0:T(8,128)(2,1)S(1)}, s32[4]{0:T(128)S(1)}) custom-call(s32[4]{0:T(128)S(1)} %get-tuple-element.99.ticket_ref, f32[240,1536]{1,0:T(8,128)S(1)} %get-tuple-element.100.refs_0_, f32[240,1536]{1,0:T(8,128)S(1)} %get-tuple-element.101.refs_1_, ...), custom_call_target="tpu_custom_call" | custom-call | flops 1358954496 | tf_op jit(solution)/shard_map/pallas_call | solution.py:36
  61.8 2.5 %collective-permute-start.13 = (bf16[128,2048]{1,0:T(8,128)(2,1)S(1)}, bf16[128,2048]{1,0:T(8,128)(2,1)S(1)}, u32[]{:S(2)}, u32[]{:S(2)}) collective-permute-start(bf16[128,2048]{1,0:T(8,128)(2,1)S(1)} %get-tuple-element.114.refs_2_), channel_id=1, source_target_pairs={{0,4},{1,5},{2,6},{3,7},{4,12},{5,13},{6,14},{7,15},{8,0},{9,1},{1... | collective-permute-start | bytes 1572872 | tf_op jit(solution)/shard_map/ppermute | solution.py:325
  64.4 4.2 %shard_map.89 = (f32[240,1536]{1,0:T(8,128)S(1)}, f32[240,1536]{1,0:T(8,128)S(1)}, bf16[112,2176]{1,0:T(8,128)(2,1)S(1)}, s32[4]{0:T(128)S(1)}) custom-call(s32[4]{0:T(128)S(1)} %get-tuple-element.106.ticket_ref, bf16[128,2176]{1,0:T(8,128)(2,1)S(1)} %get-tuple-element.107.refs_0_.refs_4_, bf16[112,2176]{1,0:T(8,128)(2,1)S(1)} %collective-permute-done.10.refs_1_.refs_5_, ...), custom_call_target="tpu_custom_call" | custom-call | flops 905969664 | tf_op jit(solution)/shard_map/pallas_call | solution.py:36
  70.0 1.6 %collective-permute-start.14 = (bf16[112,2176]{1,0:T(8,128)(2,1)S(1)}, bf16[112,2176]{1,0:T(8,128)(2,1)S(1)}, u32[]{:S(2)}, u32[]{:S(2)}) collective-permute-start(bf16[112,2176]{1,0:T(8,128)(2,1)S(1)} %get-tuple-element.119), channel_id=1, source_target_pairs={{0,2},{1,3},{2,0},{3,1},{4,6},{5,7},{6,4},{7,5},{8,10},{9,11},{10,... | collective-permute-start | bytes 1462280 | tf_op jit(solution)/shard_map/ppermute | solution.py:325
  71.6 6.6 %shard_map.91 = (bf16[128,2176]{1,0:T(8,128)(2,1)S(1)}, bf16[112,2176]{1,0:T(8,128)(2,1)S(1)}, s32[4]{0:T(128)S(1)}) custom-call(s32[4]{0:T(128)S(1)} %get-tuple-element.111.ticket_ref, f32[240,1536]{1,0:T(8,128)S(1)} %get-tuple-element.112.refs_0_, f32[240,1536]{1,0:T(8,128)S(1)} %get-tuple-element.113.refs_1_, ...), custom_call_target="tpu_custom_call" | custom-call | flops 1358954496 | tf_op jit(solution)/shard_map/pallas_call | solution.py:36
  79.8 2.0 %collective-permute-start.16 = (bf16[112,2048]{1,0:T(8,128)(2,1)S(1)}, bf16[112,2048]{1,0:T(8,128)(2,1)S(1)}, u32[]{:S(2)}, u32[]{:S(2)}) collective-permute-start(bf16[112,2048]{1,0:T(8,128)(2,1)S(1)} %get-tuple-element.127), channel_id=1, source_target_pairs={{0,2},{1,3},{2,0},{3,1},{4,6},{5,7},{6,4},{7,5},{8,10},{9,11},{10,... | collective-permute-start | bytes 1376264 | tf_op jit(solution)/shard_map/ppermute | solution.py:325
  81.7 4.2 %shard_map.93 = (f32[240,1536]{1,0:T(8,128)S(1)}, f32[240,1536]{1,0:T(8,128)S(1)}, bf16[128,2176]{1,0:T(8,128)(2,1)S(1)}, s32[4]{0:T(128)S(1)}) custom-call(s32[4]{0:T(128)S(1)} %get-tuple-element.118.ticket_ref, bf16[128,2176]{1,0:T(8,128)(2,1)S(1)} %collective-permute-done.11.refs_0_.refs_4_, ...), custom_call_target="tpu_custom_call" | custom-call | flops 905969664 | tf_op jit(solution)/shard_map/pallas_call | solution.py:36
  85.9 4.1 %collective-permute-start.18 = (bf16[128,2176]{1,0:T(8,128)(2,1)S(1)}, bf16[128,2176]{1,0:T(8,128)(2,1)S(1)}, u32[]{:S(2)}, u32[]{:S(2)}) collective-permute-start(bf16[128,2176]{1,0:T(8,128)(2,1)S(1)} %get-tuple-element.131), channel_id=1, source_target_pairs={{0,4},{1,5},{2,6},{3,7},{4,12},{5,13},{6,14},{7,15},{8,0},{9,1},{1... | collective-permute-start | bytes 1671176 | tf_op jit(solution)/shard_map/ppermute | solution.py:325
  93.3 6.7 %shard_map.95 = (bf16[128,2176]{1,0:T(8,128)(2,1)S(1)}, bf16[112,1024]{1,0:T(8,128)(2,1)S(1)}, bf16[112,1152]{1,0:T(8,128)(2,1)S(1)}, s32[4]{0:T(128)S(1)}) custom-call(s32[4]{0:T(128)S(1)} %get-tuple-element.124.ticket_ref, f32[240,1536]{1,0:T(8,128)S(1)} %get-tuple-element.125.refs_0_, f32[240,1536]{1,0:T(8,128)S(1)} %get-tuple-element.126.refs_1_, ...), custom_call_target="tpu_custom_call" | custom-call | flops 1358954496 | tf_op jit(solution)/shard_map/pallas_call | solution.py:36
  101.7 2.5 %collective-permute-start.21 = (bf16[128,1024]{1,0:T(8,128)(2,1)S(1)}, bf16[128,1024]{1,0:T(8,128)(2,1)S(1)}, u32[]{:S(2)}, u32[]{:S(2)}) collective-permute-start(bf16[128,1024]{1,0:T(8,128)(2,1)S(1)} %get-tuple-element.138), channel_id=1, source_target_pairs={{0,4},{1,5},{2,6},{3,7},{4,12},{5,13},{6,14},{7,15},{8,0},{9,1},{1... | collective-permute-start | bytes 786440 | tf_op jit(solution)/shard_map/ppermute | solution.py:325
  104.1 2.0 %collective-permute-start.22 = (bf16[112,1152]{1,0:T(8,128)(2,1)S(1)}, bf16[112,1152]{1,0:T(8,128)(2,1)S(1)}, u32[]{:S(2)}, u32[]{:S(2)}) collective-permute-start(bf16[112,1152]{1,0:T(8,128)(2,1)S(1)} %get-tuple-element.140), channel_id=1, source_target_pairs={{0,2},{1,3},{2,0},{3,1},{4,6},{5,7},{6,4},{7,5},{8,10},{9,11},{10,... | collective-permute-start | bytes 774152 | tf_op jit(solution)/shard_map/ppermute | solution.py:325
  107.5 3.2 %collective-permute-start.23 = (bf16[128,1152]{1,0:T(8,128)(2,1)S(1)}, bf16[128,1152]{1,0:T(8,128)(2,1)S(1)}, u32[]{:S(2)}, u32[]{:S(2)}) collective-permute-start(bf16[128,1152]{1,0:T(8,128)(2,1)S(1)} %get-tuple-element.141), channel_id=1, source_target_pairs={{0,4},{1,5},{2,6},{3,7},{4,12},{5,13},{6,14},{7,15},{8,0},{9,1},{1... | collective-permute-start | bytes 884744 | tf_op jit(solution)/shard_map/ppermute | solution.py:325
  110.7 2.0 %collective-permute-done.20.refs_1_ = bf16[112,1024]{1,0:T(8,128)(2,1)S(1)} collective-permute-done((bf16[112,1024]{1,0:T(8,128)(2,1)S(1)}, bf16[112,1024]{1,0:T(8,128)(2,1)S(1)}, u32[]{:S(2)}, u32[]{:S(2)}) %collective-permute-start.20) | collective-permute-done | bytes 229408 | tf_op jit(solution)/shard_map/ppermute | solution.py:325
  113.8 1.8 %collective-permute-start.25 = (bf16[128,1024]{1,0:T(8,128)(2,1)S(1)}, bf16[128,1024]{1,0:T(8,128)(2,1)S(1)}, u32[]{:S(2)}, u32[]{:S(2)}) collective-permute-start(bf16[128,1024]{1,0:T(8,128)(2,1)S(1)} %get-tuple-element.145), channel_id=1, source_target_pairs={{0,4},{1,5},{2,6},{3,7},{4,12},{5,13},{6,14},{7,15},{8,0},{9,1},{1... | collective-permute-start | bytes 786440 | tf_op jit(solution)/shard_map/ppermute | solution.py:325
  115.6 2.6 %collective-permute-done.22.refs_1_ = bf16[112,1152]{1,0:T(8,128)(2,1)S(1)} collective-permute-done((bf16[112,1152]{1,0:T(8,128)(2,1)S(1)}, bf16[112,1152]{1,0:T(8,128)(2,1)S(1)}, u32[]{:S(2)}, u32[]{:S(2)}) %collective-permute-start.22) | collective-permute-done | bytes 258080 | tf_op jit(solution)/shard_map/ppermute | solution.py:325
  119.4 2.5 %collective-permute-start.26 = (bf16[128,1152]{1,0:T(8,128)(2,1)S(1)}, bf16[128,1152]{1,0:T(8,128)(2,1)S(1)}, u32[]{:S(2)}, u32[]{:S(2)}) collective-permute-start(bf16[128,1152]{1,0:T(8,128)(2,1)S(1)} %get-tuple-element.149), channel_id=1, source_target_pairs={{0,4},{1,5},{2,6},{3,7},{4,12},{5,13},{6,14},{7,15},{8,0},{9,1},{1... | collective-permute-start | bytes 884744 | tf_op jit(solution)/shard_map/ppermute | solution.py:325
  121.8 2.9 %collective-permute-done.24.refs_1_ = bf16[112,2176]{1,0:T(8,128)(2,1)S(1)} collective-permute-done((bf16[112,2176]{1,0:T(8,128)(2,1)S(1)}, bf16[112,2176]{1,0:T(8,128)(2,1)S(1)}, u32[]{:S(2)}, u32[]{:S(2)}) %collective-permute-start.24) | collective-permute-done | bytes 487456 | tf_op jit(solution)/shard_map/ppermute | solution.py:325
  127.2 1.5 %shard_map.101 = (bf16[128,2048]{1,0:T(8,128)(2,1)}, bf16[4,128]{1,0:T(4,128)(2,1)}, s32[4]{0:T(128)}) custom-call(s32[4]{0:T(128)S(1)} %get-tuple-element.146.ticket_ref, bf16[128,1024]{1,0:T(8,128)(2,1)S(1)} %get-tuple-element.147.refs_0_, f32[128,1152]{1,0:T(8,128)S(1)} %get-tuple-element.148.refs_1_, ...), custom_call_target="tpu_custom_call" | custom-call | tf_op jit(solution)/shard_map/pallas_call | solution.py:36
  (54 shorter events, 25.9 us)
Async XLA Ops:
  0.6 17.6 %collective-permute-start = (bf16[2048,1536]{1,0:T(8,128)(2,1)}, bf16[2048,1536]{1,0:T(8,128)(2,1)}, u32[]{:S(2)}, u32[]{:S(2)}) collective-permute-start(bf16[2048,1536]{1,0:T(8,128)(2,1)} %bitcast.11), channel_id=1, source_target_pairs={{0,1},{1,0},{2,3},{3,2},{4,5},{5,4},{6,7},{7,6},{8,9},{9,8},{10,11... | collective-permute-start | bytes 18874376 | tf_op jit(solution)/shard_map/ppermute | solution.py:325
  1.1 15.6 %collective-permute-start.1 = (bf16[768,2048]{1,0:T(8,128)(2,1)}, bf16[768,2048]{1,0:T(8,128)(2,1)S(1)}, u32[]{:S(2)}, u32[]{:S(2)}) collective-permute-start(bf16[768,2048]{1,0:T(8,128)(2,1)} %bitcast.13), channel_id=1, source_target_pairs={{0,1},{1,0},{2,3},{3,2},{4,5},{5,4},{6,7},{7,6},{8,9},{9,8},{10,11... | collective-permute-start | bytes 9437192 | tf_op jit(solution)/shard_map/ppermute | solution.py:325
  3.6 19.8 %collective-permute-start.2 = (bf16[128,2176]{1,0:T(8,128)(2,1)S(1)}, bf16[128,2176]{1,0:T(8,128)(2,1)S(1)}, u32[]{:S(2)}, u32[]{:S(2)}) collective-permute-start(bf16[128,2176]{1,0:T(8,128)(2,1)S(1)} %get-tuple-element.82.refs_0_.refs_4_), channel_id=1, source_target_pairs={{0,4},{1,5},{2,6},{3,7},{4,12},{5,13},{6,14},{7,15},{8,0},{9,1},{1... | collective-permute-start | bytes 1671176 | tf_op jit(solution)/shard_map/ppermute | solution.py:325
  6.6 21.2 %collective-permute-start.3 = (bf16[112,2176]{1,0:T(8,128)(2,1)S(1)}, bf16[112,2176]{1,0:T(8,128)(2,1)S(1)}, u32[]{:S(2)}, u32[]{:S(2)}) collective-permute-start(bf16[112,2176]{1,0:T(8,128)(2,1)S(1)} %get-tuple-element.84), channel_id=1, source_target_pairs={{0,2},{1,3},{2,0},{3,1},{4,6},{5,7},{6,4},{7,5},{8,10},{9,11},{10,... | collective-permute-start | bytes 1462280 | tf_op jit(solution)/shard_map/ppermute | solution.py:325
  8.1 24.1 %collective-permute-start.4 = (bf16[128,2048]{1,0:T(8,128)(2,1)}, bf16[128,2048]{1,0:T(8,128)(2,1)S(1)}, u32[]{:S(2)}, u32[]{:S(2)}) collective-permute-start(bf16[128,2048]{1,0:T(8,128)(2,1)} %refs_2_.1), channel_id=1, source_target_pairs={{0,4},{1,5},{2,6},{3,7},{4,12},{5,13},{6,14},{7,15},{8,0},{9,1},{1... | collective-permute-start | bytes 1572872 | tf_op jit(solution)/shard_map/ppermute | solution.py:325
  10.7 4.9 %copy-start = (bf16[128,2048]{1,0:T(8,128)(2,1)S(1)}, bf16[128,2048]{1,0:T(8,128)(2,1)}, u32[]{:S(2)}) copy-start(bf16[128,2048]{1,0:T(8,128)(2,1)} %refs_2_.1) | copy-start | bytes 1572868
  16.8 1.7 %copy-start.2 = (bf16[768,2048]{1,0:T(8,128)(2,1)}, bf16[768,2048]{1,0:T(8,128)(2,1)S(1)}, u32[]{:S(2)}) copy-start(bf16[768,2048]{1,0:T(8,128)(2,1)S(1)} %collective-permute-done.1.refs_1_) | copy-start | bytes 9437188
  16.8 19.5 %collective-permute-start.5 = (bf16[112,2048]{1,0:T(8,128)(2,1)S(1)}, bf16[112,2048]{1,0:T(8,128)(2,1)S(1)}, u32[]{:S(2)}, u32[]{:S(2)}) collective-permute-start(bf16[112,2048]{1,0:T(8,128)(2,1)S(1)} %get-tuple-element.92), channel_id=1, source_target_pairs={{0,2},{1,3},{2,0},{3,1},{4,6},{5,7},{6,4},{7,5},{8,10},{9,11},{10,... | collective-permute-start | bytes 1376264 | tf_op jit(solution)/shard_map/ppermute | solution.py:325
  24.8 19.4 %collective-permute-start.6 = (bf16[128,2176]{1,0:T(8,128)(2,1)S(1)}, bf16[128,2176]{1,0:T(8,128)(2,1)S(1)}, u32[]{:S(2)}, u32[]{:S(2)}) collective-permute-start(bf16[128,2176]{1,0:T(8,128)(2,1)S(1)} %get-tuple-element.96.refs_0_.refs_4_), channel_id=1, source_target_pairs={{0,4},{1,5},{2,6},{3,7},{4,12},{5,13},{6,14},{7,15},{8,0},{9,1},{1... | collective-permute-start | bytes 1671176 | tf_op jit(solution)/shard_map/ppermute | solution.py:325
  26.3 22.1 %collective-permute-start.7 = (bf16[112,2176]{1,0:T(8,128)(2,1)S(1)}, bf16[112,2176]{1,0:T(8,128)(2,1)S(1)}, u32[]{:S(2)}, u32[]{:S(2)}) collective-permute-start(bf16[112,2176]{1,0:T(8,128)(2,1)S(1)} %get-tuple-element.98), channel_id=1, source_target_pairs={{0,2},{1,3},{2,0},{3,1},{4,6},{5,7},{6,4},{7,5},{8,10},{9,11},{10,... | collective-permute-start | bytes 1462280 | tf_op jit(solution)/shard_map/ppermute | solution.py:325
  33.4 19.2 %collective-permute-start.8 = (bf16[112,2048]{1,0:T(8,128)(2,1)S(1)}, bf16[112,2048]{1,0:T(8,128)(2,1)S(1)}, u32[]{:S(2)}, u32[]{:S(2)}) collective-permute-start(bf16[112,2048]{1,0:T(8,128)(2,1)S(1)} %get-tuple-element.103), channel_id=1, source_target_pairs={{0,2},{1,3},{2,0},{3,1},{4,6},{5,7},{6,4},{7,5},{8,10},{9,11},{10,... | collective-permute-start | bytes 1376264 | tf_op jit(solution)/shard_map/ppermute | solution.py:325
  35.4 23.9 %collective-permute-start.9 = (bf16[128,2048]{1,0:T(8,128)(2,1)S(1)}, bf16[128,2048]{1,0:T(8,128)(2,1)S(1)}, u32[]{:S(2)}, u32[]{:S(2)}) collective-permute-start(bf16[128,2048]{1,0:T(8,128)(2,1)S(1)} %get-tuple-element.102.refs_2_), channel_id=1, source_target_pairs={{0,4},{1,5},{2,6},{3,7},{4,12},{5,13},{6,14},{7,15},{8,0},{9,1},{1... | collective-permute-start | bytes 1572872 | tf_op jit(solution)/shard_map/ppermute | solution.py:325
  45.7 18.7 %collective-permute-start.10 = (bf16[112,2176]{1,0:T(8,128)(2,1)S(1)}, bf16[112,2176]{1,0:T(8,128)(2,1)S(1)}, u32[]{:S(2)}, u32[]{:S(2)}) collective-permute-start(bf16[112,2176]{1,0:T(8,128)(2,1)S(1)} %get-tuple-element.108), channel_id=1, source_target_pairs={{0,2},{1,3},{2,0},{3,1},{4,6},{5,7},{6,4},{7,5},{8,10},{9,11},{10,... | collective-permute-start | bytes 1462280 | tf_op jit(solution)/shard_map/ppermute | solution.py:325
  47.6 20.9 %collective-permute-start.11 = (bf16[128,2176]{1,0:T(8,128)(2,1)S(1)}, bf16[128,2176]{1,0:T(8,128)(2,1)S(1)}, u32[]{:S(2)}, u32[]{:S(2)}) collective-permute-start(bf16[128,2176]{1,0:T(8,128)(2,1)S(1)} %get-tuple-element.107.refs_0_.refs_4_), channel_id=1, source_target_pairs={{0,4},{1,5},{2,6},{3,7},{4,12},{5,13},{6,14},{7,15},{8,0},{9,1},{1... | collective-permute-start | bytes 1671176 | tf_op jit(solution)/shard_map/ppermute | solution.py:325
  60.4 11.1 %collective-permute-start.12 = (bf16[112,2048]{1,0:T(8,128)(2,1)S(1)}, bf16[112,2048]{1,0:T(8,128)(2,1)S(1)}, u32[]{:S(2)}, u32[]{:S(2)}) collective-permute-start(bf16[112,2048]{1,0:T(8,128)(2,1)S(1)} %get-tuple-element.115), channel_id=1, source_target_pairs={{0,2},{1,3},{2,0},{3,1},{4,6},{5,7},{6,4},{7,5},{8,10},{9,11},{10,... | collective-permute-start | bytes 1376264 | tf_op jit(solution)/shard_map/ppermute | solution.py:325
  61.8 16.8 %collective-permute-start.13 = (bf16[128,2048]{1,0:T(8,128)(2,1)S(1)}, bf16[128,2048]{1,0:T(8,128)(2,1)S(1)}, u32[]{:S(2)}, u32[]{:S(2)}) collective-permute-start(bf16[128,2048]{1,0:T(8,128)(2,1)S(1)} %get-tuple-element.114.refs_2_), channel_id=1, source_target_pairs={{0,4},{1,5},{2,6},{3,7},{4,12},{5,13},{6,14},{7,15},{8,0},{9,1},{1... | collective-permute-start | bytes 1572872 | tf_op jit(solution)/shard_map/ppermute | solution.py:325
  70.0 11.8 %collective-permute-start.14 = (bf16[112,2176]{1,0:T(8,128)(2,1)S(1)}, bf16[112,2176]{1,0:T(8,128)(2,1)S(1)}, u32[]{:S(2)}, u32[]{:S(2)}) collective-permute-start(bf16[112,2176]{1,0:T(8,128)(2,1)S(1)} %get-tuple-element.119), channel_id=1, source_target_pairs={{0,2},{1,3},{2,0},{3,1},{4,6},{5,7},{6,4},{7,5},{8,10},{9,11},{10,... | collective-permute-start | bytes 1462280 | tf_op jit(solution)/shard_map/ppermute | solution.py:325
  71.5 18.5 %collective-permute-start.15 = (bf16[112,2176]{1,0:T(8,128)(2,1)S(1)}, bf16[112,2176]{1,0:T(8,128)(2,1)S(1)}, u32[]{:S(2)}, u32[]{:S(2)}) collective-permute-start(bf16[112,2176]{1,0:T(8,128)(2,1)S(1)} %get-tuple-element.123), channel_id=1, source_target_pairs={{0,4},{1,5},{2,6},{3,7},{4,12},{5,13},{6,14},{7,15},{8,0},{9,1},{1... | collective-permute-start | bytes 1462280 | tf_op jit(solution)/shard_map/ppermute | solution.py:325
  79.8 13.5 %collective-permute-start.16 = (bf16[112,2048]{1,0:T(8,128)(2,1)S(1)}, bf16[112,2048]{1,0:T(8,128)(2,1)S(1)}, u32[]{:S(2)}, u32[]{:S(2)}) collective-permute-start(bf16[112,2048]{1,0:T(8,128)(2,1)S(1)} %get-tuple-element.127), channel_id=1, source_target_pairs={{0,2},{1,3},{2,0},{3,1},{4,6},{5,7},{6,4},{7,5},{8,10},{9,11},{10,... | collective-permute-start | bytes 1376264 | tf_op jit(solution)/shard_map/ppermute | solution.py:325
  85.9 14.6 %collective-permute-start.18 = (bf16[128,2176]{1,0:T(8,128)(2,1)S(1)}, bf16[128,2176]{1,0:T(8,128)(2,1)S(1)}, u32[]{:S(2)}, u32[]{:S(2)}) collective-permute-start(bf16[128,2176]{1,0:T(8,128)(2,1)S(1)} %get-tuple-element.131), channel_id=1, source_target_pairs={{0,4},{1,5},{2,6},{3,7},{4,12},{5,13},{6,14},{7,15},{8,0},{9,1},{1... | collective-permute-start | bytes 1671176 | tf_op jit(solution)/shard_map/ppermute | solution.py:325
  91.2 9.3 %collective-permute-start.17 = (bf16[128,1024]{1,0:T(8,128)(2,1)S(1)}, bf16[128,1024]{1,0:T(8,128)(2,1)S(1)}, u32[]{:S(2)}, u32[]{:S(2)}) collective-permute-start(bf16[128,1024]{1,0:T(8,128)(2,1)S(1)} %get-tuple-element.130), channel_id=1, source_target_pairs={{0,2},{1,3},{2,0},{3,1},{4,6},{5,7},{6,4},{7,5},{8,10},{9,11},{10,... | collective-permute-start | bytes 786440 | tf_op jit(solution)/shard_map/ppermute | solution.py:325
  92.4 13.7 %collective-permute-start.19 = (bf16[128,1152]{1,0:T(8,128)(2,1)S(1)}, bf16[128,1152]{1,0:T(8,128)(2,1)S(1)}, u32[]{:S(2)}, u32[]{:S(2)}) collective-permute-start(bf16[128,1152]{1,0:T(8,128)(2,1)S(1)} %get-tuple-element.134), channel_id=1, source_target_pairs={{0,2},{1,3},{2,0},{3,1},{4,6},{5,7},{6,4},{7,5},{8,10},{9,11},{10,... | collective-permute-start | bytes 884744 | tf_op jit(solution)/shard_map/ppermute | solution.py:325
  101.7 11.0 %collective-permute-start.21 = (bf16[128,1024]{1,0:T(8,128)(2,1)S(1)}, bf16[128,1024]{1,0:T(8,128)(2,1)S(1)}, u32[]{:S(2)}, u32[]{:S(2)}) collective-permute-start(bf16[128,1024]{1,0:T(8,128)(2,1)S(1)} %get-tuple-element.138), channel_id=1, source_target_pairs={{0,4},{1,5},{2,6},{3,7},{4,12},{5,13},{6,14},{7,15},{8,0},{9,1},{1... | collective-permute-start | bytes 786440 | tf_op jit(solution)/shard_map/ppermute | solution.py:325
  104.1 8.5 %collective-permute-start.20 = (bf16[112,1024]{1,0:T(8,128)(2,1)S(1)}, bf16[112,1024]{1,0:T(8,128)(2,1)S(1)}, u32[]{:S(2)}, u32[]{:S(2)}) collective-permute-start(bf16[112,1024]{1,0:T(8,128)(2,1)S(1)} %get-tuple-element.137), channel_id=1, source_target_pairs={{0,2},{1,3},{2,0},{3,1},{4,6},{5,7},{6,4},{7,5},{8,10},{9,11},{10,... | collective-permute-start | bytes 688136 | tf_op jit(solution)/shard_map/ppermute | solution.py:325
  104.1 14.1 %collective-permute-start.22 = (bf16[112,1152]{1,0:T(8,128)(2,1)S(1)}, bf16[112,1152]{1,0:T(8,128)(2,1)S(1)}, u32[]{:S(2)}, u32[]{:S(2)}) collective-permute-start(bf16[112,1152]{1,0:T(8,128)(2,1)S(1)} %get-tuple-element.140), channel_id=1, source_target_pairs={{0,2},{1,3},{2,0},{3,1},{4,6},{5,7},{6,4},{7,5},{8,10},{9,11},{10,... | collective-permute-start | bytes 774152 | tf_op jit(solution)/shard_map/ppermute | solution.py:325
  107.4 17.4 %collective-permute-start.24 = (bf16[112,2176]{1,0:T(8,128)(2,1)S(1)}, bf16[112,2176]{1,0:T(8,128)(2,1)S(1)}, u32[]{:S(2)}, u32[]{:S(2)}) collective-permute-start(bf16[112,2176]{1,0:T(8,128)(2,1)S(1)} %get-tuple-element.144), channel_id=1, source_target_pairs={{0,2},{1,3},{2,0},{3,1},{4,6},{5,7},{6,4},{7,5},{8,10},{9,11},{10,... | collective-permute-start | bytes 1462280 | tf_op jit(solution)/shard_map/ppermute | solution.py:325
  107.5 10.8 %collective-permute-start.23 = (bf16[128,1152]{1,0:T(8,128)(2,1)S(1)}, bf16[128,1152]{1,0:T(8,128)(2,1)S(1)}, u32[]{:S(2)}, u32[]{:S(2)}) collective-permute-start(bf16[128,1152]{1,0:T(8,128)(2,1)S(1)} %get-tuple-element.141), channel_id=1, source_target_pairs={{0,4},{1,5},{2,6},{3,7},{4,12},{5,13},{6,14},{7,15},{8,0},{9,1},{1... | collective-permute-start | bytes 884744 | tf_op jit(solution)/shard_map/ppermute | solution.py:325
  113.8 10.9 %collective-permute-start.25 = (bf16[128,1024]{1,0:T(8,128)(2,1)S(1)}, bf16[128,1024]{1,0:T(8,128)(2,1)S(1)}, u32[]{:S(2)}, u32[]{:S(2)}) collective-permute-start(bf16[128,1024]{1,0:T(8,128)(2,1)S(1)} %get-tuple-element.145), channel_id=1, source_target_pairs={{0,4},{1,5},{2,6},{3,7},{4,12},{5,13},{6,14},{7,15},{8,0},{9,1},{1... | collective-permute-start | bytes 786440 | tf_op jit(solution)/shard_map/ppermute | solution.py:325
  119.4 7.9 %collective-permute-start.26 = (bf16[128,1152]{1,0:T(8,128)(2,1)S(1)}, bf16[128,1152]{1,0:T(8,128)(2,1)S(1)}, u32[]{:S(2)}, u32[]{:S(2)}) collective-permute-start(bf16[128,1152]{1,0:T(8,128)(2,1)S(1)} %get-tuple-element.149), channel_id=1, source_target_pairs={{0,4},{1,5},{2,6},{3,7},{4,12},{5,13},{6,14},{7,15},{8,0},{9,1},{1... | collective-permute-start | bytes 884744 | tf_op jit(solution)/shard_map/ppermute | solution.py:325
  124.7 2.5 %copy-start.1 = (s32[128,4]{0,1:T(4,128)S(1)}, s32[128,4]{0,1:T(4,128)}, u32[]{:S(2)}) copy-start(s32[128,4]{0,1:T(4,128)} %param.8) | copy-start | bytes 6148

commit v7 on v6

--- a/solution.py
+++ b/solution.py
@@ -10,8 +10,8 @@
 F32, BF16 = jnp.float32, jnp.bfloat16
 LANES = 128
 VMEM_BYTES = 16 * 2**20
-COST = 30
-HOLD = 8 * 10**9, 0, 8 * 10**9
+COST = 34
+HOLD = 8 * 10**9, 8 * 10**9, 8 * 10**9
 NT = (((1,), (1,)), ((), ()))
 LOCAL = pl.BlockSpec(memory_space=pltpu.VMEM)
 SCALAR = pl.BlockSpec(memory_space=pltpu.SMEM)
@@ -160,18 +160,21 @@
     return queue.run(functools.partial(place_kernel, cuts), packed, [array(rows, end - at) for at, end in cuts])
 
 
-def gather_kernel(cut, _, own_ref, back_ref, sel_ref, *refs):
+def gather_kernel(cut, kept, _, *refs):
+    for ref, same_ref in zip(refs[:kept], refs[len(refs) - kept :]):
+        same_ref[...] = ref[...]
+    own_ref, back_ref, sel_ref, *carried_refs, out_ref = refs[kept : len(refs) - kept]
     at, end = cut
     total = own_ref[:, at:end].astype(F32) + spread(sel_ref, back_ref)
-    for ref in refs[:-1]:
+    for ref in carried_refs:
         total += (ref[...] if ref.shape == total.shape else ref[:, at:end]).astype(F32)
-    refs[-1][...] = total.astype(BF16)
-
-
-def gather(queue, own, back, sel, cut, *carried, flops=0):
-    return queue.run(
-        functools.partial(gather_kernel, cut), [own, back, sel, *carried],
-        [array(own.shape[0], cut[1] - cut[0])], flops=flops,
+    out_ref[...] = total.astype(BF16)
+
+
+def gather(queue, own, back, sel, cut, *carried, flops=0, kept=()):
+    return queue.run(
+        functools.partial(gather_kernel, cut, len(kept)), [*kept, own, back, sel, *carried],
+        [array(own.shape[0], cut[1] - cut[0])] + [array(*a.shape) for a in kept], flops=flops,
     )
 
 
@@ -394,19 +397,17 @@
     carried = [move(own[1] if early == 1 else gather(queue, own[1], back[1][0], sels[1], *whole), up)]
     for s in range(2, depth):
         if s == early + 1:
-            first = add(queue, halves[0], own[s], back[s][0], *carried)
-            second, later = add(queue, halves[1], own[s], back[s][1], *carried, kept=[far[0]])
-            back[0] = move(later, across)
-            carried = [first, second]
+            carried = [add(queue, cut, own[s], part, *carried) for cut, part in zip(halves, back[s])]
         elif s < last:
             carried = [gather(queue, own[s], back[s][0], sels[s], whole[0], *carried)]
         else:
-            if len(carried) == 1:
-                carried, back[0] = carried * 2, move(far[0], across)
-            carried = [
-                gather(queue, own[s], part, sels[s], cut, before, flops=cost)
-                for cut, part, before, cost in zip(halves, back[s], carried, HOLD)
-            ]
+            carried = carried if len(carried) == 2 else carried * 2
+            first, later = gather(
+                queue, own[s], back[s][0], sels[s], halves[0], carried[0], flops=HOLD[0], kept=[far[0]]
+            )
+            second = gather(queue, own[s], back[s][1], sels[s], halves[1], carried[1], flops=HOLD[1])
+            back[0] = move(later, across)
+            carried = [first, second]
         carried = [move(a, up) for a in carried]
     grad_tokens, grad_gates = finish(queue, own[0], back[0], sels[0], ids, *carried)
     return grad_tokens, grad_gates.T

time: 129 us -> 129 us (level)
  starting transfers between devices: 43.6 us -> 45.1 us
  waiting for transfers between devices: 11.4 us -> 9.9 us
    ppermute x27, starting transfers between devices: 43.6 us -> 45.1 us  [shards(): move = lambda a, pairs: lax.ppermute(a, 'expert', pairs)]
    ppermute x27, waiting for transfers between devices: 11.4 us -> 9.9 us  [shards(): move = lambda a, pairs: lax.ppermute(a, 'expert', pairs)]
where the time goes in v7:
time: 129 us
  Pallas kernels  72.5 us (56%)
  starting transfers between devices  45.1 us (35%)
  waiting for transfers between devices  9.9 us (8%)
    pallas_call x25, Pallas kernels, run(): pl.pallas_call(body, in_specs=[SCALAR] + [ANYWHERE] * anywhere + [LOCAL]...  72.5 us
    ppermute x27, starting transfers between devices, shards(): move = lambda a, pairs: lax.ppermute(a, 'expert', pairs)  45.1 us
    ppermute x27, waiting for transfers between devices, shards(): move = lambda a, pairs: lax.ppermute(a, 'expert', pairs)  9.9 us
  transfers between devices with their start and end apart: 27, of which 8 were waited for; matrix products, arithmetic and copies ran while one was open for 0% of the time, Pallas kernels for 55%

profile of v7, /device:TPU:0, one launch (start us, length us, event | category | flops | bytes accessed | tf_op | source)
XLA Modules:
  0.0 129.0 jit_solution(7625307327426174215)
XLA Ops:
  1.3 2.3 %shard_map.77 = (bf16[128,2176]{1,0:T(8,128)(2,1)S(1)}, bf16[112,2176]{1,0:T(8,128)(2,1)S(1)}, bf16[112,128]{1,0:T(8,128)(2,1)S(1)}, s32[4]{0:T(128)S(1)}) custom-call(s32[4]{0:T(128)S(1)} %pad_add_fusion.ticket_ref, bf16[128,2048]{1,0:T(8,128)(2,1)} %refs_0_.1, s32[4,128]{1,0:T(4,128)} %bitcast.9, bf16[4,128]{1,0:T(4,128)(2,1)} %bitcast.15), custom_call_target="tpu_custom_call" | custom-call | tf_op jit(solution)/shard_map/pallas_call | solution.py:36
  3.6 3.1 %collective-permute-start.2 = (bf16[128,2176]{1,0:T(8,128)(2,1)S(1)}, bf16[128,2176]{1,0:T(8,128)(2,1)S(1)}, u32[]{:S(2)}, u32[]{:S(2)}) collective-permute-start(bf16[128,2176]{1,0:T(8,128)(2,1)S(1)} %get-tuple-element.82.refs_0_.refs_4_), channel_id=1, source_target_pairs={{0,4},{1,5},{2,6},{3,7},{4,12},{5,13},{6,14},{7,15},{8,0},{9,1},{1... | collective-permute-start | bytes 1671176 | tf_op jit(solution)/shard_map/ppermute | solution.py:328
  6.6 1.5 %collective-permute-start.3 = (bf16[112,2176]{1,0:T(8,128)(2,1)S(1)}, bf16[112,2176]{1,0:T(8,128)(2,1)S(1)}, u32[]{:S(2)}, u32[]{:S(2)}) collective-permute-start(bf16[112,2176]{1,0:T(8,128)(2,1)S(1)} %get-tuple-element.84), channel_id=1, source_target_pairs={{0,2},{1,3},{2,0},{3,1},{4,6},{5,7},{6,4},{7,5},{8,10},{9,11},{10,... | collective-permute-start | bytes 1462280 | tf_op jit(solution)/shard_map/ppermute | solution.py:328
  8.1 2.6 %collective-permute-start.4 = (bf16[128,2048]{1,0:T(8,128)(2,1)}, bf16[128,2048]{1,0:T(8,128)(2,1)S(1)}, u32[]{:S(2)}, u32[]{:S(2)}) collective-permute-start(bf16[128,2048]{1,0:T(8,128)(2,1)} %refs_2_.1), channel_id=1, source_target_pairs={{0,4},{1,5},{2,6},{3,7},{4,12},{5,13},{6,14},{7,15},{8,0},{9,1},{1... | collective-permute-start | bytes 1572872 | tf_op jit(solution)/shard_map/ppermute | solution.py:328
  10.7 4.9 %shard_map.78 = (bf16[2048,1536]{1,0:T(8,128)(2,1)S(1)}, bf16[768,2048]{1,0:T(8,128)(2,1)S(1)}, s32[4]{0:T(128)S(1)}) custom-call(s32[4]{0:T(128)S(1)} %get-tuple-element.77.ticket_ref, bf16[2048,1536]{1,0:T(8,128)(2,1)} %bitcast.12, bf16[768,2048]{1,0:T(8,128)(2,1)} %bitcast.14), custom_call_target="tpu_custom_call" | custom-call | tf_op jit(solution)/shard_map/pallas_call | solution.py:36
  18.5 4.9 %shard_map.80 = (bf16[2048,1536]{1,0:T(8,128)(2,1)S(1)}, bf16[768,2048]{1,0:T(8,128)(2,1)S(1)}, s32[4]{0:T(128)S(1)}) custom-call(s32[4]{0:T(128)S(1)} %get-tuple-element.80.ticket_ref, bf16[2048,1536]{1,0:T(8,128)(2,1)} %collective-permute-done.refs_0_, bf16[768,2048]{1,0:T(8,128)(2,1)} %copy-done.2), custom_call_target="tpu_custom_call" | custom-call | tf_op jit(solution)/shard_map/pallas_call | solution.py:36
  23.4 1.4 %shard_map.81 = (bf16[112,2176]{1,0:T(8,128)(2,1)S(1)}, bf16[112,128]{1,0:T(8,128)(2,1)S(1)}, bf16[128,2176]{1,0:T(8,128)(2,1)S(1)}, s32[4]{0:T(128)S(1)}) custom-call(s32[4]{0:T(128)S(1)} %get-tuple-element.81.ticket_ref, bf16[128,2176]{1,0:T(8,128)(2,1)S(1)} %collective-permute-done.2.refs_0_), custom_call_target="tpu_custom_call" | custom-call | tf_op jit(solution)/shard_map/pallas_call | solution.py:36
  24.8 1.5 %collective-permute-start.6 = (bf16[128,2176]{1,0:T(8,128)(2,1)S(1)}, bf16[128,2176]{1,0:T(8,128)(2,1)S(1)}, u32[]{:S(2)}, u32[]{:S(2)}) collective-permute-start(bf16[128,2176]{1,0:T(8,128)(2,1)S(1)} %get-tuple-element.96.refs_0_.refs_4_), channel_id=1, source_target_pairs={{0,4},{1,5},{2,6},{3,7},{4,12},{5,13},{6,14},{7,15},{8,0},{9,1},{1... | collective-permute-start | bytes 1671176 | tf_op jit(solution)/shard_map/ppermute | solution.py:328
  26.3 1.5 %collective-permute-start.7 = (bf16[112,2176]{1,0:T(8,128)(2,1)S(1)}, bf16[112,2176]{1,0:T(8,128)(2,1)S(1)}, u32[]{:S(2)}, u32[]{:S(2)}) collective-permute-start(bf16[112,2176]{1,0:T(8,128)(2,1)S(1)} %get-tuple-element.98), channel_id=1, source_target_pairs={{0,2},{1,3},{2,0},{3,1},{4,6},{5,7},{6,4},{7,5},{8,10},{9,11},{10,... | collective-permute-start | bytes 1462280 | tf_op jit(solution)/shard_map/ppermute | solution.py:328
  27.9 4.1 %shard_map.82 = (f32[240,1536]{1,0:T(8,128)S(1)}, f32[240,1536]{1,0:T(8,128)S(1)}, s32[4]{0:T(128)S(1)}) custom-call(s32[4]{0:T(128)S(1)} %get-tuple-element.83.ticket_ref, bf16[128,2176]{1,0:T(8,128)(2,1)S(1)} %get-tuple-element.82.refs_0_.refs_4_, bf16[112,2176]{1,0:T(8,128)(2,1)S(1)} %collective-permute-done.3.refs_1_.refs_5_, ...), custom_call_target="tpu_custom_call" | custom-call | flops 1026765632 | tf_op jit(solution)/shard_map/pallas_call | solution.py:36
  33.4 2.0 %collective-permute-start.8 = (bf16[112,2048]{1,0:T(8,128)(2,1)S(1)}, bf16[112,2048]{1,0:T(8,128)(2,1)S(1)}, u32[]{:S(2)}, u32[]{:S(2)}) collective-permute-start(bf16[112,2048]{1,0:T(8,128)(2,1)S(1)} %get-tuple-element.103), channel_id=1, source_target_pairs={{0,2},{1,3},{2,0},{3,1},{4,6},{5,7},{6,4},{7,5},{8,10},{9,11},{10,... | collective-permute-start | bytes 1376264 | tf_op jit(solution)/shard_map/ppermute | solution.py:328
  36.3 6.7 %shard_map.84 = (bf16[128,2176]{1,0:T(8,128)(2,1)S(1)}, bf16[112,2176]{1,0:T(8,128)(2,1)S(1)}, s32[4]{0:T(128)S(1)}) custom-call(s32[4]{0:T(128)S(1)} %get-tuple-element.89.ticket_ref, f32[240,1536]{1,0:T(8,128)S(1)} %get-tuple-element.90.refs_0_, f32[240,1536]{1,0:T(8,128)S(1)} %get-tuple-element.91.refs_1_, bf16[128,2048]{1,0:T(8,128)(2,1)S(1)} %copy-done, ...), custom_call_target="tpu_custom_call" | custom-call | flops 1540148480 | tf_op jit(solution)/shard_map/pallas_call | solution.py:36
  45.7 2.0 %collective-permute-start.10 = (bf16[112,2176]{1,0:T(8,128)(2,1)S(1)}, bf16[112,2176]{1,0:T(8,128)(2,1)S(1)}, u32[]{:S(2)}, u32[]{:S(2)}) collective-permute-start(bf16[112,2176]{1,0:T(8,128)(2,1)S(1)} %get-tuple-element.108), channel_id=1, source_target_pairs={{0,2},{1,3},{2,0},{3,1},{4,6},{5,7},{6,4},{7,5},{8,10},{9,11},{10,... | collective-permute-start | bytes 1462280 | tf_op jit(solution)/shard_map/ppermute | solution.py:328
  48.4 4.2 %shard_map.86 = (f32[240,1536]{1,0:T(8,128)S(1)}, f32[240,1536]{1,0:T(8,128)S(1)}, s32[4]{0:T(128)S(1)}) custom-call(s32[4]{0:T(128)S(1)} %get-tuple-element.97.ticket_ref, bf16[128,2176]{1,0:T(8,128)(2,1)S(1)} %get-tuple-element.96.refs_0_.refs_4_, bf16[112,2176]{1,0:T(8,128)(2,1)S(1)} %collective-permute-done.7.refs_1_.refs_5_, ...), custom_call_target="tpu_custom_call" | custom-call | flops 1026765632 | tf_op jit(solution)/shard_map/pallas_call | solution.py:36
  52.6 6.7 %shard_map.87 = (bf16[128,2176]{1,0:T(8,128)(2,1)S(1)}, bf16[112,2176]{1,0:T(8,128)(2,1)S(1)}, s32[4]{0:T(128)S(1)}) custom-call(s32[4]{0:T(128)S(1)} %get-tuple-element.99.ticket_ref, f32[240,1536]{1,0:T(8,128)S(1)} %get-tuple-element.100.refs_0_, f32[240,1536]{1,0:T(8,128)S(1)} %get-tuple-element.101.refs_1_, ...), custom_call_target="tpu_custom_call" | custom-call | flops 1540148480 | tf_op jit(solution)/shard_map/pallas_call | solution.py:36
  61.8 2.5 %collective-permute-start.13 = (bf16[128,2048]{1,0:T(8,128)(2,1)S(1)}, bf16[128,2048]{1,0:T(8,128)(2,1)S(1)}, u32[]{:S(2)}, u32[]{:S(2)}) collective-permute-start(bf16[128,2048]{1,0:T(8,128)(2,1)S(1)} %get-tuple-element.114.refs_2_), channel_id=1, source_target_pairs={{0,4},{1,5},{2,6},{3,7},{4,12},{5,13},{6,14},{7,15},{8,0},{9,1},{1... | collective-permute-start | bytes 1572872 | tf_op jit(solution)/shard_map/ppermute | solution.py:328
  64.4 4.2 %shard_map.89 = (f32[240,1536]{1,0:T(8,128)S(1)}, f32[240,1536]{1,0:T(8,128)S(1)}, bf16[112,2176]{1,0:T(8,128)(2,1)S(1)}, s32[4]{0:T(128)S(1)}) custom-call(s32[4]{0:T(128)S(1)} %get-tuple-element.106.ticket_ref, bf16[128,2176]{1,0:T(8,128)(2,1)S(1)} %get-tuple-element.107.refs_0_.refs_4_, bf16[112,2176]{1,0:T(8,128)(2,1)S(1)} %collective-permute-done.10.refs_1_.refs_5_, ...), custom_call_target="tpu_custom_call" | custom-call | flops 1026765632 | tf_op jit(solution)/shard_map/pallas_call | solution.py:36
  70.0 1.6 %collective-permute-start.14 = (bf16[112,2176]{1,0:T(8,128)(2,1)S(1)}, bf16[112,2176]{1,0:T(8,128)(2,1)S(1)}, u32[]{:S(2)}, u32[]{:S(2)}) collective-permute-start(bf16[112,2176]{1,0:T(8,128)(2,1)S(1)} %get-tuple-element.119), channel_id=1, source_target_pairs={{0,2},{1,3},{2,0},{3,1},{4,6},{5,7},{6,4},{7,5},{8,10},{9,11},{10,... | collective-permute-start | bytes 1462280 | tf_op jit(solution)/shard_map/ppermute | solution.py:328
  71.6 6.6 %shard_map.91 = (bf16[128,2176]{1,0:T(8,128)(2,1)S(1)}, bf16[112,2176]{1,0:T(8,128)(2,1)S(1)}, s32[4]{0:T(128)S(1)}) custom-call(s32[4]{0:T(128)S(1)} %get-tuple-element.111.ticket_ref, f32[240,1536]{1,0:T(8,128)S(1)} %get-tuple-element.112.refs_0_, f32[240,1536]{1,0:T(8,128)S(1)} %get-tuple-element.113.refs_1_, ...), custom_call_target="tpu_custom_call" | custom-call | flops 1540148480 | tf_op jit(solution)/shard_map/pallas_call | solution.py:36
  79.8 2.0 %collective-permute-start.16 = (bf16[112,2048]{1,0:T(8,128)(2,1)S(1)}, bf16[112,2048]{1,0:T(8,128)(2,1)S(1)}, u32[]{:S(2)}, u32[]{:S(2)}) collective-permute-start(bf16[112,2048]{1,0:T(8,128)(2,1)S(1)} %get-tuple-element.127), channel_id=1, source_target_pairs={{0,2},{1,3},{2,0},{3,1},{4,6},{5,7},{6,4},{7,5},{8,10},{9,11},{10,... | collective-permute-start | bytes 1376264 | tf_op jit(solution)/shard_map/ppermute | solution.py:328
  81.7 4.2 %shard_map.93 = (f32[240,1536]{1,0:T(8,128)S(1)}, f32[240,1536]{1,0:T(8,128)S(1)}, bf16[128,2176]{1,0:T(8,128)(2,1)S(1)}, s32[4]{0:T(128)S(1)}) custom-call(s32[4]{0:T(128)S(1)} %get-tuple-element.118.ticket_ref, bf16[128,2176]{1,0:T(8,128)(2,1)S(1)} %collective-permute-done.11.refs_0_.refs_4_, ...), custom_call_target="tpu_custom_call" | custom-call | flops 1026765632 | tf_op jit(solution)/shard_map/pallas_call | solution.py:36
  85.9 4.2 %collective-permute-start.18 = (bf16[128,2176]{1,0:T(8,128)(2,1)S(1)}, bf16[128,2176]{1,0:T(8,128)(2,1)S(1)}, u32[]{:S(2)}, u32[]{:S(2)}) collective-permute-start(bf16[128,2176]{1,0:T(8,128)(2,1)S(1)} %get-tuple-element.131), channel_id=1, source_target_pairs={{0,4},{1,5},{2,6},{3,7},{4,12},{5,13},{6,14},{7,15},{8,0},{9,1},{1... | collective-permute-start | bytes 1671176 | tf_op jit(solution)/shard_map/ppermute | solution.py:328
  93.3 6.7 %shard_map.95 = (bf16[128,2176]{1,0:T(8,128)(2,1)S(1)}, bf16[112,1024]{1,0:T(8,128)(2,1)S(1)}, bf16[112,1152]{1,0:T(8,128)(2,1)S(1)}, s32[4]{0:T(128)S(1)}) custom-call(s32[4]{0:T(128)S(1)} %get-tuple-element.124.ticket_ref, f32[240,1536]{1,0:T(8,128)S(1)} %get-tuple-element.125.refs_0_, f32[240,1536]{1,0:T(8,128)S(1)} %get-tuple-element.126.refs_1_, ...), custom_call_target="tpu_custom_call" | custom-call | flops 1540148480 | tf_op jit(solution)/shard_map/pallas_call | solution.py:36
  101.7 2.5 %collective-permute-start.21 = (bf16[128,1024]{1,0:T(8,128)(2,1)S(1)}, bf16[128,1024]{1,0:T(8,128)(2,1)S(1)}, u32[]{:S(2)}, u32[]{:S(2)}) collective-permute-start(bf16[128,1024]{1,0:T(8,128)(2,1)S(1)} %get-tuple-element.138), channel_id=1, source_target_pairs={{0,4},{1,5},{2,6},{3,7},{4,12},{5,13},{6,14},{7,15},{8,0},{9,1},{1... | collective-permute-start | bytes 786440 | tf_op jit(solution)/shard_map/ppermute | solution.py:328
  104.2 2.0 %collective-permute-start.22 = (bf16[112,1152]{1,0:T(8,128)(2,1)S(1)}, bf16[112,1152]{1,0:T(8,128)(2,1)S(1)}, u32[]{:S(2)}, u32[]{:S(2)}) collective-permute-start(bf16[112,1152]{1,0:T(8,128)(2,1)S(1)} %get-tuple-element.140), channel_id=1, source_target_pairs={{0,2},{1,3},{2,0},{3,1},{4,6},{5,7},{6,4},{7,5},{8,10},{9,11},{10,... | collective-permute-start | bytes 774152 | tf_op jit(solution)/shard_map/ppermute | solution.py:328
  107.4 1.7 %collective-permute-start.23 = (bf16[128,1152]{1,0:T(8,128)(2,1)S(1)}, bf16[128,1152]{1,0:T(8,128)(2,1)S(1)}, u32[]{:S(2)}, u32[]{:S(2)}) collective-permute-start(bf16[128,1152]{1,0:T(8,128)(2,1)S(1)} %get-tuple-element.141), channel_id=1, source_target_pairs={{0,4},{1,5},{2,6},{3,7},{4,12},{5,13},{6,14},{7,15},{8,0},{9,1},{1... | collective-permute-start | bytes 884744 | tf_op jit(solution)/shard_map/ppermute | solution.py:328
  109.1 2.4 %collective-permute-done.20.refs_2_ = bf16[112,1024]{1,0:T(8,128)(2,1)S(1)} collective-permute-done((bf16[112,1024]{1,0:T(8,128)(2,1)S(1)}, bf16[112,1024]{1,0:T(8,128)(2,1)S(1)}, u32[]{:S(2)}, u32[]{:S(2)}) %collective-permute-start.20) | collective-permute-done | bytes 229408 | tf_op jit(solution)/shard_map/ppermute | solution.py:328
  112.7 1.9 %collective-permute-start.24 = (bf16[112,2176]{1,0:T(8,128)(2,1)S(1)}, bf16[112,2176]{1,0:T(8,128)(2,1)S(1)}, u32[]{:S(2)}, u32[]{:S(2)}) collective-permute-start(bf16[112,2176]{1,0:T(8,128)(2,1)S(1)} %get-tuple-element.144), channel_id=1, source_target_pairs={{0,2},{1,3},{2,0},{3,1},{4,6},{5,7},{6,4},{7,5},{8,10},{9,11},{10,... | collective-permute-start | bytes 1462280 | tf_op jit(solution)/shard_map/ppermute | solution.py:328
  114.6 2.6 %collective-permute-start.25 = (bf16[128,1024]{1,0:T(8,128)(2,1)S(1)}, bf16[128,1024]{1,0:T(8,128)(2,1)S(1)}, u32[]{:S(2)}, u32[]{:S(2)}) collective-permute-start(bf16[128,1024]{1,0:T(8,128)(2,1)S(1)} %get-tuple-element.145), channel_id=1, source_target_pairs={{0,4},{1,5},{2,6},{3,7},{4,12},{5,13},{6,14},{7,15},{8,0},{9,1},{1... | collective-permute-start | bytes 786440 | tf_op jit(solution)/shard_map/ppermute | solution.py:328
  118.4 2.8 %collective-permute-start.26 = (bf16[128,1152]{1,0:T(8,128)(2,1)S(1)}, bf16[128,1152]{1,0:T(8,128)(2,1)S(1)}, u32[]{:S(2)}, u32[]{:S(2)}) collective-permute-start(bf16[128,1152]{1,0:T(8,128)(2,1)S(1)} %get-tuple-element.149), channel_id=1, source_target_pairs={{0,4},{1,5},{2,6},{3,7},{4,12},{5,13},{6,14},{7,15},{8,0},{9,1},{1... | collective-permute-start | bytes 884744 | tf_op jit(solution)/shard_map/ppermute | solution.py:328
  121.2 3.0 %collective-permute-done.25.refs_3_ = bf16[128,1024]{1,0:T(8,128)(2,1)S(1)} collective-permute-done((bf16[128,1024]{1,0:T(8,128)(2,1)S(1)}, bf16[128,1024]{1,0:T(8,128)(2,1)S(1)}, u32[]{:S(2)}, u32[]{:S(2)}) %collective-permute-start.25) | collective-permute-done | bytes 262176 | tf_op jit(solution)/shard_map/ppermute | solution.py:328
  127.3 1.5 %shard_map.101 = (bf16[128,2048]{1,0:T(8,128)(2,1)}, bf16[4,128]{1,0:T(4,128)(2,1)}, s32[4]{0:T(128)}) custom-call(s32[4]{0:T(128)S(1)} %get-tuple-element.146.ticket_ref, bf16[128,1024]{1,0:T(8,128)(2,1)S(1)} %get-tuple-element.147.refs_0_, f32[128,1152]{1,0:T(8,128)S(1)} %get-tuple-element.148.refs_1_, ...), custom_call_target="tpu_custom_call" | custom-call | tf_op jit(solution)/shard_map/pallas_call | solution.py:36
  (54 shorter events, 26.4 us)
Async XLA Ops:
  0.6 17.6 %collective-permute-start = (bf16[2048,1536]{1,0:T(8,128)(2,1)}, bf16[2048,1536]{1,0:T(8,128)(2,1)}, u32[]{:S(2)}, u32[]{:S(2)}) collective-permute-start(bf16[2048,1536]{1,0:T(8,128)(2,1)} %bitcast.11), channel_id=1, source_target_pairs={{0,1},{1,0},{2,3},{3,2},{4,5},{5,4},{6,7},{7,6},{8,9},{9,8},{10,11... | collective-permute-start | bytes 18874376 | tf_op jit(solution)/shard_map/ppermute | solution.py:328
  1.1 15.6 %collective-permute-start.1 = (bf16[768,2048]{1,0:T(8,128)(2,1)}, bf16[768,2048]{1,0:T(8,128)(2,1)S(1)}, u32[]{:S(2)}, u32[]{:S(2)}) collective-permute-start(bf16[768,2048]{1,0:T(8,128)(2,1)} %bitcast.13), channel_id=1, source_target_pairs={{0,1},{1,0},{2,3},{3,2},{4,5},{5,4},{6,7},{7,6},{8,9},{9,8},{10,11... | collective-permute-start | bytes 9437192 | tf_op jit(solution)/shard_map/ppermute | solution.py:328
  3.6 19.8 %collective-permute-start.2 = (bf16[128,2176]{1,0:T(8,128)(2,1)S(1)}, bf16[128,2176]{1,0:T(8,128)(2,1)S(1)}, u32[]{:S(2)}, u32[]{:S(2)}) collective-permute-start(bf16[128,2176]{1,0:T(8,128)(2,1)S(1)} %get-tuple-element.82.refs_0_.refs_4_), channel_id=1, source_target_pairs={{0,4},{1,5},{2,6},{3,7},{4,12},{5,13},{6,14},{7,15},{8,0},{9,1},{1... | collective-permute-start | bytes 1671176 | tf_op jit(solution)/shard_map/ppermute | solution.py:328
  6.6 21.2 %collective-permute-start.3 = (bf16[112,2176]{1,0:T(8,128)(2,1)S(1)}, bf16[112,2176]{1,0:T(8,128)(2,1)S(1)}, u32[]{:S(2)}, u32[]{:S(2)}) collective-permute-start(bf16[112,2176]{1,0:T(8,128)(2,1)S(1)} %get-tuple-element.84), channel_id=1, source_target_pairs={{0,2},{1,3},{2,0},{3,1},{4,6},{5,7},{6,4},{7,5},{8,10},{9,11},{10,... | collective-permute-start | bytes 1462280 | tf_op jit(solution)/shard_map/ppermute | solution.py:328
  8.1 24.1 %collective-permute-start.4 = (bf16[128,2048]{1,0:T(8,128)(2,1)}, bf16[128,2048]{1,0:T(8,128)(2,1)S(1)}, u32[]{:S(2)}, u32[]{:S(2)}) collective-permute-start(bf16[128,2048]{1,0:T(8,128)(2,1)} %refs_2_.1), channel_id=1, source_target_pairs={{0,4},{1,5},{2,6},{3,7},{4,12},{5,13},{6,14},{7,15},{8,0},{9,1},{1... | collective-permute-start | bytes 1572872 | tf_op jit(solution)/shard_map/ppermute | solution.py:328
  10.7 4.9 %copy-start = (bf16[128,2048]{1,0:T(8,128)(2,1)S(1)}, bf16[128,2048]{1,0:T(8,128)(2,1)}, u32[]{:S(2)}) copy-start(bf16[128,2048]{1,0:T(8,128)(2,1)} %refs_2_.1) | copy-start | bytes 1572868
  16.8 1.7 %copy-start.2 = (bf16[768,2048]{1,0:T(8,128)(2,1)}, bf16[768,2048]{1,0:T(8,128)(2,1)S(1)}, u32[]{:S(2)}) copy-start(bf16[768,2048]{1,0:T(8,128)(2,1)S(1)} %collective-permute-done.1.refs_1_) | copy-start | bytes 9437188
  16.8 19.5 %collective-permute-start.5 = (bf16[112,2048]{1,0:T(8,128)(2,1)S(1)}, bf16[112,2048]{1,0:T(8,128)(2,1)S(1)}, u32[]{:S(2)}, u32[]{:S(2)}) collective-permute-start(bf16[112,2048]{1,0:T(8,128)(2,1)S(1)} %get-tuple-element.92), channel_id=1, source_target_pairs={{0,2},{1,3},{2,0},{3,1},{4,6},{5,7},{6,4},{7,5},{8,10},{9,11},{10,... | collective-permute-start | bytes 1376264 | tf_op jit(solution)/shard_map/ppermute | solution.py:328
  24.8 19.4 %collective-permute-start.6 = (bf16[128,2176]{1,0:T(8,128)(2,1)S(1)}, bf16[128,2176]{1,0:T(8,128)(2,1)S(1)}, u32[]{:S(2)}, u32[]{:S(2)}) collective-permute-start(bf16[128,2176]{1,0:T(8,128)(2,1)S(1)} %get-tuple-element.96.refs_0_.refs_4_), channel_id=1, source_target_pairs={{0,4},{1,5},{2,6},{3,7},{4,12},{5,13},{6,14},{7,15},{8,0},{9,1},{1... | collective-permute-start | bytes 1671176 | tf_op jit(solution)/shard_map/ppermute | solution.py:328
  26.3 22.1 %collective-permute-start.7 = (bf16[112,2176]{1,0:T(8,128)(2,1)S(1)}, bf16[112,2176]{1,0:T(8,128)(2,1)S(1)}, u32[]{:S(2)}, u32[]{:S(2)}) collective-permute-start(bf16[112,2176]{1,0:T(8,128)(2,1)S(1)} %get-tuple-element.98), channel_id=1, source_target_pairs={{0,2},{1,3},{2,0},{3,1},{4,6},{5,7},{6,4},{7,5},{8,10},{9,11},{10,... | collective-permute-start | bytes 1462280 | tf_op jit(solution)/shard_map/ppermute | solution.py:328
  33.4 19.2 %collective-permute-start.8 = (bf16[112,2048]{1,0:T(8,128)(2,1)S(1)}, bf16[112,2048]{1,0:T(8,128)(2,1)S(1)}, u32[]{:S(2)}, u32[]{:S(2)}) collective-permute-start(bf16[112,2048]{1,0:T(8,128)(2,1)S(1)} %get-tuple-element.103), channel_id=1, source_target_pairs={{0,2},{1,3},{2,0},{3,1},{4,6},{5,7},{6,4},{7,5},{8,10},{9,11},{10,... | collective-permute-start | bytes 1376264 | tf_op jit(solution)/shard_map/ppermute | solution.py:328
  35.4 23.9 %collective-permute-start.9 = (bf16[128,2048]{1,0:T(8,128)(2,1)S(1)}, bf16[128,2048]{1,0:T(8,128)(2,1)S(1)}, u32[]{:S(2)}, u32[]{:S(2)}) collective-permute-start(bf16[128,2048]{1,0:T(8,128)(2,1)S(1)} %get-tuple-element.102.refs_2_), channel_id=1, source_target_pairs={{0,4},{1,5},{2,6},{3,7},{4,12},{5,13},{6,14},{7,15},{8,0},{9,1},{1... | collective-permute-start | bytes 1572872 | tf_op jit(solution)/shard_map/ppermute | solution.py:328
  45.7 18.7 %collective-permute-start.10 = (bf16[112,2176]{1,0:T(8,128)(2,1)S(1)}, bf16[112,2176]{1,0:T(8,128)(2,1)S(1)}, u32[]{:S(2)}, u32[]{:S(2)}) collective-permute-start(bf16[112,2176]{1,0:T(8,128)(2,1)S(1)} %get-tuple-element.108), channel_id=1, source_target_pairs={{0,2},{1,3},{2,0},{3,1},{4,6},{5,7},{6,4},{7,5},{8,10},{9,11},{10,... | collective-permute-start | bytes 1462280 | tf_op jit(solution)/shard_map/ppermute | solution.py:328
  47.6 20.9 %collective-permute-start.11 = (bf16[128,2176]{1,0:T(8,128)(2,1)S(1)}, bf16[128,2176]{1,0:T(8,128)(2,1)S(1)}, u32[]{:S(2)}, u32[]{:S(2)}) collective-permute-start(bf16[128,2176]{1,0:T(8,128)(2,1)S(1)} %get-tuple-element.107.refs_0_.refs_4_), channel_id=1, source_target_pairs={{0,4},{1,5},{2,6},{3,7},{4,12},{5,13},{6,14},{7,15},{8,0},{9,1},{1... | collective-permute-start | bytes 1671176 | tf_op jit(solution)/shard_map/ppermute | solution.py:328
  60.4 11.1 %collective-permute-start.12 = (bf16[112,2048]{1,0:T(8,128)(2,1)S(1)}, bf16[112,2048]{1,0:T(8,128)(2,1)S(1)}, u32[]{:S(2)}, u32[]{:S(2)}) collective-permute-start(bf16[112,2048]{1,0:T(8,128)(2,1)S(1)} %get-tuple-element.115), channel_id=1, source_target_pairs={{0,2},{1,3},{2,0},{3,1},{4,6},{5,7},{6,4},{7,5},{8,10},{9,11},{10,... | collective-permute-start | bytes 1376264 | tf_op jit(solution)/shard_map/ppermute | solution.py:328
  61.8 16.8 %collective-permute-start.13 = (bf16[128,2048]{1,0:T(8,128)(2,1)S(1)}, bf16[128,2048]{1,0:T(8,128)(2,1)S(1)}, u32[]{:S(2)}, u32[]{:S(2)}) collective-permute-start(bf16[128,2048]{1,0:T(8,128)(2,1)S(1)} %get-tuple-element.114.refs_2_), channel_id=1, source_target_pairs={{0,4},{1,5},{2,6},{3,7},{4,12},{5,13},{6,14},{7,15},{8,0},{9,1},{1... | collective-permute-start | bytes 1572872 | tf_op jit(solution)/shard_map/ppermute | solution.py:328
  70.0 11.8 %collective-permute-start.14 = (bf16[112,2176]{1,0:T(8,128)(2,1)S(1)}, bf16[112,2176]{1,0:T(8,128)(2,1)S(1)}, u32[]{:S(2)}, u32[]{:S(2)}) collective-permute-start(bf16[112,2176]{1,0:T(8,128)(2,1)S(1)} %get-tuple-element.119), channel_id=1, source_target_pairs={{0,2},{1,3},{2,0},{3,1},{4,6},{5,7},{6,4},{7,5},{8,10},{9,11},{10,... | collective-permute-start | bytes 1462280 | tf_op jit(solution)/shard_map/ppermute | solution.py:328
  71.6 18.5 %collective-permute-start.15 = (bf16[112,2176]{1,0:T(8,128)(2,1)S(1)}, bf16[112,2176]{1,0:T(8,128)(2,1)S(1)}, u32[]{:S(2)}, u32[]{:S(2)}) collective-permute-start(bf16[112,2176]{1,0:T(8,128)(2,1)S(1)} %get-tuple-element.123), channel_id=1, source_target_pairs={{0,4},{1,5},{2,6},{3,7},{4,12},{5,13},{6,14},{7,15},{8,0},{9,1},{1... | collective-permute-start | bytes 1462280 | tf_op jit(solution)/shard_map/ppermute | solution.py:328
  79.8 13.6 %collective-permute-start.16 = (bf16[112,2048]{1,0:T(8,128)(2,1)S(1)}, bf16[112,2048]{1,0:T(8,128)(2,1)S(1)}, u32[]{:S(2)}, u32[]{:S(2)}) collective-permute-start(bf16[112,2048]{1,0:T(8,128)(2,1)S(1)} %get-tuple-element.127), channel_id=1, source_target_pairs={{0,2},{1,3},{2,0},{3,1},{4,6},{5,7},{6,4},{7,5},{8,10},{9,11},{10,... | collective-permute-start | bytes 1376264 | tf_op jit(solution)/shard_map/ppermute | solution.py:328
  85.9 14.6 %collective-permute-start.18 = (bf16[128,2176]{1,0:T(8,128)(2,1)S(1)}, bf16[128,2176]{1,0:T(8,128)(2,1)S(1)}, u32[]{:S(2)}, u32[]{:S(2)}) collective-permute-start(bf16[128,2176]{1,0:T(8,128)(2,1)S(1)} %get-tuple-element.131), channel_id=1, source_target_pairs={{0,4},{1,5},{2,6},{3,7},{4,12},{5,13},{6,14},{7,15},{8,0},{9,1},{1... | collective-permute-start | bytes 1671176 | tf_op jit(solution)/shard_map/ppermute | solution.py:328
  91.2 9.3 %collective-permute-start.17 = (bf16[128,1024]{1,0:T(8,128)(2,1)S(1)}, bf16[128,1024]{1,0:T(8,128)(2,1)S(1)}, u32[]{:S(2)}, u32[]{:S(2)}) collective-permute-start(bf16[128,1024]{1,0:T(8,128)(2,1)S(1)} %get-tuple-element.130), channel_id=1, source_target_pairs={{0,2},{1,3},{2,0},{3,1},{4,6},{5,7},{6,4},{7,5},{8,10},{9,11},{10,... | collective-permute-start | bytes 786440 | tf_op jit(solution)/shard_map/ppermute | solution.py:328
  92.5 13.7 %collective-permute-start.19 = (bf16[128,1152]{1,0:T(8,128)(2,1)S(1)}, bf16[128,1152]{1,0:T(8,128)(2,1)S(1)}, u32[]{:S(2)}, u32[]{:S(2)}) collective-permute-start(bf16[128,1152]{1,0:T(8,128)(2,1)S(1)} %get-tuple-element.133), channel_id=1, source_target_pairs={{0,2},{1,3},{2,0},{3,1},{4,6},{5,7},{6,4},{7,5},{8,10},{9,11},{10,... | collective-permute-start | bytes 884744 | tf_op jit(solution)/shard_map/ppermute | solution.py:328
  101.7 9.8 %collective-permute-start.21 = (bf16[128,1024]{1,0:T(8,128)(2,1)S(1)}, bf16[128,1024]{1,0:T(8,128)(2,1)S(1)}, u32[]{:S(2)}, u32[]{:S(2)}) collective-permute-start(bf16[128,1024]{1,0:T(8,128)(2,1)S(1)} %get-tuple-element.138), channel_id=1, source_target_pairs={{0,4},{1,5},{2,6},{3,7},{4,12},{5,13},{6,14},{7,15},{8,0},{9,1},{1... | collective-permute-start | bytes 786440 | tf_op jit(solution)/shard_map/ppermute | solution.py:328
  104.2 7.3 %collective-permute-start.20 = (bf16[112,1024]{1,0:T(8,128)(2,1)S(1)}, bf16[112,1024]{1,0:T(8,128)(2,1)S(1)}, u32[]{:S(2)}, u32[]{:S(2)}) collective-permute-start(bf16[112,1024]{1,0:T(8,128)(2,1)S(1)} %get-tuple-element.137), channel_id=1, source_target_pairs={{0,2},{1,3},{2,0},{3,1},{4,6},{5,7},{6,4},{7,5},{8,10},{9,11},{10,... | collective-permute-start | bytes 688136 | tf_op jit(solution)/shard_map/ppermute | solution.py:328
  104.2 13.0 %collective-permute-start.22 = (bf16[112,1152]{1,0:T(8,128)(2,1)S(1)}, bf16[112,1152]{1,0:T(8,128)(2,1)S(1)}, u32[]{:S(2)}, u32[]{:S(2)}) collective-permute-start(bf16[112,1152]{1,0:T(8,128)(2,1)S(1)} %get-tuple-element.140), channel_id=1, source_target_pairs={{0,2},{1,3},{2,0},{3,1},{4,6},{5,7},{6,4},{7,5},{8,10},{9,11},{10,... | collective-permute-start | bytes 774152 | tf_op jit(solution)/shard_map/ppermute | solution.py:328
  107.4 9.8 %collective-permute-start.23 = (bf16[128,1152]{1,0:T(8,128)(2,1)S(1)}, bf16[128,1152]{1,0:T(8,128)(2,1)S(1)}, u32[]{:S(2)}, u32[]{:S(2)}) collective-permute-start(bf16[128,1152]{1,0:T(8,128)(2,1)S(1)} %get-tuple-element.141), channel_id=1, source_target_pairs={{0,4},{1,5},{2,6},{3,7},{4,12},{5,13},{6,14},{7,15},{8,0},{9,1},{1... | collective-permute-start | bytes 884744 | tf_op jit(solution)/shard_map/ppermute | solution.py:328
  112.7 12.0 %collective-permute-start.24 = (bf16[112,2176]{1,0:T(8,128)(2,1)S(1)}, bf16[112,2176]{1,0:T(8,128)(2,1)S(1)}, u32[]{:S(2)}, u32[]{:S(2)}) collective-permute-start(bf16[112,2176]{1,0:T(8,128)(2,1)S(1)} %get-tuple-element.144), channel_id=1, source_target_pairs={{0,2},{1,3},{2,0},{3,1},{4,6},{5,7},{6,4},{7,5},{8,10},{9,11},{10,... | collective-permute-start | bytes 1462280 | tf_op jit(solution)/shard_map/ppermute | solution.py:328
  114.6 9.5 %collective-permute-start.25 = (bf16[128,1024]{1,0:T(8,128)(2,1)S(1)}, bf16[128,1024]{1,0:T(8,128)(2,1)S(1)}, u32[]{:S(2)}, u32[]{:S(2)}) collective-permute-start(bf16[128,1024]{1,0:T(8,128)(2,1)S(1)} %get-tuple-element.145), channel_id=1, source_target_pairs={{0,4},{1,5},{2,6},{3,7},{4,12},{5,13},{6,14},{7,15},{8,0},{9,1},{1... | collective-permute-start | bytes 786440 | tf_op jit(solution)/shard_map/ppermute | solution.py:328
  118.4 8.9 %collective-permute-start.26 = (bf16[128,1152]{1,0:T(8,128)(2,1)S(1)}, bf16[128,1152]{1,0:T(8,128)(2,1)S(1)}, u32[]{:S(2)}, u32[]{:S(2)}) collective-permute-start(bf16[128,1152]{1,0:T(8,128)(2,1)S(1)} %get-tuple-element.149), channel_id=1, source_target_pairs={{0,4},{1,5},{2,6},{3,7},{4,12},{5,13},{6,14},{7,15},{8,0},{9,1},{1... | collective-permute-start | bytes 884744 | tf_op jit(solution)/shard_map/ppermute | solution.py:328
  124.7 2.6 %copy-start.1 = (s32[128,4]{0,1:T(4,128)S(1)}, s32[128,4]{0,1:T(4,128)}, u32[]{:S(2)}) copy-start(s32[128,4]{0,1:T(4,128)} %param.8) | copy-start | bytes 6148
